TPU v7x, 128 devices: a whole 4x4x4 slice. The times are simulated.
128 devices in a mesh: tm: 8 (over x_hi, y), row: 8 (over z, core), col: 2 (over x_lo).
Axes of the slice: x: 4 (x_hi: 2, x_lo: 2; x = x_hi * 2 + x_lo), y: 4, z: 4, core: 2. Of those that a mesh axis runs over, the one named last changes fastest.
Arguments:
- states: bfloat16 [6144, 1024], P('tm'), may hold values from -4.5 to 4.5
- projection: bfloat16 [1024, 8192], P(None, ('row', 'col')), may hold values from -0.375 to 0.375
- offsets: float32 [8192], P(('row', 'col')), may hold values from -1 to 1
Outputs:
- instant_cov: float32 [8192, 8, 1024], P('row', 'tm', 'col')
- lagged_cov: float32 [8192, 8, 1024], P('row', 'tm', 'col')
All inputs are finite; a program needn't handle non-finite values.
Results may differ from a plain program's by a relative error of at most 0.00032.
Values may be sent and summed in bfloat16 or wider, within the bound.
No kernel may reach another device: no remote copies, remote signals or barrier semaphores. Data moves between devices by JAX's collectives and lax.ppermute only.
A program may use at most 128 MiB of HBM per device.

v0:
```python
import functools
import jax
import jax.numpy as jnp
from jax import lax
from jax.experimental import pallas as pl
from jax.experimental.pallas import tpu as pltpu
from jax.sharding import PartitionSpec as P

LAG = 64
Y = 4
AXES = ("tm", "row", "col")
SPARE = 16
MIB = 1024 * 1024
TIME_TILES, COL_TILES = 1, 1


def route(target):
    tm_count, row_count, col_count = (lax.axis_size(a) for a in AXES)
    flat = lambda tm, row, col: (tm * row_count + row) * col_count + col
    pairs = []
    for tm in range(tm_count):
        for row in range(row_count):
            for col in range(col_count):
                to = target(tm // Y, tm % Y, row // 2, row % 2, col)
                if to is not None:
                    x_hi, y, z, core, x_lo = to
                    pairs.append((flat(tm, row, col), flat(x_hi * Y + y % Y, z * 2 + core, x_lo)))
    return pairs


def move(block, target):
    return lax.ppermute(block, AXES, route(target))


def crossing(x_hi, y, z, core, x_lo):
    return 1 - x_hi, y, z, core, 1 - x_lo


def inner(x_hi, y, z, core, x_lo):
    return x_hi, y, z, core, 1 - x_lo


def other_core(x_hi, y, z, core, x_lo):
    return x_hi, y, z, 1 - core, x_lo


def along_y(step):
    return lambda x_hi, y, z, core, x_lo: (x_hi, y + step, z, core, x_lo)


def out_y(x_hi, y, z, core, x_lo):
    return x_hi, y + 1 - 2 * core, z, core, x_lo


def back_y(x_hi, y, z, core, x_lo):
    return x_hi, y - 1 + 2 * core, z, core, x_lo


def along_z(step):
    def target(x_hi, y, z, core, x_lo):
        return (x_hi, y, (z + step) % 4, core, x_lo) if x_hi * Y + y == z * 2 + core else None
    return target


def any_spec():
    return pl.BlockSpec(memory_space=pl.ANY)


def vmem_spec():
    return pl.BlockSpec(memory_space=pltpu.VMEM)


def hbm_spec():
    return pl.BlockSpec(memory_space=pltpu.HBM)


def in_hbm(x):
    return pltpu.with_memory_space_constraint(x, pltpu.HBM)


def in_vmem(x):
    return pltpu.with_memory_space_constraint(x, pltpu.VMEM)


def smem_spec():
    return pl.BlockSpec(memory_space=pltpu.SMEM)


def row_features(row_proj, turned, row_off, start, valid_rows):
    row_off = jnp.concatenate([row_off] * (turned.shape[1] // row_off.shape[1]), axis=1)
    features = jnp.tanh(jnp.dot(row_proj, turned, preferred_element_type=jnp.float32) + row_off)
    position = start + lax.broadcasted_iota(jnp.int32, (1, turned.shape[1]), 1)
    return jnp.where(position < valid_rows, features, 0.0).astype(jnp.bfloat16)


def col_features(states, col_proj, col_off):
    return jnp.tanh(
        jnp.dot(states, col_proj, preferred_element_type=jnp.float32) + col_off
    ).astype(jnp.bfloat16)


def start(copies):
    for copy in copies:
        copy.start()


def wait(copies):
    for copy in copies:
        copy.wait()


def prepare_kernel(at, numbers, projection, offsets, states, columns, turned, mine, line, sems):
    half = mine.shape[0]
    units, cols = projection.shape
    copies = [
        pltpu.make_async_copy(projection, columns.at[pl.ds(0, units)], sems.at[0]),
        pltpu.make_async_copy(offsets, line, sems.at[1]),
        pltpu.make_async_copy(states.at[pl.ds(pl.multiple_of(numbers[at] * half, 16), half)], mine, sems.at[2]),
    ]
    start(copies)
    turned[cols:] = jnp.zeros_like(turned[cols:])
    wait(copies[1:2])
    high = line[...].astype(jnp.bfloat16)
    rest = line[...] - high.astype(jnp.float32)
    middle = rest.astype(jnp.bfloat16)
    low = (rest - middle.astype(jnp.float32)).astype(jnp.bfloat16)
    parts = jnp.concatenate([high, middle, low, jnp.zeros((SPARE - 3, cols), jnp.bfloat16)], axis=0)
    columns[units:] = parts
    turned[cols:, :cols] = parts
    wait(copies[:1])
    turned[:cols] = columns[:units].T
    wait(copies[2:])


def prepare(at, numbers, projection, offsets, states):
    units, cols = projection.shape
    half = states.shape[0] // 2
    return pl.pallas_call(
        functools.partial(prepare_kernel, at),
        in_specs=[smem_spec(), hbm_spec(), hbm_spec(), hbm_spec()],
        out_specs=[vmem_spec(), vmem_spec(), vmem_spec()],
        out_shape=[jax.ShapeDtypeStruct((units + SPARE, cols), jnp.bfloat16),
                   jax.ShapeDtypeStruct((cols + SPARE, units), jnp.bfloat16),
                   jax.ShapeDtypeStruct((half, units), jnp.bfloat16)],
        scratch_shapes=[pltpu.VMEM((1, cols), jnp.float32), pltpu.SemaphoreType.DMA((3,))],
        compiler_params=pltpu.CompilerParams(vmem_limit_bytes=12 * MIB),
    )(numbers, in_hbm(projection), in_hbm(offsets), in_hbm(states))


class OneOf:
    def __init__(self, number, sources, dst, sem):
        self.number, self.copies = number, [pltpu.make_async_copy(x, dst, sem) for x in sources]

    def start(self):
        for n, copy in enumerate(self.copies):
            pl.when(self.number == n)(copy.start)

    def wait(self):
        self.copies[0].wait()


def pick_kernel(at, numbers, *refs):
    *sources, out, sem = refs
    copy = OneOf(numbers[at], sources, out, sem)
    copy.start()
    copy.wait()


def pick(at, numbers, *sources):
    return pl.pallas_call(
        functools.partial(pick_kernel, at),
        in_specs=[smem_spec()] + [any_spec()] * len(sources),
        out_specs=vmem_spec(),
        out_shape=jax.ShapeDtypeStruct(sources[0].shape, sources[0].dtype),
        scratch_shapes=[pltpu.SemaphoreType.DMA],
        compiler_params=pltpu.CompilerParams(vmem_limit_bytes=8 * MIB),
    )(numbers, *sources)


def slab_copies(pieces, core, dst, sems):
    if len(pieces) == 1:
        return [pltpu.make_async_copy(pieces[0], dst, sems.at[0])]
    half = pieces[0].shape[0]
    return [
        pltpu.make_async_copy(piece, dst.at[pl.ds(pl.multiple_of(place * half, 16), half)], sems.at[n])
        for n, (piece, place) in enumerate(zip(pieces, (core, 1 - core)))
    ]


def lane_broadcast(line):
    return jnp.broadcast_to(line, (128, line.shape[1])).T


def opening_kernel(count, valid_rows, ids, *refs):
    refs = list(refs)
    take = lambda n: [refs.pop(0) for _ in range(n)]
    pieces = [take(1 if k == 0 else 2) for k in range(count)]
    turned, partner, offsets = take(3)
    row_proj, row_off, slab, features, parts, proj_sem, in_sem = take(7)
    rows = row_proj.shape[0]
    own, slab_rows = rows // 2, slab.shape[1]
    core = ids[(valid_rows + LAG) // slab_rows]
    row_loads = [
        pltpu.make_async_copy(turned.at[pl.ds(0, own)], row_proj.at[pl.ds(0, own)], proj_sem.at[0]),
        pltpu.make_async_copy(partner.at[pl.ds(0, own)], row_proj.at[pl.ds(own, own)], proj_sem.at[1]),
        pltpu.make_async_copy(partner.at[pl.ds(own, SPARE)], parts, proj_sem.at[2]),
    ]
    loads = [slab_copies(pieces[k], core, slab.at[k], in_sem.at[k]) for k in range(count)]
    start([row_loads[0], *loads[0], *row_loads[1:]])
    row_off[:own] = lane_broadcast(offsets[...])
    wait(row_loads[:1])
    for k in range(count):
        wait(loads[k])
        if k == 0:
            start([copy for load in loads[1:] for copy in load])
        turned_states = slab[k].T
        for n, part in enumerate((slice(0, own), slice(own, rows))):
            if k == 0 and n == 1:
                wait(row_loads[1:])
                row_off[own:] = lane_broadcast(jnp.sum(parts[:, :own].astype(jnp.float32), axis=0, keepdims=True))
            features[k, part] = row_features(
                row_proj[part], turned_states, row_off[part], ids[k] * slab_rows, valid_rows
            )


def opening(slabs, numbers, turned, partner, offsets, slab_rows, valid_rows):
    rows, units, count = 2 * (turned.shape[0] - SPARE), turned.shape[1], len(slabs)
    pieces = [p for s in slabs for p in s]
    dma = pltpu.SemaphoreType.DMA
    return pl.pallas_call(
        functools.partial(opening_kernel, count, valid_rows),
        in_specs=[smem_spec()] + [any_spec()] * (len(pieces) + 2) + [vmem_spec()],
        out_specs=[vmem_spec()] * 4,
        out_shape=[
            pltpu.VMEM((rows, units), jnp.bfloat16),
            pltpu.VMEM((rows, 128), jnp.float32),
            pltpu.VMEM((count, slab_rows, units), jnp.bfloat16),
            pltpu.VMEM((count, rows, slab_rows), jnp.bfloat16),
        ],
        scratch_shapes=[pltpu.VMEM((SPARE, units), jnp.bfloat16), dma((3,)), dma((count, 2))],
        compiler_params=pltpu.CompilerParams(vmem_limit_bytes=12 * MIB),
        cost_estimate=pl.CostEstimate(
            flops=2 * count * slab_rows * units * rows, bytes_accessed=2 * count * slab_rows * units,
            transcendentals=count * slab_rows * rows,
        ),
    )(numbers, *pieces, turned, partner, offsets)


def moments_kernel(count, ready, at, last, slab_rows, valid_rows, *refs):
    first = not last
    refs = list(refs)
    take = lambda n: [refs.pop(0) for _ in range(n)]
    (ids,) = take(1)
    slabs = (valid_rows + LAG) // slab_rows
    pieces = [take(1 if last and k == 0 else 2) for k in range(slabs if last else count - ready)]
    here = [None] * ready + pieces[ready - count:]
    if first:
        ready_slab, ready_rows, *columns, row_proj, row_off = take(6)
    else:
        row_proj, row_off, col_proj, row_next, col_next = take(5)
        take(2)
        acc_out = take(2)
    instant, lagged = take(2)
    if first:
        col_proj, row_next, col_next = take(3)
    slab, turned_states, row_a, row_b, col_a, col_b, in_sem = take(7)
    if first:
        (proj_sem,) = take(1)
    if last:
        instant_end, lagged_end, tails, heads, turned_edges, edge_sem, out_sem = take(7)
    rows, cols = instant.shape
    units = col_proj.shape[0] - SPARE
    half = slab_rows // 2
    time_tile, col_tile = slab_rows // TIME_TILES, cols // COL_TILES
    core, col, source = ids[slabs], ids[slabs + 1], ids[slabs + 2]
    number = lambda k: ids[at + k]

    loads = [[] if k < ready else slab_copies(here[k], core, slab.at[k - ready], in_sem.at[k - ready]) for k in range(count)]
    states = lambda k: ready_slab.at[k] if k < ready else slab.at[k - ready]
    between = count - 1 if first else 0
    row_bufs = lambda k: row_next if k == between else (row_a, row_b)[k % 2]
    col_bufs = lambda k: col_next if k == between else (col_a, col_b)[k % 2]
    col_loads, edge_loads = [], []
    if first:
        col_loads = [OneOf(source, columns, col_proj, proj_sem)]
    if last:
        for k, piece in enumerate(pieces):
            tail, head = tails.at[ids[k]], heads.at[lax.rem(ids[k] + slabs - 1, slabs)]
            if len(piece) == 1:
                edge_loads.append(pltpu.make_async_copy(piece[0].at[pl.ds(slab_rows - LAG, LAG)], tail, edge_sem.at[k, 0]))
                edge_loads.append(pltpu.make_async_copy(piece[0].at[pl.ds(0, LAG)], head, edge_sem.at[k, 1]))
            else:
                ends = [p.at[pl.ds(half - LAG, LAG)] for p in piece]
                starts = [p.at[pl.ds(0, LAG)] for p in piece]
                edge_loads.append(OneOf(1 - core, ends, tail, edge_sem.at[k, 0]))
                edge_loads.append(OneOf(core, starts, head, edge_sem.at[k, 1]))
    start([*col_loads, *loads[ready]])

    for buf in (col_a, col_b) + ((col_next,) if first else ()):
        buf[slab_rows:] = jnp.zeros_like(buf[slab_rows:])

    row_part = lambda h: slice(h * rows // 2, (h + 1) * rows // 2)

    def row_tile(k, u, h):
        span, part = slice(u * time_tile, (u + 1) * time_tile), row_part(h)
        if h == 0:
            turned_states[...] = states(k)[span].T
        row_bufs(k)[part, span] = row_features(
            row_proj[part], turned_states[...], row_off[part], number(k) * slab_rows + u * time_tile, valid_rows
        )

    def col_off(span):
        return jnp.sum(col_proj[units:, span].astype(jnp.float32), axis=0, keepdims=True)

    def col_tile_features(k, n, h):
        span, part = slice(n * col_tile, (n + 1) * col_tile), slice(h * half, (h + 1) * half)
        col_bufs(k)[part, span] = col_features(states(k)[part], col_proj[:units, span], col_off(span))

    def edge_rows(h):
        size, part = slabs * LAG, row_part(h)
        if h == 0:
            turned_edges[...] = tails[...].reshape(size, units).T
        row_bufs(count)[part, :size] = row_features(
            row_proj[part], turned_edges[...], row_off[part], 0, (slabs - 1) * LAG
        )

    def edge_cols(n):
        span = slice(n * col_tile, (n + 1) * col_tile)
        col_bufs(count)[:slabs * LAG, span] = col_features(
            heads[...].reshape(slabs * LAG, units), col_proj[:units, span], col_off(span)
        )

    def moment_tile(k, lag, n, h):
        span, part = slice(n * col_tile, (n + 1) * col_tile), row_part(h)
        acc = lagged if lag else instant
        buf_r, buf_c = row_bufs(k), col_bufs(k)
        if k < count:
            value = jnp.dot(ready_rows[k, part] if k < ready and first else buf_r[part], buf_c[lag:lag + slab_rows, span], preferred_element_type=jnp.float32)
        else:
            value = jnp.dot(buf_r[part, :slabs * LAG], buf_c[:slabs * LAG, span], preferred_element_type=jnp.float32)
        if k > 0 or not first:
            value = acc[part, span] + value
        if last and k == (count if lag else count - 1):
            end = lagged_end if lag else instant_end
            value = value * (1.0 / valid_rows)
            groups = cols // 128
            for g in range(col_tile // 128):
                at = h * (rows // 2) * groups + n * (col_tile // 128) + g
                end[pl.ds(at, rows // 2, stride=groups), :] = value[:, g * 128:(g + 1) * 128]
            if n == COL_TILES - 1:
                start([stores[1 if lag else 0][h]])
        else:
            acc[part, span] = value

    def feature_steps(k):
        steps = [functools.partial(col_tile_features, k, n, h) for n in range(COL_TILES) for h in range(2)]
        if k >= ready:
            steps += [functools.partial(row_tile, k, u, h) for u in range(TIME_TILES) for h in range(2)]
        return steps

    def interleave(steps, others):
        done = 0
        for n, step in enumerate(steps):
            upto = (n + 1) * len(others) // len(steps)
            for other in others[done:upto]:
                other()
            done = upto
            step()

    stores = []
    if last:
        for m, (a, b) in enumerate(zip((instant_end, lagged_end), acc_out)):
            size = a.shape[0] // 2
            stores.append([
                pltpu.make_async_copy(
                    a.at[pl.ds(n * size, size)], b.at[pl.ds(pl.multiple_of(place * size, 8), size)], out_sem.at[m, n]
                )
                for n, place in enumerate((col, 1 - col))
            ])

    if first:
        wait(col_loads)
        for step in feature_steps(0):
            step()
    for k in range(count - 1 if first else count):
        ahead = []
        steps = [functools.partial(moment_tile, k, lag, n, h) for lag in (0, LAG) for h in range(2) for n in range(COL_TILES)]
        if last and k == 0:
            steps.pop(0)()
            steps.pop(0)()
        if k + 1 < count:
            wait(loads[k + 1])
            if k == 0:
                start([copy for load in loads[ready + 1:] for copy in load] + edge_loads)
            ahead = feature_steps(k + 1)
        elif last:
            wait(edge_loads)
            ahead = [functools.partial(edge_cols, n) for n in range(COL_TILES)]
            ahead += [functools.partial(edge_rows, h) for h in range(2)]
        interleave(steps, ahead)
    if last:
        for h in range(2):
            for n in range(COL_TILES):
                moment_tile(count, LAG, n, h)
        wait(stores[0] + stores[1])


def moments(slabs, count, numbers, opened, panels, carry, slab_rows, valid_rows):
    first, last = carry is None, carry is not None
    units = slabs[0][0].shape[1]
    cols = panels[0].shape[1] if first else carry[0].shape[1]
    rows = 2 * cols
    at = len(slabs) - count
    ready = opened[0].shape[0] if first else 1
    if first:
        slabs = slabs[at + ready:]
    pieces = [p for s in slabs for p in s]
    end_shape = (rows * cols // 128, 128)
    outs = [pltpu.VMEM((rows, cols), jnp.float32)] * 2
    dma = pltpu.SemaphoreType.DMA
    scratch = [
        pltpu.VMEM((count - ready, slab_rows, units), jnp.bfloat16),
        pltpu.VMEM((units, slab_rows // TIME_TILES), jnp.bfloat16),
        pltpu.VMEM((rows, slab_rows), jnp.bfloat16),
        pltpu.VMEM((rows, slab_rows), jnp.bfloat16),
        pltpu.VMEM((slab_rows + LAG, cols), jnp.bfloat16),
        pltpu.VMEM((slab_rows + LAG, cols), jnp.bfloat16),
        dma((count - ready, 2)),
    ]
    args = [numbers, *pieces]
    specs = [smem_spec()] + [any_spec()] * len(pieces)
    aliases = {}
    if first:
        args += [*map(in_vmem, opened), *panels[:2], *map(in_vmem, panels[2:])]
        specs += [vmem_spec()] * 2 + [any_spec()] * 2 + [vmem_spec()] * 2
        outs = outs + [
            pltpu.VMEM((units + SPARE, cols), jnp.bfloat16),
            pltpu.VMEM((rows, slab_rows), jnp.bfloat16),
            pltpu.VMEM((slab_rows + LAG, cols), jnp.bfloat16),
        ]
        out_specs = [vmem_spec()] * 5
        scratch.append(dma)
    else:
        outs, out_specs = [pltpu.HBM(end_shape, jnp.float32)] * 2 + outs, [hbm_spec()] * 2 + [vmem_spec()] * 2
        scratch += [pltpu.VMEM(end_shape, jnp.float32)] * 2
        scratch += [pltpu.VMEM((len(slabs), LAG, units), jnp.bfloat16)] * 2
        scratch += [pltpu.VMEM((units, len(slabs) * LAG), jnp.bfloat16), dma((len(slabs), 2)), dma((2, 2))]
        args += [in_vmem(x) for x in (*panels, *carry[2:], *carry[:2])]
        specs += [vmem_spec()] * 7
        aliases = {len(args) - 2 + n: 2 + n for n in range(2)}
    return pl.pallas_call(
        functools.partial(moments_kernel, count, ready, at, last, slab_rows, valid_rows),
        in_specs=specs,
        out_specs=out_specs,
        out_shape=outs,
        scratch_shapes=scratch,
        input_output_aliases=aliases,
        compiler_params=pltpu.CompilerParams(vmem_limit_bytes=(24 if last else 16) * MIB),
        cost_estimate=pl.CostEstimate(
            flops=2 * count * slab_rows * (units * (rows + cols) + 2 * rows * cols),
            bytes_accessed=2 * count * slab_rows * units,
            transcendentals=count * slab_rows * (rows + cols),
        ),
    )(*args)


def on_device(states, projection, offsets):
    slab_rows = states.shape[0]
    tm_count = lax.axis_size("tm")
    tm, row, col = (lax.axis_index(a) for a in AXES)
    x_hi, y, core = tm // Y, tm % Y, row % 2
    valid_rows = slab_rows * tm_count - LAG
    cols = projection.shape[1]
    swap = lambda piece: move(piece, other_core)

    y_first, y_second = y - 1 + 2 * core, y + 1 - 2 * core
    place = lambda other, at: jnp.where(other, 1 - x_hi, x_hi) * Y + at % Y
    ids = [tm, place(False, y_first), place(False, y_second), place(True, y), place(False, y + 2),
           place(True, y_first), place(True, y_second), place(True, y + 2)]
    source, steps = jnp.where(core == y % 2, 0, 1), (row // 2 - tm // 2) % 4
    numbers = jnp.stack([*ids, core, col, source, steps]).astype(jnp.int32)
    after = len(ids)
    line = offsets[None, :]
    numbers, line = lax.optimization_barrier((numbers, line))
    sizes = (slab_rows, valid_rows)

    columns, turned, mine = prepare(after, numbers, projection, line, states)
    ahead, behind = move(columns, along_z(1)), move(columns, along_z(-1))
    over, partner, y_out = move(mine, crossing), move(turned, inner), move(mine, out_y)
    ahead, columns = lax.optimization_barrier((ahead, columns))
    beyond = move(columns, along_z(2))
    y_out, mine = lax.optimization_barrier((y_out, mine))
    y_back = move(mine, back_y)
    over, y_out = lax.optimization_barrier((over, y_out))
    swapped_out = swap(y_out)
    ahead, behind, beyond, partner, y_back, swapped_out = lax.optimization_barrier(
        (ahead, behind, beyond, partner, y_back, swapped_out)
    )

    panel = pick(after + 3, numbers, columns, ahead, beyond, behind)
    swapped = swap(panel)
    swapped_back, swapped_over = swap(y_back), swap(over)
    slabs = [(in_hbm(states),), (y_out, swapped_back), (y_back, swapped_out)]
    row_proj, row_off, *opened = opening(slabs, numbers, turned, partner, line, *sizes)

    over_out, y_far, over_back = move(over, out_y), move(y_out, out_y), move(y_back, crossing)
    row_off, over_out = lax.optimization_barrier((row_off, over_out))
    over_far = move(over_out, out_y)
    slabs += [(over, swapped_over)]
    carry = moments(slabs, 4, numbers, opened, (panel, swapped, row_proj, row_off), None, *sizes)

    *carry, y_far, over_back, over_far = lax.optimization_barrier((*carry, y_far, over_back, over_far))
    slabs += [(y_far, swap(y_far)), (over_out, swap(over_back)), (over_back, swap(over_out)), (over_far, swap(over_far))]
    instant, lagged, *_ = moments(slabs, 5, numbers, None, (row_proj, row_off), carry, *sizes)
    shape = (2 * cols, 1, cols)
    return instant.reshape(shape), lagged.reshape(shape)


def solution(mesh):
    return jax.shard_map(
        on_device,
        mesh=mesh,
        in_specs=(P("tm", None), P(None, ("row", "col")), P(("row", "col"))),
        out_specs=(P("row", "tm", "col"), P("row", "tm", "col")),
        check_vma=False,
    )
```

profile of v0, /device:TPU:1, one launch (start us, length us, event | category | flops | bytes accessed | tf_op | source)
XLA Modules:
  0.0 99.2 jit_solution(1614834305356987716)
XLA Ops:
  0.8 0.1 stack.51.numbers.ids.refs_0_
  0.9 2.1 %shard_map.50 = (bf16[1040,512]{1,0:T(8,128)(2,1)S(1)}, bf16[528,1024]{1,0:T(8,128)(2,1)S(1)}, bf16[384,1024]{1,0:T(8,128)(2,1)S(1)}) custom-call(s32[12]{0:T(128)S(1)} %stack.51.numbers.ids.refs_0_, bf16[1024,512]{1,0:T(8,128)(2,1)} %projection.1, f32[1,512]{1,0:T(1,128)} %bitcast.15, bf16[768,1024]{1,0:T(8,128)(2,1)} %refs_1_.1), custom_call_target="tpu_custom_call" | custom-call | tf_op jit(solution)/shard_map/pallas_call | solution.py:138
  3.0 0.7 collective-permute-start.2
  3.7 3.6 %collective-permute-start.1 = (bf16[384,1024]{1,0:T(8,128)(2,1)S(1)}, bf16[384,1024]{1,0:T(8,128)(2,1)S(1)}, u32[]{:S(2)}, u32[]{:S(2)}) collective-permute-start(bf16[384,1024]{1,0:T(8,128)(2,1)S(1)} %get-tuple-element.49), channel_id=1, source_target_pairs={{0,16},{1,17},{2,50},{3,51},{4,20},{5,21},{6,54},{7,55},{8,24},{9,... | collective-permute-start | bytes 2359304 | tf_op jit(solution)/shard_map/ppermute | solution.py:32
  7.4 3.0 %collective-permute-start = (bf16[384,1024]{1,0:T(8,128)(2,1)S(1)}, bf16[384,1024]{1,0:T(8,128)(2,1)S(1)}, u32[]{:S(2)}, u32[]{:S(2)}) collective-permute-start(bf16[384,1024]{1,0:T(8,128)(2,1)S(1)} %get-tuple-element.49), channel_id=1, source_target_pairs={{0,65},{1,64},{2,67},{3,66},{4,69},{5,68},{6,71},{7,70},{8,73},{9,... | collective-permute-start | bytes 2359304 | tf_op jit(solution)/shard_map/ppermute | solution.py:32
  10.4 0.0 copy-start
  10.4 0.0 collective-permute-start.5
  10.4 0.8 collective-permute-start.3
  11.3 0.0 collective-permute-done.2.refs_1_
  11.3 0.7 collective-permute-start.4
  12.0 6.5 %collective-permute-done.1.refs_1_.refs_2_ = bf16[384,1024]{1,0:T(8,128)(2,1)S(1)} collective-permute-done((bf16[384,1024]{1,0:T(8,128)(2,1)S(1)}, bf16[384,1024]{1,0:T(8,128)(2,1)S(1)}, u32[]{:S(2)}, u32[]{:S(2)}) %collective-permute-start.1) | collective-permute-done | bytes 786464 | tf_op jit(solution)/shard_map/ppermute | solution.py:32
  18.5 3.5 %collective-permute-start.6 = (bf16[384,1024]{1,0:T(8,128)(2,1)S(1)}, bf16[384,1024]{1,0:T(8,128)(2,1)S(1)}, u32[]{:S(2)}, u32[]{:S(2)}) collective-permute-start(bf16[384,1024]{1,0:T(8,128)(2,1)S(1)} %get-tuple-element.49), channel_id=1, source_target_pairs={{0,48},{1,49},{2,18},{3,19},{4,52},{5,53},{6,22},{7,23},{8,56},{9,... | collective-permute-start | bytes 2359304 | tf_op jit(solution)/shard_map/ppermute | solution.py:32
  22.0 5.2 %collective-permute-done.refs_1_.refs_6_ = bf16[384,1024]{1,0:T(8,128)(2,1)S(1)} collective-permute-done((bf16[384,1024]{1,0:T(8,128)(2,1)S(1)}, bf16[384,1024]{1,0:T(8,128)(2,1)S(1)}, u32[]{:S(2)}, u32[]{:S(2)}) %collective-permute-start) | collective-permute-done | bytes 786464 | tf_op jit(solution)/shard_map/ppermute | solution.py:32
  27.2 1.7 %collective-permute-start.7 = (bf16[384,1024]{1,0:T(8,128)(2,1)S(1)}, bf16[384,1024]{1,0:T(8,128)(2,1)S(1)}, u32[]{:S(2)}, u32[]{:S(2)}) collective-permute-start(bf16[384,1024]{1,0:T(8,128)(2,1)S(1)} %collective-permute-done.1.refs_1_.refs_2_), channel_id=1, source_target_pairs={{0,2},{1,3},{2,0},{3,1},{4,6},{5,7},{6,4},{7,5},{8,10},{9,11},{10,... | collective-permute-start | bytes 2359304 | tf_op jit(solution)/shard_map/ppermute | solution.py:32
  28.9 0.0 collective-permute-done.3.refs_3_
  28.9 6.8 %collective-permute-done.5.refs_6_ = bf16[528,1024]{1,0:T(8,128)(2,1)S(1)} collective-permute-done((bf16[528,1024]{1,0:T(8,128)(2,1)S(1)}, bf16[528,1024]{1,0:T(8,128)(2,1)S(1)}, u32[]{:S(2)}, u32[]{:S(2)}) %collective-permute-start.5) | collective-permute-done | bytes 1081376 | tf_op jit(solution)/shard_map/ppermute | solution.py:32
  35.7 0.0 collective-permute-done.6.refs_3_.refs_4_
  35.7 0.0 collective-permute-done.7.refs_4_.refs_5_
  35.7 0.0 collective-permute-done.4.refs_2_
  35.7 0.5 collective-permute-start.8
  36.2 0.7 shard_map.52.refs_5_
  36.9 0.2 collective-permute-start.10
  37.1 0.7 collective-permute-start.11
  37.7 0.0 collective-permute-start.9
  37.7 2.7 %collective-permute-start.12 = (bf16[384,1024]{1,0:T(8,128)(2,1)S(1)}, bf16[384,1024]{1,0:T(8,128)(2,1)S(1)}, u32[]{:S(2)}, u32[]{:S(2)}) collective-permute-start(bf16[384,1024]{1,0:T(8,128)(2,1)S(1)} %collective-permute-done.1.refs_1_.refs_2_), channel_id=1, source_target_pairs={{0,16},{1,17},{2,50},{3,51},{4,20},{5,21},{6,54},{7,55},{8,24},{9,... | collective-permute-start | bytes 2359304 | tf_op jit(solution)/shard_map/ppermute | solution.py:32
  40.4 0.0 collective-permute-done.8.refs_2_.refs_3_
  40.4 4.9 %collective-permute-start.13 = (bf16[384,1024]{1,0:T(8,128)(2,1)S(1)}, bf16[384,1024]{1,0:T(8,128)(2,1)S(1)}, u32[]{:S(2)}, u32[]{:S(2)}) collective-permute-start(bf16[384,1024]{1,0:T(8,128)(2,1)S(1)} %collective-permute-done.6.refs_3_.refs_4_), channel_id=1, source_target_pairs={{0,65},{1,64},{2,67},{3,66},{4,69},{5,68},{6,71},{7,70},{8,73},{9,... | collective-permute-start | bytes 2359304 | tf_op jit(solution)/shard_map/ppermute | solution.py:32
  45.3 0.0 copy-done
  45.3 8.6 %shard_map.51 = (bf16[1024,1024]{1,0:T(8,128)(2,1)S(1)}, f32[1024,128]{1,0:T(8,128)S(1)}, bf16[3,768,1024]{2,1,0:T(8,128)(2,1)S(1)}, bf16[3,1024,768]{2,1,0:T(8,128)(2,1)S(1)}) custom-call(s32[12]{0:T(128)S(1)} %stack.51.numbers.ids.refs_0_, bf16[768,1024]{1,0:T(8,128)(2,1)} %refs_1_.1, bf16[384,1024]{1,0:T(8,128)(2,1)S(1)} %collective-permute-done.1.refs_1_.refs_2_, ...), custom_call_target="tpu_custom_call" | custom-call | flops 4831838208 | bytes 4718592 | tf_op jit(solution)/shard_map/pallas_call | solution.py:230
  53.9 0.0 collective-permute-done.11.refs_10_
  53.9 0.1 collective-permute-start.17
  54.0 0.0 collective-permute-done.9.refs_2_.refs_7_
  54.1 0.4 collective-permute-start.14
  54.5 0.0 collective-permute-done.10.refs_6_
  54.5 11.3 %shard_map.53 = (f32[1024,512]{1,0:T(8,128)S(1)}, f32[1024,512]{1,0:T(8,128)S(1)}, bf16[1040,512]{1,0:T(8,128)(2,1)S(1)}, bf16[1024,768]{1,0:T(8,128)(2,1)S(1)}, bf16[832,512]{1,0:T(8,128)(2,1)S(1)}) custom-call(s32[12]{0:T(128)S(1)} %stack.51.numbers.ids.refs_0_, bf16[384,1024]{1,0:T(8,128)(2,1)S(1)} %collective-permute-done.refs_1_.refs_6_, ...), custom_call_target="tpu_custom_call" | custom-call | flops 16106127360 | bytes 6291456 | tf_op jit(solution)/shard_map/pallas_call | solution.py:451
  65.8 0.0 collective-permute-done.12.refs_8_
  65.8 0.0 collective-permute-done.13.refs_12_
  65.8 0.0 collective-permute-done.14.refs_14_
  65.8 1.9 %collective-permute-start.15 = (bf16[384,1024]{1,0:T(8,128)(2,1)S(1)}, bf16[384,1024]{1,0:T(8,128)(2,1)S(1)}, u32[]{:S(2)}, u32[]{:S(2)}) collective-permute-start(bf16[384,1024]{1,0:T(8,128)(2,1)S(1)} %collective-permute-done.12.refs_8_), channel_id=1, source_target_pairs={{0,2},{1,3},{2,0},{3,1},{4,6},{5,7},{6,4},{7,5},{8,10},{9,11},{10,... | collective-permute-start | bytes 2359304 | tf_op jit(solution)/shard_map/ppermute | solution.py:32
  67.7 0.0 collective-permute-start.16
  67.7 0.5 collective-permute-start.18
  68.3 0.0 collective-permute-done.17.refs_13_
  68.3 1.4 %collective-permute-done.15.refs_9_ = bf16[384,1024]{1,0:T(8,128)(2,1)S(1)} collective-permute-done((bf16[384,1024]{1,0:T(8,128)(2,1)S(1)}, bf16[384,1024]{1,0:T(8,128)(2,1)S(1)}, u32[]{:S(2)}, u32[]{:S(2)}) %collective-permute-start.15) | collective-permute-done | bytes 786464 | tf_op jit(solution)/shard_map/ppermute | solution.py:32
  69.7 1.1 %collective-permute-done.16.refs_11_ = bf16[384,1024]{1,0:T(8,128)(2,1)S(1)} collective-permute-done((bf16[384,1024]{1,0:T(8,128)(2,1)S(1)}, bf16[384,1024]{1,0:T(8,128)(2,1)S(1)}, u32[]{:S(2)}, u32[]{:S(2)}) %collective-permute-start.16) | collective-permute-done | bytes 786464 | tf_op jit(solution)/shard_map/ppermute | solution.py:32
  70.8 1.1 %collective-permute-done.18.refs_15_ = bf16[384,1024]{1,0:T(8,128)(2,1)S(1)} collective-permute-done((bf16[384,1024]{1,0:T(8,128)(2,1)S(1)}, bf16[384,1024]{1,0:T(8,128)(2,1)S(1)}, u32[]{:S(2)}, u32[]{:S(2)}) %collective-permute-start.18) | collective-permute-done | bytes 786464 | tf_op jit(solution)/shard_map/ppermute | solution.py:32
  71.9 27.1 %shard_map.54 = (f32[4096,128]{1,0:T(8,128)}, f32[4096,128]{1,0:T(8,128)}, f32[1024,512]{1,0:T(8,128)S(1)}, f32[1024,512]{1,0:T(8,128)S(1)}) custom-call(s32[12]{0:T(128)S(1)} %stack.51.numbers.ids.refs_0_, bf16[768,1024]{1,0:T(8,128)(2,1)} %refs_1_.1, ...), custom_call_target="tpu_custom_call", output_to_operand_aliasing={{2}: (21, {}), {3}: (22, {})} | custom-call | flops 20132659200 | bytes 7864320 | tf_op jit(solution)/shard_map/pallas_call | solution.py:451
Async XLA Ops:
  3.0 8.3 %collective-permute-start.2 = (bf16[1040,512]{1,0:T(8,128)(2,1)S(1)}, bf16[1040,512]{1,0:T(8,128)(2,1)S(1)}, u32[]{:S(2)}, u32[]{:S(2)}) collective-permute-start(bf16[1040,512]{1,0:T(8,128)(2,1)S(1)} %get-tuple-element.47.refs_0_), channel_id=1, source_target_pairs={{0,4},{1,5},{18,22},{19,23},{36,40},{37,41},{54,58},{55,59},{72,76... | collective-permute-start | bytes 3194888 | tf_op jit(solution)/shard_map/ppermute | solution.py:32
  3.7 14.8 %collective-permute-start.1 = (bf16[384,1024]{1,0:T(8,128)(2,1)S(1)}, bf16[384,1024]{1,0:T(8,128)(2,1)S(1)}, u32[]{:S(2)}, u32[]{:S(2)}) collective-permute-start(bf16[384,1024]{1,0:T(8,128)(2,1)S(1)} %get-tuple-element.49), channel_id=1, source_target_pairs={{0,16},{1,17},{2,50},{3,51},{4,20},{5,21},{6,54},{7,55},{8,24},{9,... | collective-permute-start | bytes 2359304 | tf_op jit(solution)/shard_map/ppermute | solution.py:32
  7.4 19.8 %collective-permute-start = (bf16[384,1024]{1,0:T(8,128)(2,1)S(1)}, bf16[384,1024]{1,0:T(8,128)(2,1)S(1)}, u32[]{:S(2)}, u32[]{:S(2)}) collective-permute-start(bf16[384,1024]{1,0:T(8,128)(2,1)S(1)} %get-tuple-element.49), channel_id=1, source_target_pairs={{0,65},{1,64},{2,67},{3,66},{4,69},{5,68},{6,71},{7,70},{8,73},{9,... | collective-permute-start | bytes 2359304 | tf_op jit(solution)/shard_map/ppermute | solution.py:32
  10.4 34.9 %copy-start = (f32[512]{0:T(512)S(1)}, f32[512]{0:T(512)}, u32[]{:S(2)}) copy-start(f32[512]{0:T(512)} %param.5) | copy-start | bytes 6148
  10.4 25.3 %collective-permute-start.5 = (bf16[528,1024]{1,0:T(8,128)(2,1)S(1)}, bf16[528,1024]{1,0:T(8,128)(2,1)S(1)}, u32[]{:S(2)}, u32[]{:S(2)}) collective-permute-start(bf16[528,1024]{1,0:T(8,128)(2,1)S(1)} %get-tuple-element.48.refs_5_), channel_id=1, source_target_pairs={{0,1},{1,0},{2,3},{3,2},{4,5},{5,4},{6,7},{7,6},{8,9},{9,8},{10,11... | collective-permute-start | bytes 3244040 | tf_op jit(solution)/shard_map/ppermute | solution.py:32
  10.4 18.5 %collective-permute-start.3 = (bf16[1040,512]{1,0:T(8,128)(2,1)S(1)}, bf16[1040,512]{1,0:T(8,128)(2,1)S(1)}, u32[]{:S(2)}, u32[]{:S(2)}) collective-permute-start(bf16[1040,512]{1,0:T(8,128)(2,1)S(1)} %get-tuple-element.47.refs_0_), channel_id=1, source_target_pairs={{0,12},{1,13},{18,30},{19,31},{36,32},{37,33},{54,50},{55,51},{72,... | collective-permute-start | bytes 3194888 | tf_op jit(solution)/shard_map/ppermute | solution.py:32
  11.3 24.4 %collective-permute-start.4 = (bf16[1040,512]{1,0:T(8,128)(2,1)S(1)}, bf16[1040,512]{1,0:T(8,128)(2,1)S(1)}, u32[]{:S(2)}, u32[]{:S(2)}) collective-permute-start(bf16[1040,512]{1,0:T(8,128)(2,1)S(1)} %get-tuple-element.47.refs_0_), channel_id=1, source_target_pairs={{0,8},{1,9},{18,26},{19,27},{36,44},{37,45},{54,62},{55,63},{72,64... | collective-permute-start | bytes 3194888 | tf_op jit(solution)/shard_map/ppermute | solution.py:32
  18.5 17.2 %collective-permute-start.6 = (bf16[384,1024]{1,0:T(8,128)(2,1)S(1)}, bf16[384,1024]{1,0:T(8,128)(2,1)S(1)}, u32[]{:S(2)}, u32[]{:S(2)}) collective-permute-start(bf16[384,1024]{1,0:T(8,128)(2,1)S(1)} %get-tuple-element.49), channel_id=1, source_target_pairs={{0,48},{1,49},{2,18},{3,19},{4,52},{5,53},{6,22},{7,23},{8,56},{9,... | collective-permute-start | bytes 2359304 | tf_op jit(solution)/shard_map/ppermute | solution.py:32
  27.2 8.5 %collective-permute-start.7 = (bf16[384,1024]{1,0:T(8,128)(2,1)S(1)}, bf16[384,1024]{1,0:T(8,128)(2,1)S(1)}, u32[]{:S(2)}, u32[]{:S(2)}) collective-permute-start(bf16[384,1024]{1,0:T(8,128)(2,1)S(1)} %collective-permute-done.1.refs_1_.refs_2_), channel_id=1, source_target_pairs={{0,2},{1,3},{2,0},{3,1},{4,6},{5,7},{6,4},{7,5},{8,10},{9,11},{10,... | collective-permute-start | bytes 2359304 | tf_op jit(solution)/shard_map/ppermute | solution.py:32
  35.7 4.7 %collective-permute-start.8 = (bf16[384,1024]{1,0:T(8,128)(2,1)S(1)}, bf16[384,1024]{1,0:T(8,128)(2,1)S(1)}, u32[]{:S(2)}, u32[]{:S(2)}) collective-permute-start(bf16[384,1024]{1,0:T(8,128)(2,1)S(1)} %collective-permute-done.6.refs_3_.refs_4_), channel_id=1, source_target_pairs={{0,2},{1,3},{2,0},{3,1},{4,6},{5,7},{6,4},{7,5},{8,10},{9,11},{10,... | collective-permute-start | bytes 2359304 | tf_op jit(solution)/shard_map/ppermute | solution.py:32
  36.9 17.6 %collective-permute-start.10 = (bf16[1040,512]{1,0:T(8,128)(2,1)S(1)}, bf16[1040,512]{1,0:T(8,128)(2,1)S(1)}, u32[]{:S(2)}, u32[]{:S(2)}) collective-permute-start(bf16[1040,512]{1,0:T(8,128)(2,1)S(1)} %shard_map.52.refs_5_), channel_id=1, source_target_pairs={{0,2},{1,3},{2,0},{3,1},{4,6},{5,7},{6,4},{7,5},{8,10},{9,11},{10,... | collective-permute-start | bytes 3194888 | tf_op jit(solution)/shard_map/ppermute | solution.py:32
  37.1 16.9 %collective-permute-start.11 = (bf16[384,1024]{1,0:T(8,128)(2,1)S(1)}, bf16[384,1024]{1,0:T(8,128)(2,1)S(1)}, u32[]{:S(2)}, u32[]{:S(2)}) collective-permute-start(bf16[384,1024]{1,0:T(8,128)(2,1)S(1)} %collective-permute-done.refs_1_.refs_6_), channel_id=1, source_target_pairs={{0,16},{1,17},{2,50},{3,51},{4,20},{5,21},{6,54},{7,55},{8,24},{9,... | collective-permute-start | bytes 2359304 | tf_op jit(solution)/shard_map/ppermute | solution.py:32
  37.7 16.3 %collective-permute-start.9 = (bf16[384,1024]{1,0:T(8,128)(2,1)S(1)}, bf16[384,1024]{1,0:T(8,128)(2,1)S(1)}, u32[]{:S(2)}, u32[]{:S(2)}) collective-permute-start(bf16[384,1024]{1,0:T(8,128)(2,1)S(1)} %collective-permute-done.refs_1_.refs_6_), channel_id=1, source_target_pairs={{0,2},{1,3},{2,0},{3,1},{4,6},{5,7},{6,4},{7,5},{8,10},{9,11},{10,... | collective-permute-start | bytes 2359304 | tf_op jit(solution)/shard_map/ppermute | solution.py:32
  37.7 28.1 %collective-permute-start.12 = (bf16[384,1024]{1,0:T(8,128)(2,1)S(1)}, bf16[384,1024]{1,0:T(8,128)(2,1)S(1)}, u32[]{:S(2)}, u32[]{:S(2)}) collective-permute-start(bf16[384,1024]{1,0:T(8,128)(2,1)S(1)} %collective-permute-done.1.refs_1_.refs_2_), channel_id=1, source_target_pairs={{0,16},{1,17},{2,50},{3,51},{4,20},{5,21},{6,54},{7,55},{8,24},{9,... | collective-permute-start | bytes 2359304 | tf_op jit(solution)/shard_map/ppermute | solution.py:32
  40.4 25.4 %collective-permute-start.13 = (bf16[384,1024]{1,0:T(8,128)(2,1)S(1)}, bf16[384,1024]{1,0:T(8,128)(2,1)S(1)}, u32[]{:S(2)}, u32[]{:S(2)}) collective-permute-start(bf16[384,1024]{1,0:T(8,128)(2,1)S(1)} %collective-permute-done.6.refs_3_.refs_4_), channel_id=1, source_target_pairs={{0,65},{1,64},{2,67},{3,66},{4,69},{5,68},{6,71},{7,70},{8,73},{9,... | collective-permute-start | bytes 2359304 | tf_op jit(solution)/shard_map/ppermute | solution.py:32
  53.9 14.3 %collective-permute-start.17 = (bf16[384,1024]{1,0:T(8,128)(2,1)S(1)}, bf16[384,1024]{1,0:T(8,128)(2,1)S(1)}, u32[]{:S(2)}, u32[]{:S(2)}) collective-permute-start(bf16[384,1024]{1,0:T(8,128)(2,1)S(1)} %collective-permute-done.11.refs_10_), channel_id=1, source_target_pairs={{0,2},{1,3},{2,0},{3,1},{4,6},{5,7},{6,4},{7,5},{8,10},{9,11},{10,... | collective-permute-start | bytes 2359304 | tf_op jit(solution)/shard_map/ppermute | solution.py:32
  54.1 11.8 %collective-permute-start.14 = (bf16[384,1024]{1,0:T(8,128)(2,1)S(1)}, bf16[384,1024]{1,0:T(8,128)(2,1)S(1)}, u32[]{:S(2)}, u32[]{:S(2)}) collective-permute-start(bf16[384,1024]{1,0:T(8,128)(2,1)S(1)} %collective-permute-done.11.refs_10_), channel_id=1, source_target_pairs={{0,16},{1,17},{2,50},{3,51},{4,20},{5,21},{6,54},{7,55},{8,24},{9,... | collective-permute-start | bytes 2359304 | tf_op jit(solution)/shard_map/ppermute | solution.py:32
  65.8 3.8 %collective-permute-start.15 = (bf16[384,1024]{1,0:T(8,128)(2,1)S(1)}, bf16[384,1024]{1,0:T(8,128)(2,1)S(1)}, u32[]{:S(2)}, u32[]{:S(2)}) collective-permute-start(bf16[384,1024]{1,0:T(8,128)(2,1)S(1)} %collective-permute-done.12.refs_8_), channel_id=1, source_target_pairs={{0,2},{1,3},{2,0},{3,1},{4,6},{5,7},{6,4},{7,5},{8,10},{9,11},{10,... | collective-permute-start | bytes 2359304 | tf_op jit(solution)/shard_map/ppermute | solution.py:32
  67.7 3.0 %collective-permute-start.16 = (bf16[384,1024]{1,0:T(8,128)(2,1)S(1)}, bf16[384,1024]{1,0:T(8,128)(2,1)S(1)}, u32[]{:S(2)}, u32[]{:S(2)}) collective-permute-start(bf16[384,1024]{1,0:T(8,128)(2,1)S(1)} %collective-permute-done.13.refs_12_), channel_id=1, source_target_pairs={{0,2},{1,3},{2,0},{3,1},{4,6},{5,7},{6,4},{7,5},{8,10},{9,11},{10,... | collective-permute-start | bytes 2359304 | tf_op jit(solution)/shard_map/ppermute | solution.py:32
  67.7 4.2 %collective-permute-start.18 = (bf16[384,1024]{1,0:T(8,128)(2,1)S(1)}, bf16[384,1024]{1,0:T(8,128)(2,1)S(1)}, u32[]{:S(2)}, u32[]{:S(2)}) collective-permute-start(bf16[384,1024]{1,0:T(8,128)(2,1)S(1)} %collective-permute-done.14.refs_14_), channel_id=1, source_target_pairs={{0,2},{1,3},{2,0},{3,1},{4,6},{5,7},{6,4},{7,5},{8,10},{9,11},{10,... | collective-permute-start | bytes 2359304 | tf_op jit(solution)/shard_map/ppermute | solution.py:32
where the time goes:
time: 101 us; the launch traced here: 99.2 us
  Pallas kernels  49.7 us (49%)
  starting transfers between devices  26.1 us (26%)
  waiting for transfers between devices  22.1 us (22%)
  between operations  1.1 us (1%)
    pallas_call x2, Pallas kernels, moments(): pl.pallas_call(functools.partial(moments_kernel, count, ready, at, last,...  38.3 us
    ppermute x19, starting transfers between devices, move(): return lax.ppermute(block, AXES, route(target))  26.1 us
    ppermute x19, waiting for transfers between devices, move(): return lax.ppermute(block, AXES, route(target))  22.1 us
    pallas_call x1, Pallas kernels, opening(): pl.pallas_call(functools.partial(opening_kernel, count, valid_rows), in_s...  8.6 us
    pallas_call x1, Pallas kernels, prepare(): pl.pallas_call(functools.partial(prepare_kernel, at), in_specs=[smem_spec...  2.14 us
  transfers between devices with their start and end apart: 19, of which 6 were waited for; matrix products, arithmetic and copies ran while one was open for 0% of the time, Pallas kernels for 21%

commit v1 on v0

--- a/solution.py
+++ b/solution.py
@@ -206,21 +206,21 @@
         pltpu.make_async_copy(partner.at[pl.ds(own, SPARE)], parts, proj_sem.at[2]),
     ]
     loads = [slab_copies(pieces[k], core, slab.at[k], in_sem.at[k]) for k in range(count)]
-    start([row_loads[0], *loads[0], *row_loads[1:]])
+    start([*row_loads, *loads[0]])
     row_off[:own] = lane_broadcast(offsets[...])
-    wait(row_loads[:1])
+    wait(row_loads)
+    start([copy for load in loads[1:] for copy in load])
+    row_off[own:] = lane_broadcast(jnp.sum(parts[:, :own].astype(jnp.float32), axis=0, keepdims=True))
+    tile = slab_rows // TIME_TILES
     for k in range(count):
         wait(loads[k])
-        if k == 0:
-            start([copy for load in loads[1:] for copy in load])
-        turned_states = slab[k].T
-        for n, part in enumerate((slice(0, own), slice(own, rows))):
-            if k == 0 and n == 1:
-                wait(row_loads[1:])
-                row_off[own:] = lane_broadcast(jnp.sum(parts[:, :own].astype(jnp.float32), axis=0, keepdims=True))
-            features[k, part] = row_features(
-                row_proj[part], turned_states, row_off[part], ids[k] * slab_rows, valid_rows
-            )
+        for u in range(TIME_TILES):
+            span = slice(u * tile, (u + 1) * tile)
+            turned_states = slab[k, span].T
+            for part in (slice(0, own), slice(own, rows)):
+                features[k, part, span] = row_features(
+                    row_proj[part], turned_states, row_off[part], ids[k] * slab_rows + u * tile, valid_rows
+                )
 
 
 def opening(slabs, numbers, turned, partner, offsets, slab_rows, valid_rows):
@@ -267,7 +267,7 @@
     if first:
         (proj_sem,) = take(1)
     if last:
-        instant_end, lagged_end, tails, heads, turned_edges, edge_sem, out_sem = take(7)
+        tails, heads, turned_edges, edge_sem, out_sem = take(5)
     rows, cols = instant.shape
     units = col_proj.shape[0] - SPARE
     half = slab_rows // 2
@@ -341,12 +341,7 @@
         if k > 0 or not first:
             value = acc[part, span] + value
         if last and k == (count if lag else count - 1):
-            end = lagged_end if lag else instant_end
-            value = value * (1.0 / valid_rows)
-            groups = cols // 128
-            for g in range(col_tile // 128):
-                at = h * (rows // 2) * groups + n * (col_tile // 128) + g
-                end[pl.ds(at, rows // 2, stride=groups), :] = value[:, g * 128:(g + 1) * 128]
+            acc[part, span] = value * (1.0 / valid_rows)
             if n == COL_TILES - 1:
                 start([stores[1 if lag else 0][h]])
         else:
@@ -369,13 +364,12 @@
 
     stores = []
     if last:
-        for m, (a, b) in enumerate(zip((instant_end, lagged_end), acc_out)):
-            size = a.shape[0] // 2
+        for m, (a, b) in enumerate(zip((instant, lagged), acc_out)):
             stores.append([
                 pltpu.make_async_copy(
-                    a.at[pl.ds(n * size, size)], b.at[pl.ds(pl.multiple_of(place * size, 8), size)], out_sem.at[m, n]
+                    a.at[row_part(h)], b.at[pl.ds(pl.multiple_of(place * (rows // 2), 8), rows // 2), 0], out_sem.at[m, h]
                 )
-                for n, place in enumerate((col, 1 - col))
+                for h, place in enumerate((col, 1 - col))
             ])
 
     if first:
@@ -415,7 +409,7 @@
     if first:
         slabs = slabs[at + ready:]
     pieces = [p for s in slabs for p in s]
-    end_shape = (rows * cols // 128, 128)
+    end_shape = (rows, 1, cols)
     outs = [pltpu.VMEM((rows, cols), jnp.float32)] * 2
     dma = pltpu.SemaphoreType.DMA
     scratch = [
@@ -442,7 +436,6 @@
         scratch.append(dma)
     else:
         outs, out_specs = [pltpu.HBM(end_shape, jnp.float32)] * 2 + outs, [hbm_spec()] * 2 + [vmem_spec()] * 2
-        scratch += [pltpu.VMEM(end_shape, jnp.float32)] * 2
         scratch += [pltpu.VMEM((len(slabs), LAG, units), jnp.bfloat16)] * 2
         scratch += [pltpu.VMEM((units, len(slabs) * LAG), jnp.bfloat16), dma((len(slabs), 2)), dma((2, 2))]
         args += [in_vmem(x) for x in (*panels, *carry[2:], *carry[:2])]
@@ -509,11 +502,12 @@
     slabs += [(over, swapped_over)]
     carry = moments(slabs, 4, numbers, opened, (panel, swapped, row_proj, row_off), None, *sizes)
 
-    *carry, y_far, over_back, over_far = lax.optimization_barrier((*carry, y_far, over_back, over_far))
-    slabs += [(y_far, swap(y_far)), (over_out, swap(over_back)), (over_back, swap(over_out)), (over_far, swap(over_far))]
+    *carry, y_far, over_back = lax.optimization_barrier((*carry, y_far, over_back))
+    swapped_far, swapped_over_back = swap(y_far), swap(over_back)
+    swapped_far, swapped_over_back, over_far = lax.optimization_barrier((swapped_far, swapped_over_back, over_far))
+    slabs += [(y_far, swapped_far), (over_out, swapped_over_back), (over_back, swap(over_out)), (over_far, swap(over_far))]
     instant, lagged, *_ = moments(slabs, 5, numbers, None, (row_proj, row_off), carry, *sizes)
-    shape = (2 * cols, 1, cols)
-    return instant.reshape(shape), lagged.reshape(shape)
+    return instant, lagged
 
 
 def solution(mesh):

time: 101 us -> 98.8 us (0.978)
  starting transfers between devices: 26.1 us -> 24 us
  waiting for transfers between devices: 22.1 us -> 23.4 us
    ppermute x19, starting transfers between devices: 26.1 us -> 24 us  [move(): return lax.ppermute(block, AXES, route(target))]
    ppermute x19, waiting for transfers between devices: 22.1 us -> 23.4 us  [move(): return lax.ppermute(block, AXES, route(target))]
  transfers between devices with their start and end apart: 19 -> 19, of which waited for: 6 -> 7; matrix products, arithmetic and copies ran while one was open for 0% -> 0% of each run, Pallas kernels for 21% -> 20%
where the time goes in v1:
time: 98.8 us; the launch traced here: 97.9 us
  Pallas kernels  49.3 us (50%)
  starting transfers between devices  24 us (24%)
  waiting for transfers between devices  23.4 us (24%)
  between operations  1.11 us (1%)
    pallas_call x2, Pallas kernels, moments(): pl.pallas_call(functools.partial(moments_kernel, count, ready, at, last,...  38.7 us
    ppermute x19, starting transfers between devices, move(): return lax.ppermute(block, AXES, route(target))  24 us
    ppermute x19, waiting for transfers between devices, move(): return lax.ppermute(block, AXES, route(target))  23.4 us
    pallas_call x1, Pallas kernels, opening(): pl.pallas_call(functools.partial(opening_kernel, count, valid_rows), in_s...  7.78 us
    pallas_call x1, Pallas kernels, prepare(): pl.pallas_call(functools.partial(prepare_kernel, at), in_specs=[smem_spec...  2.14 us
  transfers between devices with their start and end apart: 19, of which 7 were waited for; matrix products, arithmetic and copies ran while one was open for 0% of the time, Pallas kernels for 20%

profile of v1, /device:TPU:1, one launch (start us, length us, event | category | flops | bytes accessed | tf_op | source)
XLA Modules:
  0.0 97.9 jit_solution(15205774469609774984)
XLA Ops:
  0.8 0.1 stack.51.numbers.ids.refs_0_
  0.9 2.1 %shard_map.50 = (bf16[1040,512]{1,0:T(8,128)(2,1)S(1)}, bf16[528,1024]{1,0:T(8,128)(2,1)S(1)}, bf16[384,1024]{1,0:T(8,128)(2,1)S(1)}) custom-call(s32[12]{0:T(128)S(1)} %stack.51.numbers.ids.refs_0_, bf16[1024,512]{1,0:T(8,128)(2,1)} %projection.1, f32[1,512]{1,0:T(1,128)} %bitcast.13, bf16[768,1024]{1,0:T(8,128)(2,1)} %refs_1_.1), custom_call_target="tpu_custom_call" | custom-call | tf_op jit(solution)/shard_map/pallas_call | solution.py:138
  3.0 0.7 collective-permute-start.2
  3.7 3.6 %collective-permute-start.1 = (bf16[384,1024]{1,0:T(8,128)(2,1)S(1)}, bf16[384,1024]{1,0:T(8,128)(2,1)S(1)}, u32[]{:S(2)}, u32[]{:S(2)}) collective-permute-start(bf16[384,1024]{1,0:T(8,128)(2,1)S(1)} %get-tuple-element.51), channel_id=1, source_target_pairs={{0,16},{1,17},{2,50},{3,51},{4,20},{5,21},{6,54},{7,55},{8,24},{9,... | collective-permute-start | bytes 2359304 | tf_op jit(solution)/shard_map/ppermute | solution.py:32
  7.4 3.0 %collective-permute-start = (bf16[384,1024]{1,0:T(8,128)(2,1)S(1)}, bf16[384,1024]{1,0:T(8,128)(2,1)S(1)}, u32[]{:S(2)}, u32[]{:S(2)}) collective-permute-start(bf16[384,1024]{1,0:T(8,128)(2,1)S(1)} %get-tuple-element.51), channel_id=1, source_target_pairs={{0,65},{1,64},{2,67},{3,66},{4,69},{5,68},{6,71},{7,70},{8,73},{9,... | collective-permute-start | bytes 2359304 | tf_op jit(solution)/shard_map/ppermute | solution.py:32
  10.4 0.0 copy-start
  10.4 0.0 collective-permute-start.5
  10.4 0.8 collective-permute-start.3
  11.3 0.0 collective-permute-done.2.refs_1_
  11.3 0.7 collective-permute-start.4
  12.0 6.5 %collective-permute-done.1.refs_1_.refs_2_ = bf16[384,1024]{1,0:T(8,128)(2,1)S(1)} collective-permute-done((bf16[384,1024]{1,0:T(8,128)(2,1)S(1)}, bf16[384,1024]{1,0:T(8,128)(2,1)S(1)}, u32[]{:S(2)}, u32[]{:S(2)}) %collective-permute-start.1) | collective-permute-done | bytes 786464 | tf_op jit(solution)/shard_map/ppermute | solution.py:32
  18.5 3.5 %collective-permute-start.6 = (bf16[384,1024]{1,0:T(8,128)(2,1)S(1)}, bf16[384,1024]{1,0:T(8,128)(2,1)S(1)}, u32[]{:S(2)}, u32[]{:S(2)}) collective-permute-start(bf16[384,1024]{1,0:T(8,128)(2,1)S(1)} %get-tuple-element.51), channel_id=1, source_target_pairs={{0,48},{1,49},{2,18},{3,19},{4,52},{5,53},{6,22},{7,23},{8,56},{9,... | collective-permute-start | bytes 2359304 | tf_op jit(solution)/shard_map/ppermute | solution.py:32
  22.0 5.2 %collective-permute-done.refs_1_.refs_6_ = bf16[384,1024]{1,0:T(8,128)(2,1)S(1)} collective-permute-done((bf16[384,1024]{1,0:T(8,128)(2,1)S(1)}, bf16[384,1024]{1,0:T(8,128)(2,1)S(1)}, u32[]{:S(2)}, u32[]{:S(2)}) %collective-permute-start) | collective-permute-done | bytes 786464 | tf_op jit(solution)/shard_map/ppermute | solution.py:32
  27.2 1.7 %collective-permute-start.7 = (bf16[384,1024]{1,0:T(8,128)(2,1)S(1)}, bf16[384,1024]{1,0:T(8,128)(2,1)S(1)}, u32[]{:S(2)}, u32[]{:S(2)}) collective-permute-start(bf16[384,1024]{1,0:T(8,128)(2,1)S(1)} %collective-permute-done.1.refs_1_.refs_2_), channel_id=1, source_target_pairs={{0,2},{1,3},{2,0},{3,1},{4,6},{5,7},{6,4},{7,5},{8,10},{9,11},{10,... | collective-permute-start | bytes 2359304 | tf_op jit(solution)/shard_map/ppermute | solution.py:32
  28.9 0.0 collective-permute-done.3.refs_3_
  28.9 6.8 %collective-permute-done.5.refs_6_ = bf16[528,1024]{1,0:T(8,128)(2,1)S(1)} collective-permute-done((bf16[528,1024]{1,0:T(8,128)(2,1)S(1)}, bf16[528,1024]{1,0:T(8,128)(2,1)S(1)}, u32[]{:S(2)}, u32[]{:S(2)}) %collective-permute-start.5) | collective-permute-done | bytes 1081376 | tf_op jit(solution)/shard_map/ppermute | solution.py:32
  35.7 0.0 collective-permute-done.6.refs_3_.refs_4_
  35.7 0.0 collective-permute-done.7.refs_4_.refs_5_
  35.7 0.0 collective-permute-done.4.refs_2_
  35.7 0.5 collective-permute-start.8
  36.2 0.7 shard_map.52.refs_5_
  36.9 0.2 collective-permute-start.10
  37.1 0.7 collective-permute-start.11
  37.7 0.0 collective-permute-start.9
  37.7 2.7 %collective-permute-start.12 = (bf16[384,1024]{1,0:T(8,128)(2,1)S(1)}, bf16[384,1024]{1,0:T(8,128)(2,1)S(1)}, u32[]{:S(2)}, u32[]{:S(2)}) collective-permute-start(bf16[384,1024]{1,0:T(8,128)(2,1)S(1)} %collective-permute-done.1.refs_1_.refs_2_), channel_id=1, source_target_pairs={{0,16},{1,17},{2,50},{3,51},{4,20},{5,21},{6,54},{7,55},{8,24},{9,... | collective-permute-start | bytes 2359304 | tf_op jit(solution)/shard_map/ppermute | solution.py:32
  40.4 0.0 collective-permute-done.8.refs_2_.refs_3_
  40.4 4.9 %collective-permute-start.13 = (bf16[384,1024]{1,0:T(8,128)(2,1)S(1)}, bf16[384,1024]{1,0:T(8,128)(2,1)S(1)}, u32[]{:S(2)}, u32[]{:S(2)}) collective-permute-start(bf16[384,1024]{1,0:T(8,128)(2,1)S(1)} %collective-permute-done.6.refs_3_.refs_4_), channel_id=1, source_target_pairs={{0,65},{1,64},{2,67},{3,66},{4,69},{5,68},{6,71},{7,70},{8,73},{9,... | collective-permute-start | bytes 2359304 | tf_op jit(solution)/shard_map/ppermute | solution.py:32
  45.3 0.0 copy-done
  45.3 7.8 %shard_map.51 = (bf16[1024,1024]{1,0:T(8,128)(2,1)S(1)}, f32[1024,128]{1,0:T(8,128)S(1)}, bf16[3,768,1024]{2,1,0:T(8,128)(2,1)S(1)}, bf16[3,1024,768]{2,1,0:T(8,128)(2,1)S(1)}) custom-call(s32[12]{0:T(128)S(1)} %stack.51.numbers.ids.refs_0_, bf16[768,1024]{1,0:T(8,128)(2,1)} %refs_1_.1, bf16[384,1024]{1,0:T(8,128)(2,1)S(1)} %collective-permute-done.1.refs_1_.refs_2_, ...), custom_call_target="tpu_custom_call" | custom-call | flops 4831838208 | bytes 4718592 | tf_op jit(solution)/shard_map/pallas_call | solution.py:230
  53.1 0.0 collective-permute-done.11.refs_10_
  53.1 0.1 collective-permute-start.16
  53.2 0.0 collective-permute-done.9.refs_2_.refs_7_
  53.2 0.0 collective-permute-done.10.refs_6_
  53.2 11.3 %shard_map.53 = (f32[1024,512]{1,0:T(8,128)S(1)}, f32[1024,512]{1,0:T(8,128)S(1)}, bf16[1040,512]{1,0:T(8,128)(2,1)S(1)}, bf16[1024,768]{1,0:T(8,128)(2,1)S(1)}, bf16[832,512]{1,0:T(8,128)(2,1)S(1)}) custom-call(s32[12]{0:T(128)S(1)} %stack.51.numbers.ids.refs_0_, bf16[384,1024]{1,0:T(8,128)(2,1)S(1)} %collective-permute-done.refs_1_.refs_6_, ...), custom_call_target="tpu_custom_call" | custom-call | flops 16106127360 | bytes 6291456 | tf_op jit(solution)/shard_map/pallas_call | solution.py:444
  64.5 0.0 collective-permute-done.12.refs_8_
  64.5 0.0 collective-permute-done.13.refs_12_
  64.5 0.1 collective-permute-start.14
  64.6 0.5 collective-permute-start.15
  65.1 0.1 collective-permute-start.17
  65.2 0.0 collective-permute-done.16.refs_14_
  65.2 1.7 %collective-permute-done.14.refs_9_ = bf16[384,1024]{1,0:T(8,128)(2,1)S(1)} collective-permute-done((bf16[384,1024]{1,0:T(8,128)(2,1)S(1)}, bf16[384,1024]{1,0:T(8,128)(2,1)S(1)}, u32[]{:S(2)}, u32[]{:S(2)}) %collective-permute-start.14) | collective-permute-done | bytes 786464 | tf_op jit(solution)/shard_map/ppermute | solution.py:32
  66.9 1.1 %collective-permute-done.15.refs_11_ = bf16[384,1024]{1,0:T(8,128)(2,1)S(1)} collective-permute-done((bf16[384,1024]{1,0:T(8,128)(2,1)S(1)}, bf16[384,1024]{1,0:T(8,128)(2,1)S(1)}, u32[]{:S(2)}, u32[]{:S(2)}) %collective-permute-start.15) | collective-permute-done | bytes 786464 | tf_op jit(solution)/shard_map/ppermute | solution.py:32
  68.0 0.1 collective-permute-start.18
  68.2 1.0 %collective-permute-done.17.refs_13_ = bf16[384,1024]{1,0:T(8,128)(2,1)S(1)} collective-permute-done((bf16[384,1024]{1,0:T(8,128)(2,1)S(1)}, bf16[384,1024]{1,0:T(8,128)(2,1)S(1)}, u32[]{:S(2)}, u32[]{:S(2)}) %collective-permute-start.17) | collective-permute-done | bytes 786464 | tf_op jit(solution)/shard_map/ppermute | solution.py:32
  69.2 1.2 %collective-permute-done.18.refs_15_ = bf16[384,1024]{1,0:T(8,128)(2,1)S(1)} collective-permute-done((bf16[384,1024]{1,0:T(8,128)(2,1)S(1)}, bf16[384,1024]{1,0:T(8,128)(2,1)S(1)}, u32[]{:S(2)}, u32[]{:S(2)}) %collective-permute-start.18) | collective-permute-done | bytes 786464 | tf_op jit(solution)/shard_map/ppermute | solution.py:32
  70.3 27.4 %shard_map.54 = (f32[1024,1,512]{2,1,0:T(1,128)}, f32[1024,1,512]{2,1,0:T(1,128)}, f32[1024,512]{1,0:T(8,128)S(1)}, f32[1024,512]{1,0:T(8,128)S(1)}) custom-call(s32[12]{0:T(128)S(1)} %stack.51.numbers.ids.refs_0_, bf16[768,1024]{1,0:T(8,128)(2,1)} %refs_1_.1, ...), custom_call_target="tpu_custom_call", output_to_operand_aliasing={{2}: (21, {}), {3}: (22, {})} | custom-call | flops 20132659200 | bytes 7864320 | tf_op jit(solution)/shard_map/pallas_call | solution.py:444
Async XLA Ops:
  3.0 8.3 %collective-permute-start.2 = (bf16[1040,512]{1,0:T(8,128)(2,1)S(1)}, bf16[1040,512]{1,0:T(8,128)(2,1)S(1)}, u32[]{:S(2)}, u32[]{:S(2)}) collective-permute-start(bf16[1040,512]{1,0:T(8,128)(2,1)S(1)} %get-tuple-element.49.refs_0_), channel_id=1, source_target_pairs={{0,4},{1,5},{18,22},{19,23},{36,40},{37,41},{54,58},{55,59},{72,76... | collective-permute-start | bytes 3194888 | tf_op jit(solution)/shard_map/ppermute | solution.py:32
  3.7 14.8 %collective-permute-start.1 = (bf16[384,1024]{1,0:T(8,128)(2,1)S(1)}, bf16[384,1024]{1,0:T(8,128)(2,1)S(1)}, u32[]{:S(2)}, u32[]{:S(2)}) collective-permute-start(bf16[384,1024]{1,0:T(8,128)(2,1)S(1)} %get-tuple-element.51), channel_id=1, source_target_pairs={{0,16},{1,17},{2,50},{3,51},{4,20},{5,21},{6,54},{7,55},{8,24},{9,... | collective-permute-start | bytes 2359304 | tf_op jit(solution)/shard_map/ppermute | solution.py:32
  7.4 19.8 %collective-permute-start = (bf16[384,1024]{1,0:T(8,128)(2,1)S(1)}, bf16[384,1024]{1,0:T(8,128)(2,1)S(1)}, u32[]{:S(2)}, u32[]{:S(2)}) collective-permute-start(bf16[384,1024]{1,0:T(8,128)(2,1)S(1)} %get-tuple-element.51), channel_id=1, source_target_pairs={{0,65},{1,64},{2,67},{3,66},{4,69},{5,68},{6,71},{7,70},{8,73},{9,... | collective-permute-start | bytes 2359304 | tf_op jit(solution)/shard_map/ppermute | solution.py:32
  10.4 34.9 %copy-start = (f32[512]{0:T(512)S(1)}, f32[512]{0:T(512)}, u32[]{:S(2)}) copy-start(f32[512]{0:T(512)} %param.5) | copy-start | bytes 6148
  10.4 25.3 %collective-permute-start.5 = (bf16[528,1024]{1,0:T(8,128)(2,1)S(1)}, bf16[528,1024]{1,0:T(8,128)(2,1)S(1)}, u32[]{:S(2)}, u32[]{:S(2)}) collective-permute-start(bf16[528,1024]{1,0:T(8,128)(2,1)S(1)} %get-tuple-element.50.refs_5_), channel_id=1, source_target_pairs={{0,1},{1,0},{2,3},{3,2},{4,5},{5,4},{6,7},{7,6},{8,9},{9,8},{10,11... | collective-permute-start | bytes 3244040 | tf_op jit(solution)/shard_map/ppermute | solution.py:32
  10.4 18.5 %collective-permute-start.3 = (bf16[1040,512]{1,0:T(8,128)(2,1)S(1)}, bf16[1040,512]{1,0:T(8,128)(2,1)S(1)}, u32[]{:S(2)}, u32[]{:S(2)}) collective-permute-start(bf16[1040,512]{1,0:T(8,128)(2,1)S(1)} %get-tuple-element.49.refs_0_), channel_id=1, source_target_pairs={{0,12},{1,13},{18,30},{19,31},{36,32},{37,33},{54,50},{55,51},{72,... | collective-permute-start | bytes 3194888 | tf_op jit(solution)/shard_map/ppermute | solution.py:32
  11.3 24.4 %collective-permute-start.4 = (bf16[1040,512]{1,0:T(8,128)(2,1)S(1)}, bf16[1040,512]{1,0:T(8,128)(2,1)S(1)}, u32[]{:S(2)}, u32[]{:S(2)}) collective-permute-start(bf16[1040,512]{1,0:T(8,128)(2,1)S(1)} %get-tuple-element.49.refs_0_), channel_id=1, source_target_pairs={{0,8},{1,9},{18,26},{19,27},{36,44},{37,45},{54,62},{55,63},{72,64... | collective-permute-start | bytes 3194888 | tf_op jit(solution)/shard_map/ppermute | solution.py:32
  18.5 17.2 %collective-permute-start.6 = (bf16[384,1024]{1,0:T(8,128)(2,1)S(1)}, bf16[384,1024]{1,0:T(8,128)(2,1)S(1)}, u32[]{:S(2)}, u32[]{:S(2)}) collective-permute-start(bf16[384,1024]{1,0:T(8,128)(2,1)S(1)} %get-tuple-element.51), channel_id=1, source_target_pairs={{0,48},{1,49},{2,18},{3,19},{4,52},{5,53},{6,22},{7,23},{8,56},{9,... | collective-permute-start | bytes 2359304 | tf_op jit(solution)/shard_map/ppermute | solution.py:32
  27.2 8.5 %collective-permute-start.7 = (bf16[384,1024]{1,0:T(8,128)(2,1)S(1)}, bf16[384,1024]{1,0:T(8,128)(2,1)S(1)}, u32[]{:S(2)}, u32[]{:S(2)}) collective-permute-start(bf16[384,1024]{1,0:T(8,128)(2,1)S(1)} %collective-permute-done.1.refs_1_.refs_2_), channel_id=1, source_target_pairs={{0,2},{1,3},{2,0},{3,1},{4,6},{5,7},{6,4},{7,5},{8,10},{9,11},{10,... | collective-permute-start | bytes 2359304 | tf_op jit(solution)/shard_map/ppermute | solution.py:32
  35.7 4.7 %collective-permute-start.8 = (bf16[384,1024]{1,0:T(8,128)(2,1)S(1)}, bf16[384,1024]{1,0:T(8,128)(2,1)S(1)}, u32[]{:S(2)}, u32[]{:S(2)}) collective-permute-start(bf16[384,1024]{1,0:T(8,128)(2,1)S(1)} %collective-permute-done.6.refs_3_.refs_4_), channel_id=1, source_target_pairs={{0,2},{1,3},{2,0},{3,1},{4,6},{5,7},{6,4},{7,5},{8,10},{9,11},{10,... | collective-permute-start | bytes 2359304 | tf_op jit(solution)/shard_map/ppermute | solution.py:32
  36.9 16.4 %collective-permute-start.10 = (bf16[1040,512]{1,0:T(8,128)(2,1)S(1)}, bf16[1040,512]{1,0:T(8,128)(2,1)S(1)}, u32[]{:S(2)}, u32[]{:S(2)}) collective-permute-start(bf16[1040,512]{1,0:T(8,128)(2,1)S(1)} %shard_map.52.refs_5_), channel_id=1, source_target_pairs={{0,2},{1,3},{2,0},{3,1},{4,6},{5,7},{6,4},{7,5},{8,10},{9,11},{10,... | collective-permute-start | bytes 3194888 | tf_op jit(solution)/shard_map/ppermute | solution.py:32
  37.1 16.1 %collective-permute-start.11 = (bf16[384,1024]{1,0:T(8,128)(2,1)S(1)}, bf16[384,1024]{1,0:T(8,128)(2,1)S(1)}, u32[]{:S(2)}, u32[]{:S(2)}) collective-permute-start(bf16[384,1024]{1,0:T(8,128)(2,1)S(1)} %collective-permute-done.refs_1_.refs_6_), channel_id=1, source_target_pairs={{0,16},{1,17},{2,50},{3,51},{4,20},{5,21},{6,54},{7,55},{8,24},{9,... | collective-permute-start | bytes 2359304 | tf_op jit(solution)/shard_map/ppermute | solution.py:32
  37.7 15.5 %collective-permute-start.9 = (bf16[384,1024]{1,0:T(8,128)(2,1)S(1)}, bf16[384,1024]{1,0:T(8,128)(2,1)S(1)}, u32[]{:S(2)}, u32[]{:S(2)}) collective-permute-start(bf16[384,1024]{1,0:T(8,128)(2,1)S(1)} %collective-permute-done.refs_1_.refs_6_), channel_id=1, source_target_pairs={{0,2},{1,3},{2,0},{3,1},{4,6},{5,7},{6,4},{7,5},{8,10},{9,11},{10,... | collective-permute-start | bytes 2359304 | tf_op jit(solution)/shard_map/ppermute | solution.py:32
  37.7 26.8 %collective-permute-start.12 = (bf16[384,1024]{1,0:T(8,128)(2,1)S(1)}, bf16[384,1024]{1,0:T(8,128)(2,1)S(1)}, u32[]{:S(2)}, u32[]{:S(2)}) collective-permute-start(bf16[384,1024]{1,0:T(8,128)(2,1)S(1)} %collective-permute-done.1.refs_1_.refs_2_), channel_id=1, source_target_pairs={{0,16},{1,17},{2,50},{3,51},{4,20},{5,21},{6,54},{7,55},{8,24},{9,... | collective-permute-start | bytes 2359304 | tf_op jit(solution)/shard_map/ppermute | solution.py:32
  40.4 24.1 %collective-permute-start.13 = (bf16[384,1024]{1,0:T(8,128)(2,1)S(1)}, bf16[384,1024]{1,0:T(8,128)(2,1)S(1)}, u32[]{:S(2)}, u32[]{:S(2)}) collective-permute-start(bf16[384,1024]{1,0:T(8,128)(2,1)S(1)} %collective-permute-done.6.refs_3_.refs_4_), channel_id=1, source_target_pairs={{0,65},{1,64},{2,67},{3,66},{4,69},{5,68},{6,71},{7,70},{8,73},{9,... | collective-permute-start | bytes 2359304 | tf_op jit(solution)/shard_map/ppermute | solution.py:32
  53.1 12.1 %collective-permute-start.16 = (bf16[384,1024]{1,0:T(8,128)(2,1)S(1)}, bf16[384,1024]{1,0:T(8,128)(2,1)S(1)}, u32[]{:S(2)}, u32[]{:S(2)}) collective-permute-start(bf16[384,1024]{1,0:T(8,128)(2,1)S(1)} %collective-permute-done.11.refs_10_), channel_id=1, source_target_pairs={{0,16},{1,17},{2,50},{3,51},{4,20},{5,21},{6,54},{7,55},{8,24},{9,... | collective-permute-start | bytes 2359304 | tf_op jit(solution)/shard_map/ppermute | solution.py:32
  64.5 2.4 %collective-permute-start.14 = (bf16[384,1024]{1,0:T(8,128)(2,1)S(1)}, bf16[384,1024]{1,0:T(8,128)(2,1)S(1)}, u32[]{:S(2)}, u32[]{:S(2)}) collective-permute-start(bf16[384,1024]{1,0:T(8,128)(2,1)S(1)} %collective-permute-done.12.refs_8_), channel_id=1, source_target_pairs={{0,2},{1,3},{2,0},{3,1},{4,6},{5,7},{6,4},{7,5},{8,10},{9,11},{10,... | collective-permute-start | bytes 2359304 | tf_op jit(solution)/shard_map/ppermute | solution.py:32
  64.6 3.4 %collective-permute-start.15 = (bf16[384,1024]{1,0:T(8,128)(2,1)S(1)}, bf16[384,1024]{1,0:T(8,128)(2,1)S(1)}, u32[]{:S(2)}, u32[]{:S(2)}) collective-permute-start(bf16[384,1024]{1,0:T(8,128)(2,1)S(1)} %collective-permute-done.13.refs_12_), channel_id=1, source_target_pairs={{0,2},{1,3},{2,0},{3,1},{4,6},{5,7},{6,4},{7,5},{8,10},{9,11},{10,... | collective-permute-start | bytes 2359304 | tf_op jit(solution)/shard_map/ppermute | solution.py:32
  65.1 4.0 %collective-permute-start.17 = (bf16[384,1024]{1,0:T(8,128)(2,1)S(1)}, bf16[384,1024]{1,0:T(8,128)(2,1)S(1)}, u32[]{:S(2)}, u32[]{:S(2)}) collective-permute-start(bf16[384,1024]{1,0:T(8,128)(2,1)S(1)} %collective-permute-done.11.refs_10_), channel_id=1, source_target_pairs={{0,2},{1,3},{2,0},{3,1},{4,6},{5,7},{6,4},{7,5},{8,10},{9,11},{10,... | collective-permute-start | bytes 2359304 | tf_op jit(solution)/shard_map/ppermute | solution.py:32
  68.0 2.3 %collective-permute-start.18 = (bf16[384,1024]{1,0:T(8,128)(2,1)S(1)}, bf16[384,1024]{1,0:T(8,128)(2,1)S(1)}, u32[]{:S(2)}, u32[]{:S(2)}) collective-permute-start(bf16[384,1024]{1,0:T(8,128)(2,1)S(1)} %collective-permute-done.16.refs_14_), channel_id=1, source_target_pairs={{0,2},{1,3},{2,0},{3,1},{4,6},{5,7},{6,4},{7,5},{8,10},{9,11},{10,... | collective-permute-start | bytes 2359304 | tf_op jit(solution)/shard_map/ppermute | solution.py:32

commit v2 on v1

--- a/solution.py
+++ b/solution.py
@@ -330,8 +330,8 @@
             heads[...].reshape(slabs * LAG, units), col_proj[:units, span], col_off(span)
         )
 
-    def moment_tile(k, lag, n, h):
-        span, part = slice(n * col_tile, (n + 1) * col_tile), row_part(h)
+    def moment_tile(k, lag, n, h, parts=2):
+        span, part = slice(n * col_tile, (n + 1) * col_tile), slice(h * rows // parts, (h + 1) * rows // parts)
         acc = lagged if lag else instant
         buf_r, buf_c = row_bufs(k), col_bufs(k)
         if k < count:
@@ -365,11 +365,13 @@
     stores = []
     if last:
         for m, (a, b) in enumerate(zip((instant, lagged), acc_out)):
+            size = rows // 2 // (m + 1)
             stores.append([
                 pltpu.make_async_copy(
-                    a.at[row_part(h)], b.at[pl.ds(pl.multiple_of(place * (rows // 2), 8), rows // 2), 0], out_sem.at[m, h]
+                    a.at[pl.ds(h * size, size)],
+                    b.at[pl.ds(pl.multiple_of(place * (rows // 2) + h % (m + 1) * size, 8), size), 0], out_sem.at[m, h]
                 )
-                for h, place in enumerate((col, 1 - col))
+                for h, place in enumerate([col] * (m + 1) + [1 - col] * (m + 1))
             ])
 
     if first:
@@ -384,8 +386,10 @@
             steps.pop(0)()
         if k + 1 < count:
             wait(loads[k + 1])
-            if k == 0:
-                start([copy for load in loads[ready + 1:] for copy in load] + edge_loads)
+            if k + 2 < count:
+                start(loads[k + 2] if last else [])
+            elif last:
+                start(edge_loads)
             ahead = feature_steps(k + 1)
         elif last:
             wait(edge_loads)
@@ -393,9 +397,9 @@
             ahead += [functools.partial(edge_rows, h) for h in range(2)]
         interleave(steps, ahead)
     if last:
-        for h in range(2):
+        for h in range(4):
             for n in range(COL_TILES):
-                moment_tile(count, LAG, n, h)
+                moment_tile(count, LAG, n, h, 4)
         wait(stores[0] + stores[1])
 
 
@@ -437,7 +441,7 @@
     else:
         outs, out_specs = [pltpu.HBM(end_shape, jnp.float32)] * 2 + outs, [hbm_spec()] * 2 + [vmem_spec()] * 2
         scratch += [pltpu.VMEM((len(slabs), LAG, units), jnp.bfloat16)] * 2
-        scratch += [pltpu.VMEM((units, len(slabs) * LAG), jnp.bfloat16), dma((len(slabs), 2)), dma((2, 2))]
+        scratch += [pltpu.VMEM((units, len(slabs) * LAG), jnp.bfloat16), dma((len(slabs), 2)), dma((2, 4))]
         args += [in_vmem(x) for x in (*panels, *carry[2:], *carry[:2])]
         specs += [vmem_spec()] * 7
         aliases = {len(args) - 2 + n: 2 + n for n in range(2)}
@@ -478,8 +482,8 @@
     sizes = (slab_rows, valid_rows)
 
     columns, turned, mine = prepare(after, numbers, projection, line, states)
+    partner, over, y_out = move(turned, inner), move(mine, crossing), move(mine, out_y)
     ahead, behind = move(columns, along_z(1)), move(columns, along_z(-1))
-    over, partner, y_out = move(mine, crossing), move(turned, inner), move(mine, out_y)
     ahead, columns = lax.optimization_barrier((ahead, columns))
     beyond = move(columns, along_z(2))
     y_out, mine = lax.optimization_barrier((y_out, mine))

time: 98.8 us -> 98.9 us (level)
  no operation moved by 1% of the time
where the time goes in v2:
time: 98.9 us; the launch traced here: 98 us
  Pallas kernels  49.3 us (50%)
  starting transfers between devices  24 us (24%)
  waiting for transfers between devices  23.4 us (24%)
  between operations  1.11 us (1%)
    pallas_call x2, Pallas kernels, moments(): pl.pallas_call(functools.partial(moments_kernel, count, ready, at, last,...  38.7 us
    ppermute x19, starting transfers between devices, move(): return lax.ppermute(block, AXES, route(target))  24 us
    ppermute x19, waiting for transfers between devices, move(): return lax.ppermute(block, AXES, route(target))  23.4 us
    pallas_call x1, Pallas kernels, opening(): pl.pallas_call(functools.partial(opening_kernel, count, valid_rows), in_s...  7.78 us
    pallas_call x1, Pallas kernels, prepare(): pl.pallas_call(functools.partial(prepare_kernel, at), in_specs=[smem_spec...  2.14 us
  transfers between devices with their start and end apart: 19, of which 7 were waited for; matrix products, arithmetic and copies ran while one was open for 0% of the time, Pallas kernels for 20%

profile of v2, /device:TPU:1, one launch (start us, length us, event | category | flops | bytes accessed | tf_op | source)
XLA Modules:
  0.0 98.0 jit_solution(17784699275010254218)
XLA Ops:
  0.8 0.1 stack.51.numbers.ids.refs_0_
  0.9 2.1 %shard_map.50 = (bf16[1040,512]{1,0:T(8,128)(2,1)S(1)}, bf16[528,1024]{1,0:T(8,128)(2,1)S(1)}, bf16[384,1024]{1,0:T(8,128)(2,1)S(1)}) custom-call(s32[12]{0:T(128)S(1)} %stack.51.numbers.ids.refs_0_, bf16[1024,512]{1,0:T(8,128)(2,1)} %projection.1, f32[1,512]{1,0:T(1,128)} %bitcast.13, bf16[768,1024]{1,0:T(8,128)(2,1)} %refs_1_.1), custom_call_target="tpu_custom_call" | custom-call | tf_op jit(solution)/shard_map/pallas_call | solution.py:138
  3.0 0.7 collective-permute-start.2
  3.7 3.6 %collective-permute-start.1 = (bf16[384,1024]{1,0:T(8,128)(2,1)S(1)}, bf16[384,1024]{1,0:T(8,128)(2,1)S(1)}, u32[]{:S(2)}, u32[]{:S(2)}) collective-permute-start(bf16[384,1024]{1,0:T(8,128)(2,1)S(1)} %get-tuple-element.51), channel_id=1, source_target_pairs={{0,16},{1,17},{2,50},{3,51},{4,20},{5,21},{6,54},{7,55},{8,24},{9,... | collective-permute-start | bytes 2359304 | tf_op jit(solution)/shard_map/ppermute | solution.py:32
  7.4 3.0 %collective-permute-start = (bf16[384,1024]{1,0:T(8,128)(2,1)S(1)}, bf16[384,1024]{1,0:T(8,128)(2,1)S(1)}, u32[]{:S(2)}, u32[]{:S(2)}) collective-permute-start(bf16[384,1024]{1,0:T(8,128)(2,1)S(1)} %get-tuple-element.51), channel_id=1, source_target_pairs={{0,65},{1,64},{2,67},{3,66},{4,69},{5,68},{6,71},{7,70},{8,73},{9,... | collective-permute-start | bytes 2359304 | tf_op jit(solution)/shard_map/ppermute | solution.py:32
  10.4 0.0 copy-start
  10.4 0.0 collective-permute-start.5
  10.4 0.8 collective-permute-start.3
  11.3 0.0 collective-permute-done.2.refs_1_
  11.3 0.7 collective-permute-start.4
  12.0 6.5 %collective-permute-done.1.refs_1_.refs_2_ = bf16[384,1024]{1,0:T(8,128)(2,1)S(1)} collective-permute-done((bf16[384,1024]{1,0:T(8,128)(2,1)S(1)}, bf16[384,1024]{1,0:T(8,128)(2,1)S(1)}, u32[]{:S(2)}, u32[]{:S(2)}) %collective-permute-start.1) | collective-permute-done | bytes 786464 | tf_op jit(solution)/shard_map/ppermute | solution.py:32
  18.5 3.5 %collective-permute-start.6 = (bf16[384,1024]{1,0:T(8,128)(2,1)S(1)}, bf16[384,1024]{1,0:T(8,128)(2,1)S(1)}, u32[]{:S(2)}, u32[]{:S(2)}) collective-permute-start(bf16[384,1024]{1,0:T(8,128)(2,1)S(1)} %get-tuple-element.51), channel_id=1, source_target_pairs={{0,48},{1,49},{2,18},{3,19},{4,52},{5,53},{6,22},{7,23},{8,56},{9,... | collective-permute-start | bytes 2359304 | tf_op jit(solution)/shard_map/ppermute | solution.py:32
  22.0 5.2 %collective-permute-done.refs_1_.refs_6_ = bf16[384,1024]{1,0:T(8,128)(2,1)S(1)} collective-permute-done((bf16[384,1024]{1,0:T(8,128)(2,1)S(1)}, bf16[384,1024]{1,0:T(8,128)(2,1)S(1)}, u32[]{:S(2)}, u32[]{:S(2)}) %collective-permute-start) | collective-permute-done | bytes 786464 | tf_op jit(solution)/shard_map/ppermute | solution.py:32
  27.2 1.7 %collective-permute-start.7 = (bf16[384,1024]{1,0:T(8,128)(2,1)S(1)}, bf16[384,1024]{1,0:T(8,128)(2,1)S(1)}, u32[]{:S(2)}, u32[]{:S(2)}) collective-permute-start(bf16[384,1024]{1,0:T(8,128)(2,1)S(1)} %collective-permute-done.1.refs_1_.refs_2_), channel_id=1, source_target_pairs={{0,2},{1,3},{2,0},{3,1},{4,6},{5,7},{6,4},{7,5},{8,10},{9,11},{10,... | collective-permute-start | bytes 2359304 | tf_op jit(solution)/shard_map/ppermute | solution.py:32
  28.9 0.0 collective-permute-done.3.refs_3_
  28.9 6.8 %collective-permute-done.5.refs_6_ = bf16[528,1024]{1,0:T(8,128)(2,1)S(1)} collective-permute-done((bf16[528,1024]{1,0:T(8,128)(2,1)S(1)}, bf16[528,1024]{1,0:T(8,128)(2,1)S(1)}, u32[]{:S(2)}, u32[]{:S(2)}) %collective-permute-start.5) | collective-permute-done | bytes 1081376 | tf_op jit(solution)/shard_map/ppermute | solution.py:32
  35.7 0.0 collective-permute-done.6.refs_3_.refs_4_
  35.7 0.0 collective-permute-done.7.refs_4_.refs_5_
  35.7 0.0 collective-permute-done.4.refs_2_
  35.7 0.5 collective-permute-start.8
  36.2 0.7 shard_map.52.refs_5_
  36.9 0.2 collective-permute-start.10
  37.1 0.7 collective-permute-start.11
  37.7 0.0 collective-permute-start.9
  37.7 2.7 %collective-permute-start.12 = (bf16[384,1024]{1,0:T(8,128)(2,1)S(1)}, bf16[384,1024]{1,0:T(8,128)(2,1)S(1)}, u32[]{:S(2)}, u32[]{:S(2)}) collective-permute-start(bf16[384,1024]{1,0:T(8,128)(2,1)S(1)} %collective-permute-done.1.refs_1_.refs_2_), channel_id=1, source_target_pairs={{0,16},{1,17},{2,50},{3,51},{4,20},{5,21},{6,54},{7,55},{8,24},{9,... | collective-permute-start | bytes 2359304 | tf_op jit(solution)/shard_map/ppermute | solution.py:32
  40.4 0.0 collective-permute-done.8.refs_2_.refs_3_
  40.4 4.9 %collective-permute-start.13 = (bf16[384,1024]{1,0:T(8,128)(2,1)S(1)}, bf16[384,1024]{1,0:T(8,128)(2,1)S(1)}, u32[]{:S(2)}, u32[]{:S(2)}) collective-permute-start(bf16[384,1024]{1,0:T(8,128)(2,1)S(1)} %collective-permute-done.6.refs_3_.refs_4_), channel_id=1, source_target_pairs={{0,65},{1,64},{2,67},{3,66},{4,69},{5,68},{6,71},{7,70},{8,73},{9,... | collective-permute-start | bytes 2359304 | tf_op jit(solution)/shard_map/ppermute | solution.py:32
  45.3 0.0 copy-done
  45.3 7.8 %shard_map.51 = (bf16[1024,1024]{1,0:T(8,128)(2,1)S(1)}, f32[1024,128]{1,0:T(8,128)S(1)}, bf16[3,768,1024]{2,1,0:T(8,128)(2,1)S(1)}, bf16[3,1024,768]{2,1,0:T(8,128)(2,1)S(1)}) custom-call(s32[12]{0:T(128)S(1)} %stack.51.numbers.ids.refs_0_, bf16[768,1024]{1,0:T(8,128)(2,1)} %refs_1_.1, bf16[384,1024]{1,0:T(8,128)(2,1)S(1)} %collective-permute-done.1.refs_1_.refs_2_, ...), custom_call_target="tpu_custom_call" | custom-call | flops 4831838208 | bytes 4718592 | tf_op jit(solution)/shard_map/pallas_call | solution.py:230
  53.1 0.0 collective-permute-done.11.refs_10_
  53.1 0.1 collective-permute-start.16
  53.2 0.0 collective-permute-done.9.refs_2_.refs_7_
  53.2 0.0 collective-permute-done.10.refs_6_
  53.2 11.3 %shard_map.53 = (f32[1024,512]{1,0:T(8,128)S(1)}, f32[1024,512]{1,0:T(8,128)S(1)}, bf16[1040,512]{1,0:T(8,128)(2,1)S(1)}, bf16[1024,768]{1,0:T(8,128)(2,1)S(1)}, bf16[832,512]{1,0:T(8,128)(2,1)S(1)}) custom-call(s32[12]{0:T(128)S(1)} %stack.51.numbers.ids.refs_0_, bf16[384,1024]{1,0:T(8,128)(2,1)S(1)} %collective-permute-done.refs_1_.refs_6_, ...), custom_call_target="tpu_custom_call" | custom-call | flops 16106127360 | bytes 6291456 | tf_op jit(solution)/shard_map/pallas_call | solution.py:448
  64.5 0.0 collective-permute-done.12.refs_8_
  64.5 0.0 collective-permute-done.13.refs_12_
  64.5 0.1 collective-permute-start.14
  64.6 0.5 collective-permute-start.15
  65.1 0.1 collective-permute-start.17
  65.2 0.0 collective-permute-done.16.refs_14_
  65.2 1.7 %collective-permute-done.14.refs_9_ = bf16[384,1024]{1,0:T(8,128)(2,1)S(1)} collective-permute-done((bf16[384,1024]{1,0:T(8,128)(2,1)S(1)}, bf16[384,1024]{1,0:T(8,128)(2,1)S(1)}, u32[]{:S(2)}, u32[]{:S(2)}) %collective-permute-start.14) | collective-permute-done | bytes 786464 | tf_op jit(solution)/shard_map/ppermute | solution.py:32
  66.9 1.1 %collective-permute-done.15.refs_11_ = bf16[384,1024]{1,0:T(8,128)(2,1)S(1)} collective-permute-done((bf16[384,1024]{1,0:T(8,128)(2,1)S(1)}, bf16[384,1024]{1,0:T(8,128)(2,1)S(1)}, u32[]{:S(2)}, u32[]{:S(2)}) %collective-permute-start.15) | collective-permute-done | bytes 786464 | tf_op jit(solution)/shard_map/ppermute | solution.py:32
  68.0 0.1 collective-permute-start.18
  68.2 1.0 %collective-permute-done.17.refs_13_ = bf16[384,1024]{1,0:T(8,128)(2,1)S(1)} collective-permute-done((bf16[384,1024]{1,0:T(8,128)(2,1)S(1)}, bf16[384,1024]{1,0:T(8,128)(2,1)S(1)}, u32[]{:S(2)}, u32[]{:S(2)}) %collective-permute-start.17) | collective-permute-done | bytes 786464 | tf_op jit(solution)/shard_map/ppermute | solution.py:32
  69.2 1.2 %collective-permute-done.18.refs_15_ = bf16[384,1024]{1,0:T(8,128)(2,1)S(1)} collective-permute-done((bf16[384,1024]{1,0:T(8,128)(2,1)S(1)}, bf16[384,1024]{1,0:T(8,128)(2,1)S(1)}, u32[]{:S(2)}, u32[]{:S(2)}) %collective-permute-start.18) | collective-permute-done | bytes 786464 | tf_op jit(solution)/shard_map/ppermute | solution.py:32
  70.3 27.4 %shard_map.54 = (f32[1024,1,512]{2,1,0:T(1,128)}, f32[1024,1,512]{2,1,0:T(1,128)}, f32[1024,512]{1,0:T(8,128)S(1)}, f32[1024,512]{1,0:T(8,128)S(1)}) custom-call(s32[12]{0:T(128)S(1)} %stack.51.numbers.ids.refs_0_, bf16[768,1024]{1,0:T(8,128)(2,1)} %refs_1_.1, ...), custom_call_target="tpu_custom_call", output_to_operand_aliasing={{2}: (21, {}), {3}: (22, {})} | custom-call | flops 20132659200 | bytes 7864320 | tf_op jit(solution)/shard_map/pallas_call | solution.py:448
Async XLA Ops:
  3.0 8.3 %collective-permute-start.2 = (bf16[1040,512]{1,0:T(8,128)(2,1)S(1)}, bf16[1040,512]{1,0:T(8,128)(2,1)S(1)}, u32[]{:S(2)}, u32[]{:S(2)}) collective-permute-start(bf16[1040,512]{1,0:T(8,128)(2,1)S(1)} %get-tuple-element.49.refs_0_), channel_id=1, source_target_pairs={{0,4},{1,5},{18,22},{19,23},{36,40},{37,41},{54,58},{55,59},{72,76... | collective-permute-start | bytes 3194888 | tf_op jit(solution)/shard_map/ppermute | solution.py:32
  3.7 14.8 %collective-permute-start.1 = (bf16[384,1024]{1,0:T(8,128)(2,1)S(1)}, bf16[384,1024]{1,0:T(8,128)(2,1)S(1)}, u32[]{:S(2)}, u32[]{:S(2)}) collective-permute-start(bf16[384,1024]{1,0:T(8,128)(2,1)S(1)} %get-tuple-element.51), channel_id=1, source_target_pairs={{0,16},{1,17},{2,50},{3,51},{4,20},{5,21},{6,54},{7,55},{8,24},{9,... | collective-permute-start | bytes 2359304 | tf_op jit(solution)/shard_map/ppermute | solution.py:32
  7.4 19.8 %collective-permute-start = (bf16[384,1024]{1,0:T(8,128)(2,1)S(1)}, bf16[384,1024]{1,0:T(8,128)(2,1)S(1)}, u32[]{:S(2)}, u32[]{:S(2)}) collective-permute-start(bf16[384,1024]{1,0:T(8,128)(2,1)S(1)} %get-tuple-element.51), channel_id=1, source_target_pairs={{0,65},{1,64},{2,67},{3,66},{4,69},{5,68},{6,71},{7,70},{8,73},{9,... | collective-permute-start | bytes 2359304 | tf_op jit(solution)/shard_map/ppermute | solution.py:32
  10.4 34.9 %copy-start = (f32[512]{0:T(512)S(1)}, f32[512]{0:T(512)}, u32[]{:S(2)}) copy-start(f32[512]{0:T(512)} %param.5) | copy-start | bytes 6148
  10.4 25.3 %collective-permute-start.5 = (bf16[528,1024]{1,0:T(8,128)(2,1)S(1)}, bf16[528,1024]{1,0:T(8,128)(2,1)S(1)}, u32[]{:S(2)}, u32[]{:S(2)}) collective-permute-start(bf16[528,1024]{1,0:T(8,128)(2,1)S(1)} %get-tuple-element.50.refs_5_), channel_id=1, source_target_pairs={{0,1},{1,0},{2,3},{3,2},{4,5},{5,4},{6,7},{7,6},{8,9},{9,8},{10,11... | collective-permute-start | bytes 3244040 | tf_op jit(solution)/shard_map/ppermute | solution.py:32
  10.4 18.5 %collective-permute-start.3 = (bf16[1040,512]{1,0:T(8,128)(2,1)S(1)}, bf16[1040,512]{1,0:T(8,128)(2,1)S(1)}, u32[]{:S(2)}, u32[]{:S(2)}) collective-permute-start(bf16[1040,512]{1,0:T(8,128)(2,1)S(1)} %get-tuple-element.49.refs_0_), channel_id=1, source_target_pairs={{0,12},{1,13},{18,30},{19,31},{36,32},{37,33},{54,50},{55,51},{72,... | collective-permute-start | bytes 3194888 | tf_op jit(solution)/shard_map/ppermute | solution.py:32
  11.3 24.4 %collective-permute-start.4 = (bf16[1040,512]{1,0:T(8,128)(2,1)S(1)}, bf16[1040,512]{1,0:T(8,128)(2,1)S(1)}, u32[]{:S(2)}, u32[]{:S(2)}) collective-permute-start(bf16[1040,512]{1,0:T(8,128)(2,1)S(1)} %get-tuple-element.49.refs_0_), channel_id=1, source_target_pairs={{0,8},{1,9},{18,26},{19,27},{36,44},{37,45},{54,62},{55,63},{72,64... | collective-permute-start | bytes 3194888 | tf_op jit(solution)/shard_map/ppermute | solution.py:32
  18.5 17.2 %collective-permute-start.6 = (bf16[384,1024]{1,0:T(8,128)(2,1)S(1)}, bf16[384,1024]{1,0:T(8,128)(2,1)S(1)}, u32[]{:S(2)}, u32[]{:S(2)}) collective-permute-start(bf16[384,1024]{1,0:T(8,128)(2,1)S(1)} %get-tuple-element.51), channel_id=1, source_target_pairs={{0,48},{1,49},{2,18},{3,19},{4,52},{5,53},{6,22},{7,23},{8,56},{9,... | collective-permute-start | bytes 2359304 | tf_op jit(solution)/shard_map/ppermute | solution.py:32
  27.2 8.5 %collective-permute-start.7 = (bf16[384,1024]{1,0:T(8,128)(2,1)S(1)}, bf16[384,1024]{1,0:T(8,128)(2,1)S(1)}, u32[]{:S(2)}, u32[]{:S(2)}) collective-permute-start(bf16[384,1024]{1,0:T(8,128)(2,1)S(1)} %collective-permute-done.1.refs_1_.refs_2_), channel_id=1, source_target_pairs={{0,2},{1,3},{2,0},{3,1},{4,6},{5,7},{6,4},{7,5},{8,10},{9,11},{10,... | collective-permute-start | bytes 2359304 | tf_op jit(solution)/shard_map/ppermute | solution.py:32
  35.7 4.7 %collective-permute-start.8 = (bf16[384,1024]{1,0:T(8,128)(2,1)S(1)}, bf16[384,1024]{1,0:T(8,128)(2,1)S(1)}, u32[]{:S(2)}, u32[]{:S(2)}) collective-permute-start(bf16[384,1024]{1,0:T(8,128)(2,1)S(1)} %collective-permute-done.6.refs_3_.refs_4_), channel_id=1, source_target_pairs={{0,2},{1,3},{2,0},{3,1},{4,6},{5,7},{6,4},{7,5},{8,10},{9,11},{10,... | collective-permute-start | bytes 2359304 | tf_op jit(solution)/shard_map/ppermute | solution.py:32
  36.9 16.4 %collective-permute-start.10 = (bf16[1040,512]{1,0:T(8,128)(2,1)S(1)}, bf16[1040,512]{1,0:T(8,128)(2,1)S(1)}, u32[]{:S(2)}, u32[]{:S(2)}) collective-permute-start(bf16[1040,512]{1,0:T(8,128)(2,1)S(1)} %shard_map.52.refs_5_), channel_id=1, source_target_pairs={{0,2},{1,3},{2,0},{3,1},{4,6},{5,7},{6,4},{7,5},{8,10},{9,11},{10,... | collective-permute-start | bytes 3194888 | tf_op jit(solution)/shard_map/ppermute | solution.py:32
  37.1 16.1 %collective-permute-start.11 = (bf16[384,1024]{1,0:T(8,128)(2,1)S(1)}, bf16[384,1024]{1,0:T(8,128)(2,1)S(1)}, u32[]{:S(2)}, u32[]{:S(2)}) collective-permute-start(bf16[384,1024]{1,0:T(8,128)(2,1)S(1)} %collective-permute-done.refs_1_.refs_6_), channel_id=1, source_target_pairs={{0,16},{1,17},{2,50},{3,51},{4,20},{5,21},{6,54},{7,55},{8,24},{9,... | collective-permute-start | bytes 2359304 | tf_op jit(solution)/shard_map/ppermute | solution.py:32
  37.7 15.5 %collective-permute-start.9 = (bf16[384,1024]{1,0:T(8,128)(2,1)S(1)}, bf16[384,1024]{1,0:T(8,128)(2,1)S(1)}, u32[]{:S(2)}, u32[]{:S(2)}) collective-permute-start(bf16[384,1024]{1,0:T(8,128)(2,1)S(1)} %collective-permute-done.refs_1_.refs_6_), channel_id=1, source_target_pairs={{0,2},{1,3},{2,0},{3,1},{4,6},{5,7},{6,4},{7,5},{8,10},{9,11},{10,... | collective-permute-start | bytes 2359304 | tf_op jit(solution)/shard_map/ppermute | solution.py:32
  37.7 26.8 %collective-permute-start.12 = (bf16[384,1024]{1,0:T(8,128)(2,1)S(1)}, bf16[384,1024]{1,0:T(8,128)(2,1)S(1)}, u32[]{:S(2)}, u32[]{:S(2)}) collective-permute-start(bf16[384,1024]{1,0:T(8,128)(2,1)S(1)} %collective-permute-done.1.refs_1_.refs_2_), channel_id=1, source_target_pairs={{0,16},{1,17},{2,50},{3,51},{4,20},{5,21},{6,54},{7,55},{8,24},{9,... | collective-permute-start | bytes 2359304 | tf_op jit(solution)/shard_map/ppermute | solution.py:32
  40.4 24.1 %collective-permute-start.13 = (bf16[384,1024]{1,0:T(8,128)(2,1)S(1)}, bf16[384,1024]{1,0:T(8,128)(2,1)S(1)}, u32[]{:S(2)}, u32[]{:S(2)}) collective-permute-start(bf16[384,1024]{1,0:T(8,128)(2,1)S(1)} %collective-permute-done.6.refs_3_.refs_4_), channel_id=1, source_target_pairs={{0,65},{1,64},{2,67},{3,66},{4,69},{5,68},{6,71},{7,70},{8,73},{9,... | collective-permute-start | bytes 2359304 | tf_op jit(solution)/shard_map/ppermute | solution.py:32
  53.1 12.1 %collective-permute-start.16 = (bf16[384,1024]{1,0:T(8,128)(2,1)S(1)}, bf16[384,1024]{1,0:T(8,128)(2,1)S(1)}, u32[]{:S(2)}, u32[]{:S(2)}) collective-permute-start(bf16[384,1024]{1,0:T(8,128)(2,1)S(1)} %collective-permute-done.11.refs_10_), channel_id=1, source_target_pairs={{0,16},{1,17},{2,50},{3,51},{4,20},{5,21},{6,54},{7,55},{8,24},{9,... | collective-permute-start | bytes 2359304 | tf_op jit(solution)/shard_map/ppermute | solution.py:32
  64.5 2.4 %collective-permute-start.14 = (bf16[384,1024]{1,0:T(8,128)(2,1)S(1)}, bf16[384,1024]{1,0:T(8,128)(2,1)S(1)}, u32[]{:S(2)}, u32[]{:S(2)}) collective-permute-start(bf16[384,1024]{1,0:T(8,128)(2,1)S(1)} %collective-permute-done.12.refs_8_), channel_id=1, source_target_pairs={{0,2},{1,3},{2,0},{3,1},{4,6},{5,7},{6,4},{7,5},{8,10},{9,11},{10,... | collective-permute-start | bytes 2359304 | tf_op jit(solution)/shard_map/ppermute | solution.py:32
  64.6 3.4 %collective-permute-start.15 = (bf16[384,1024]{1,0:T(8,128)(2,1)S(1)}, bf16[384,1024]{1,0:T(8,128)(2,1)S(1)}, u32[]{:S(2)}, u32[]{:S(2)}) collective-permute-start(bf16[384,1024]{1,0:T(8,128)(2,1)S(1)} %collective-permute-done.13.refs_12_), channel_id=1, source_target_pairs={{0,2},{1,3},{2,0},{3,1},{4,6},{5,7},{6,4},{7,5},{8,10},{9,11},{10,... | collective-permute-start | bytes 2359304 | tf_op jit(solution)/shard_map/ppermute | solution.py:32
  65.1 4.0 %collective-permute-start.17 = (bf16[384,1024]{1,0:T(8,128)(2,1)S(1)}, bf16[384,1024]{1,0:T(8,128)(2,1)S(1)}, u32[]{:S(2)}, u32[]{:S(2)}) collective-permute-start(bf16[384,1024]{1,0:T(8,128)(2,1)S(1)} %collective-permute-done.11.refs_10_), channel_id=1, source_target_pairs={{0,2},{1,3},{2,0},{3,1},{4,6},{5,7},{6,4},{7,5},{8,10},{9,11},{10,... | collective-permute-start | bytes 2359304 | tf_op jit(solution)/shard_map/ppermute | solution.py:32
  68.0 2.3 %collective-permute-start.18 = (bf16[384,1024]{1,0:T(8,128)(2,1)S(1)}, bf16[384,1024]{1,0:T(8,128)(2,1)S(1)}, u32[]{:S(2)}, u32[]{:S(2)}) collective-permute-start(bf16[384,1024]{1,0:T(8,128)(2,1)S(1)} %collective-permute-done.16.refs_14_), channel_id=1, source_target_pairs={{0,2},{1,3},{2,0},{3,1},{4,6},{5,7},{6,4},{7,5},{8,10},{9,11},{10,... | collective-permute-start | bytes 2359304 | tf_op jit(solution)/shard_map/ppermute | solution.py:32

commit v3 on v2

--- a/solution.py
+++ b/solution.py
@@ -252,22 +252,21 @@
     take = lambda n: [refs.pop(0) for _ in range(n)]
     (ids,) = take(1)
     slabs = (valid_rows + LAG) // slab_rows
-    pieces = [take(1 if last and k == 0 else 2) for k in range(slabs if last else count - ready)]
-    here = [None] * ready + pieces[ready - count:]
+    pieces = [None] * ready + [take(2) for _ in range(count - ready)]
     if first:
         ready_slab, ready_rows, *columns, row_proj, row_off = take(6)
     else:
         row_proj, row_off, col_proj, row_next, col_next = take(5)
-        take(2)
+        take(4)
         acc_out = take(2)
-    instant, lagged = take(2)
+    instant, lagged, tails, heads = take(4)
     if first:
         col_proj, row_next, col_next = take(3)
     slab, turned_states, row_a, row_b, col_a, col_b, in_sem = take(7)
     if first:
         (proj_sem,) = take(1)
     if last:
-        tails, heads, turned_edges, edge_sem, out_sem = take(5)
+        turned_edges, out_sem = take(2)
     rows, cols = instant.shape
     units = col_proj.shape[0] - SPARE
     half = slab_rows // 2
@@ -275,25 +274,17 @@
     core, col, source = ids[slabs], ids[slabs + 1], ids[slabs + 2]
     number = lambda k: ids[at + k]
 
-    loads = [[] if k < ready else slab_copies(here[k], core, slab.at[k - ready], in_sem.at[k - ready]) for k in range(count)]
+    loads = [[] if k < ready else slab_copies(pieces[k], core, slab.at[k - ready], in_sem.at[k - ready]) for k in range(count)]
     states = lambda k: ready_slab.at[k] if k < ready else slab.at[k - ready]
     between = count - 1 if first else 0
     row_bufs = lambda k: row_next if k == between else (row_a, row_b)[k % 2]
     col_bufs = lambda k: col_next if k == between else (col_a, col_b)[k % 2]
-    col_loads, edge_loads = [], []
-    if first:
-        col_loads = [OneOf(source, columns, col_proj, proj_sem)]
-    if last:
-        for k, piece in enumerate(pieces):
-            tail, head = tails.at[ids[k]], heads.at[lax.rem(ids[k] + slabs - 1, slabs)]
-            if len(piece) == 1:
-                edge_loads.append(pltpu.make_async_copy(piece[0].at[pl.ds(slab_rows - LAG, LAG)], tail, edge_sem.at[k, 0]))
-                edge_loads.append(pltpu.make_async_copy(piece[0].at[pl.ds(0, LAG)], head, edge_sem.at[k, 1]))
-            else:
-                ends = [p.at[pl.ds(half - LAG, LAG)] for p in piece]
-                starts = [p.at[pl.ds(0, LAG)] for p in piece]
-                edge_loads.append(OneOf(1 - core, ends, tail, edge_sem.at[k, 0]))
-                edge_loads.append(OneOf(core, starts, head, edge_sem.at[k, 1]))
+    col_loads = [OneOf(source, columns, col_proj, proj_sem)] if first else []
+
+    def keep_borders(k):
+        tails[number(k)] = states(k)[slab_rows - LAG:]
+        heads[lax.rem(number(k) + slabs - 1, slabs)] = states(k)[:LAG]
+
     start([*col_loads, *loads[ready]])
 
     for buf in (col_a, col_b) + ((col_next,) if first else ()):
@@ -378,6 +369,8 @@
         wait(col_loads)
         for step in feature_steps(0):
             step()
+        for k in range(ready):
+            keep_borders(k)
     for k in range(count - 1 if first else count):
         ahead = []
         steps = [functools.partial(moment_tile, k, lag, n, h) for lag in (0, LAG) for h in range(2) for n in range(COL_TILES)]
@@ -386,13 +379,12 @@
             steps.pop(0)()
         if k + 1 < count:
             wait(loads[k + 1])
-            if k + 2 < count:
-                start(loads[k + 2] if last else [])
-            elif last:
-                start(edge_loads)
+            if last and k + 2 < count:
+                start(loads[k + 2])
             ahead = feature_steps(k + 1)
+            if k + 1 >= ready:
+                keep_borders(k + 1)
         elif last:
-            wait(edge_loads)
             ahead = [functools.partial(edge_cols, n) for n in range(COL_TILES)]
             ahead += [functools.partial(edge_rows, h) for h in range(2)]
         interleave(steps, ahead)
@@ -403,18 +395,16 @@
         wait(stores[0] + stores[1])
 
 
-def moments(slabs, count, numbers, opened, panels, carry, slab_rows, valid_rows):
+def moments(slabs, at, numbers, opened, panels, carry, slab_rows, valid_rows):
     first, last = carry is None, carry is not None
     units = slabs[0][0].shape[1]
     cols = panels[0].shape[1] if first else carry[0].shape[1]
-    rows = 2 * cols
-    at = len(slabs) - count
+    rows, borders = 2 * cols, valid_rows // slab_rows + 1
     ready = opened[0].shape[0] if first else 1
-    if first:
-        slabs = slabs[at + ready:]
+    count = ready + len(slabs)
     pieces = [p for s in slabs for p in s]
     end_shape = (rows, 1, cols)
-    outs = [pltpu.VMEM((rows, cols), jnp.float32)] * 2
+    outs = [pltpu.VMEM((rows, cols), jnp.float32)] * 2 + [pltpu.VMEM((borders, LAG, units), jnp.bfloat16)] * 2
     dma = pltpu.SemaphoreType.DMA
     scratch = [
         pltpu.VMEM((count - ready, slab_rows, units), jnp.bfloat16),
@@ -436,15 +426,14 @@
             pltpu.VMEM((rows, slab_rows), jnp.bfloat16),
             pltpu.VMEM((slab_rows + LAG, cols), jnp.bfloat16),
         ]
-        out_specs = [vmem_spec()] * 5
+        out_specs = [vmem_spec()] * 7
         scratch.append(dma)
     else:
-        outs, out_specs = [pltpu.HBM(end_shape, jnp.float32)] * 2 + outs, [hbm_spec()] * 2 + [vmem_spec()] * 2
-        scratch += [pltpu.VMEM((len(slabs), LAG, units), jnp.bfloat16)] * 2
-        scratch += [pltpu.VMEM((units, len(slabs) * LAG), jnp.bfloat16), dma((len(slabs), 2)), dma((2, 4))]
-        args += [in_vmem(x) for x in (*panels, *carry[2:], *carry[:2])]
-        specs += [vmem_spec()] * 7
-        aliases = {len(args) - 2 + n: 2 + n for n in range(2)}
+        outs, out_specs = [pltpu.HBM(end_shape, jnp.float32)] * 2 + outs, [hbm_spec()] * 2 + [vmem_spec()] * 4
+        scratch += [pltpu.VMEM((units, borders * LAG), jnp.bfloat16), dma((2, 4))]
+        args += [in_vmem(x) for x in (*panels, *carry[4:], *carry[:4])]
+        specs += [vmem_spec()] * 9
+        aliases = {len(args) - 4 + n: 2 + n for n in range(4)}
     return pl.pallas_call(
         functools.partial(moments_kernel, count, ready, at, last, slab_rows, valid_rows),
         in_specs=specs,
@@ -503,14 +492,13 @@
     over_out, y_far, over_back = move(over, out_y), move(y_out, out_y), move(y_back, crossing)
     row_off, over_out = lax.optimization_barrier((row_off, over_out))
     over_far = move(over_out, out_y)
-    slabs += [(over, swapped_over)]
-    carry = moments(slabs, 4, numbers, opened, (panel, swapped, row_proj, row_off), None, *sizes)
+    carry = moments([(over, swapped_over)], 0, numbers, opened, (panel, swapped, row_proj, row_off), None, *sizes)
 
     *carry, y_far, over_back = lax.optimization_barrier((*carry, y_far, over_back))
     swapped_far, swapped_over_back = swap(y_far), swap(over_back)
     swapped_far, swapped_over_back, over_far = lax.optimization_barrier((swapped_far, swapped_over_back, over_far))
-    slabs += [(y_far, swapped_far), (over_out, swapped_over_back), (over_back, swap(over_out)), (over_far, swap(over_far))]
-    instant, lagged, *_ = moments(slabs, 5, numbers, None, (row_proj, row_off), carry, *sizes)
+    slabs = [(y_far, swapped_far), (over_out, swapped_over_back), (over_back, swap(over_out)), (over_far, swap(over_far))]
+    instant, lagged, *_ = moments(slabs, 3, numbers, None, (row_proj, row_off), carry, *sizes)
     return instant, lagged
 
 

time: 98.9 us -> 95.8 us (0.969)
  Pallas kernels: 49.3 us -> 46.3 us
    pallas_call x2, Pallas kernels: 38.7 us -> 35.6 us  [moments(): pl.pallas_call(functools.partial(moments_kernel, count, ready, at, last,...]
  transfers between devices with their start and end apart: 19 -> 19, of which waited for: 7 -> 7; matrix products, arithmetic and copies ran while one was open for 0% -> 0% of each run, Pallas kernels for 20% -> 21%
where the time goes in v3:
time: 95.8 us; the launch traced here: 94.9 us
  Pallas kernels  46.3 us (48%)
  starting transfers between devices  24 us (25%)
  waiting for transfers between devices  23.4 us (24%)
  between operations  1.11 us (1%)
    pallas_call x2, Pallas kernels, moments(): pl.pallas_call(functools.partial(moments_kernel, count, ready, at, last,...  35.6 us
    ppermute x19, starting transfers between devices, move(): return lax.ppermute(block, AXES, route(target))  24 us
    ppermute x19, waiting for transfers between devices, move(): return lax.ppermute(block, AXES, route(target))  23.4 us
    pallas_call x1, Pallas kernels, opening(): pl.pallas_call(functools.partial(opening_kernel, count, valid_rows), in_s...  7.81 us
    pallas_call x1, Pallas kernels, prepare(): pl.pallas_call(functools.partial(prepare_kernel, at), in_specs=[smem_spec...  2.14 us
  transfers between devices with their start and end apart: 19, of which 7 were waited for; matrix products, arithmetic and copies ran while one was open for 0% of the time, Pallas kernels for 21%

profile of v3, /device:TPU:1, one launch (start us, length us, event | category | flops | bytes accessed | tf_op | source)
XLA Modules:
  0.0 94.9 jit_solution(18111611547159055294)
XLA Ops:
  0.8 0.1 stack.51.numbers.ids.refs_0_
  0.9 2.1 %shard_map.50 = (bf16[1040,512]{1,0:T(8,128)(2,1)S(1)}, bf16[528,1024]{1,0:T(8,128)(2,1)S(1)}, bf16[384,1024]{1,0:T(8,128)(2,1)S(1)}) custom-call(s32[12]{0:T(128)S(1)} %stack.51.numbers.ids.refs_0_, bf16[1024,512]{1,0:T(8,128)(2,1)} %projection.1, f32[1,512]{1,0:T(1,128)} %bitcast.13, bf16[768,1024]{1,0:T(8,128)(2,1)} %refs_0_.1), custom_call_target="tpu_custom_call" | custom-call | tf_op jit(solution)/shard_map/pallas_call | solution.py:138
  3.0 0.7 collective-permute-start.3
  3.7 3.6 %collective-permute-start.1 = (bf16[384,1024]{1,0:T(8,128)(2,1)S(1)}, bf16[384,1024]{1,0:T(8,128)(2,1)S(1)}, u32[]{:S(2)}, u32[]{:S(2)}) collective-permute-start(bf16[384,1024]{1,0:T(8,128)(2,1)S(1)} %get-tuple-element.56), channel_id=1, source_target_pairs={{0,16},{1,17},{2,50},{3,51},{4,20},{5,21},{6,54},{7,55},{8,24},{9,... | collective-permute-start | bytes 2359304 | tf_op jit(solution)/shard_map/ppermute | solution.py:32
  7.4 3.0 %collective-permute-start = (bf16[384,1024]{1,0:T(8,128)(2,1)S(1)}, bf16[384,1024]{1,0:T(8,128)(2,1)S(1)}, u32[]{:S(2)}, u32[]{:S(2)}) collective-permute-start(bf16[384,1024]{1,0:T(8,128)(2,1)S(1)} %get-tuple-element.56), channel_id=1, source_target_pairs={{0,65},{1,64},{2,67},{3,66},{4,69},{5,68},{6,71},{7,70},{8,73},{9,... | collective-permute-start | bytes 2359304 | tf_op jit(solution)/shard_map/ppermute | solution.py:32
  10.4 0.0 copy-start
  10.4 0.0 collective-permute-start.6
  10.4 0.8 collective-permute-start.4
  11.3 0.0 collective-permute-done.3.refs_1_
  11.3 0.7 collective-permute-start.5
  12.0 6.5 %collective-permute-done.1.refs_1_ = bf16[384,1024]{1,0:T(8,128)(2,1)S(1)} collective-permute-done((bf16[384,1024]{1,0:T(8,128)(2,1)S(1)}, bf16[384,1024]{1,0:T(8,128)(2,1)S(1)}, u32[]{:S(2)}, u32[]{:S(2)}) %collective-permute-start.1) | collective-permute-done | bytes 786464 | tf_op jit(solution)/shard_map/ppermute | solution.py:32
  18.5 3.5 %collective-permute-start.7 = (bf16[384,1024]{1,0:T(8,128)(2,1)S(1)}, bf16[384,1024]{1,0:T(8,128)(2,1)S(1)}, u32[]{:S(2)}, u32[]{:S(2)}) collective-permute-start(bf16[384,1024]{1,0:T(8,128)(2,1)S(1)} %get-tuple-element.56), channel_id=1, source_target_pairs={{0,48},{1,49},{2,18},{3,19},{4,52},{5,53},{6,22},{7,23},{8,56},{9,... | collective-permute-start | bytes 2359304 | tf_op jit(solution)/shard_map/ppermute | solution.py:32
  22.0 5.2 %collective-permute-done.refs_1_ = bf16[384,1024]{1,0:T(8,128)(2,1)S(1)} collective-permute-done((bf16[384,1024]{1,0:T(8,128)(2,1)S(1)}, bf16[384,1024]{1,0:T(8,128)(2,1)S(1)}, u32[]{:S(2)}, u32[]{:S(2)}) %collective-permute-start) | collective-permute-done | bytes 786464 | tf_op jit(solution)/shard_map/ppermute | solution.py:32
  27.2 1.7 %collective-permute-start.8 = (bf16[384,1024]{1,0:T(8,128)(2,1)S(1)}, bf16[384,1024]{1,0:T(8,128)(2,1)S(1)}, u32[]{:S(2)}, u32[]{:S(2)}) collective-permute-start(bf16[384,1024]{1,0:T(8,128)(2,1)S(1)} %collective-permute-done.1.refs_1_), channel_id=1, source_target_pairs={{0,2},{1,3},{2,0},{3,1},{4,6},{5,7},{6,4},{7,5},{8,10},{9,11},{10,... | collective-permute-start | bytes 2359304 | tf_op jit(solution)/shard_map/ppermute | solution.py:32
  28.9 0.0 collective-permute-done.4.refs_3_
  28.9 6.8 %collective-permute-done.6.refs_6_ = bf16[528,1024]{1,0:T(8,128)(2,1)S(1)} collective-permute-done((bf16[528,1024]{1,0:T(8,128)(2,1)S(1)}, bf16[528,1024]{1,0:T(8,128)(2,1)S(1)}, u32[]{:S(2)}, u32[]{:S(2)}) %collective-permute-start.6) | collective-permute-done | bytes 1081376 | tf_op jit(solution)/shard_map/ppermute | solution.py:32
  35.7 0.0 collective-permute-done.7.refs_3_
  35.7 0.0 collective-permute-done.8.refs_4_
  35.7 0.0 collective-permute-done.5.refs_2_
  35.7 0.5 collective-permute-start.9
  36.2 0.7 shard_map.52.refs_5_
  36.9 0.2 collective-permute-start.10
  37.1 0.7 collective-permute-start.11
  37.7 0.0 collective-permute-start.2
  37.7 2.7 %collective-permute-start.12 = (bf16[384,1024]{1,0:T(8,128)(2,1)S(1)}, bf16[384,1024]{1,0:T(8,128)(2,1)S(1)}, u32[]{:S(2)}, u32[]{:S(2)}) collective-permute-start(bf16[384,1024]{1,0:T(8,128)(2,1)S(1)} %collective-permute-done.1.refs_1_), channel_id=1, source_target_pairs={{0,16},{1,17},{2,50},{3,51},{4,20},{5,21},{6,54},{7,55},{8,24},{9,... | collective-permute-start | bytes 2359304 | tf_op jit(solution)/shard_map/ppermute | solution.py:32
  40.4 0.0 collective-permute-done.9.refs_2_
  40.4 4.9 %collective-permute-start.13 = (bf16[384,1024]{1,0:T(8,128)(2,1)S(1)}, bf16[384,1024]{1,0:T(8,128)(2,1)S(1)}, u32[]{:S(2)}, u32[]{:S(2)}) collective-permute-start(bf16[384,1024]{1,0:T(8,128)(2,1)S(1)} %collective-permute-done.7.refs_3_), channel_id=1, source_target_pairs={{0,65},{1,64},{2,67},{3,66},{4,69},{5,68},{6,71},{7,70},{8,73},{9,... | collective-permute-start | bytes 2359304 | tf_op jit(solution)/shard_map/ppermute | solution.py:32
  45.3 0.0 copy-done
  45.3 7.8 %shard_map.51 = (bf16[1024,1024]{1,0:T(8,128)(2,1)S(1)}, f32[1024,128]{1,0:T(8,128)S(1)}, bf16[3,768,1024]{2,1,0:T(8,128)(2,1)S(1)}, bf16[3,1024,768]{2,1,0:T(8,128)(2,1)S(1)}) custom-call(s32[12]{0:T(128)S(1)} %stack.51.numbers.ids.refs_0_, bf16[768,1024]{1,0:T(8,128)(2,1)} %refs_0_.1, bf16[384,1024]{1,0:T(8,128)(2,1)S(1)} %collective-permute-done.1.refs_1_, ...), custom_call_target="tpu_custom_call" | custom-call | flops 4831838208 | bytes 4718592 | tf_op jit(solution)/shard_map/pallas_call | solution.py:230
  53.1 0.0 collective-permute-done.11.refs_3_
  53.2 0.1 collective-permute-start.16
  53.2 0.0 collective-permute-done.2.refs_2_
  53.2 0.0 collective-permute-done.10.refs_6_
  53.3 11.3 %shard_map.53 = (f32[1024,512]{1,0:T(8,128)S(1)}, f32[1024,512]{1,0:T(8,128)S(1)}, bf16[8,64,1024]{2,1,0:T(8,128)(2,1)S(1)}, bf16[8,64,1024]{2,1,0:T(8,128)(2,1)...) custom-call(s32[12]{0:T(128)S(1)} %stack.51.numbers.ids.refs_0_, ...), custom_call_target="tpu_custom_call" | custom-call | flops 16106127360 | bytes 6291456 | tf_op jit(solution)/shard_map/pallas_call | solution.py:437
  64.5 0.0 collective-permute-done.12.refs_1_
  64.5 0.0 collective-permute-done.13.refs_5_
  64.6 0.1 collective-permute-start.14
  64.6 0.5 collective-permute-start.15
  65.1 0.1 collective-permute-start.17
  65.2 0.0 collective-permute-done.16.refs_7_
  65.2 1.7 %collective-permute-done.14.refs_2_ = bf16[384,1024]{1,0:T(8,128)(2,1)S(1)} collective-permute-done((bf16[384,1024]{1,0:T(8,128)(2,1)S(1)}, bf16[384,1024]{1,0:T(8,128)(2,1)S(1)}, u32[]{:S(2)}, u32[]{:S(2)}) %collective-permute-start.14) | collective-permute-done | bytes 786464 | tf_op jit(solution)/shard_map/ppermute | solution.py:32
  66.9 1.1 %collective-permute-done.15.refs_4_ = bf16[384,1024]{1,0:T(8,128)(2,1)S(1)} collective-permute-done((bf16[384,1024]{1,0:T(8,128)(2,1)S(1)}, bf16[384,1024]{1,0:T(8,128)(2,1)S(1)}, u32[]{:S(2)}, u32[]{:S(2)}) %collective-permute-start.15) | collective-permute-done | bytes 786464 | tf_op jit(solution)/shard_map/ppermute | solution.py:32
  68.0 0.1 collective-permute-start.18
  68.2 1.0 %collective-permute-done.17.refs_6_ = bf16[384,1024]{1,0:T(8,128)(2,1)S(1)} collective-permute-done((bf16[384,1024]{1,0:T(8,128)(2,1)S(1)}, bf16[384,1024]{1,0:T(8,128)(2,1)S(1)}, u32[]{:S(2)}, u32[]{:S(2)}) %collective-permute-start.17) | collective-permute-done | bytes 786464 | tf_op jit(solution)/shard_map/ppermute | solution.py:32
  69.2 1.2 %collective-permute-done.18.refs_8_ = bf16[384,1024]{1,0:T(8,128)(2,1)S(1)} collective-permute-done((bf16[384,1024]{1,0:T(8,128)(2,1)S(1)}, bf16[384,1024]{1,0:T(8,128)(2,1)S(1)}, u32[]{:S(2)}, u32[]{:S(2)}) %collective-permute-start.18) | collective-permute-done | bytes 786464 | tf_op jit(solution)/shard_map/ppermute | solution.py:32
  70.3 24.4 %shard_map.54 = (f32[1024,1,512]{2,1,0:T(1,128)}, f32[1024,1,512]{2,1,0:T(1,128)}, f32[1024,512]{1,0:T(8,128)S(1)}, f32[1024,512]{1,0:T(8,128)S(1)}, bf16[8,64,1...) custom-call(s32[12]{0:T(128)S(1)} %stack.51.numbers.ids.refs_0_, ...), custom_call_target="tpu_custom_call", output_to_operand_aliasing={{2}: (14, {}), {3}: (15, {}), {4}: (16, {}), {5}: (17, {})} | custom-call | flops 20132659200 | bytes 7864320 | tf_op jit(solution)/shard_map/pallas_call | solution.py:437
Async XLA Ops:
  3.0 8.3 %collective-permute-start.3 = (bf16[1040,512]{1,0:T(8,128)(2,1)S(1)}, bf16[1040,512]{1,0:T(8,128)(2,1)S(1)}, u32[]{:S(2)}, u32[]{:S(2)}) collective-permute-start(bf16[1040,512]{1,0:T(8,128)(2,1)S(1)} %get-tuple-element.54.refs_0_), channel_id=1, source_target_pairs={{0,4},{1,5},{18,22},{19,23},{36,40},{37,41},{54,58},{55,59},{72,76... | collective-permute-start | bytes 3194888 | tf_op jit(solution)/shard_map/ppermute | solution.py:32
  3.7 14.8 %collective-permute-start.1 = (bf16[384,1024]{1,0:T(8,128)(2,1)S(1)}, bf16[384,1024]{1,0:T(8,128)(2,1)S(1)}, u32[]{:S(2)}, u32[]{:S(2)}) collective-permute-start(bf16[384,1024]{1,0:T(8,128)(2,1)S(1)} %get-tuple-element.56), channel_id=1, source_target_pairs={{0,16},{1,17},{2,50},{3,51},{4,20},{5,21},{6,54},{7,55},{8,24},{9,... | collective-permute-start | bytes 2359304 | tf_op jit(solution)/shard_map/ppermute | solution.py:32
  7.4 19.8 %collective-permute-start = (bf16[384,1024]{1,0:T(8,128)(2,1)S(1)}, bf16[384,1024]{1,0:T(8,128)(2,1)S(1)}, u32[]{:S(2)}, u32[]{:S(2)}) collective-permute-start(bf16[384,1024]{1,0:T(8,128)(2,1)S(1)} %get-tuple-element.56), channel_id=1, source_target_pairs={{0,65},{1,64},{2,67},{3,66},{4,69},{5,68},{6,71},{7,70},{8,73},{9,... | collective-permute-start | bytes 2359304 | tf_op jit(solution)/shard_map/ppermute | solution.py:32
  10.4 34.9 %copy-start = (f32[512]{0:T(512)S(1)}, f32[512]{0:T(512)}, u32[]{:S(2)}) copy-start(f32[512]{0:T(512)} %param.5) | copy-start | bytes 6148
  10.4 25.3 %collective-permute-start.6 = (bf16[528,1024]{1,0:T(8,128)(2,1)S(1)}, bf16[528,1024]{1,0:T(8,128)(2,1)S(1)}, u32[]{:S(2)}, u32[]{:S(2)}) collective-permute-start(bf16[528,1024]{1,0:T(8,128)(2,1)S(1)} %get-tuple-element.55.refs_5_), channel_id=1, source_target_pairs={{0,1},{1,0},{2,3},{3,2},{4,5},{5,4},{6,7},{7,6},{8,9},{9,8},{10,11... | collective-permute-start | bytes 3244040 | tf_op jit(solution)/shard_map/ppermute | solution.py:32
  10.4 18.5 %collective-permute-start.4 = (bf16[1040,512]{1,0:T(8,128)(2,1)S(1)}, bf16[1040,512]{1,0:T(8,128)(2,1)S(1)}, u32[]{:S(2)}, u32[]{:S(2)}) collective-permute-start(bf16[1040,512]{1,0:T(8,128)(2,1)S(1)} %get-tuple-element.54.refs_0_), channel_id=1, source_target_pairs={{0,12},{1,13},{18,30},{19,31},{36,32},{37,33},{54,50},{55,51},{72,... | collective-permute-start | bytes 3194888 | tf_op jit(solution)/shard_map/ppermute | solution.py:32
  11.3 24.4 %collective-permute-start.5 = (bf16[1040,512]{1,0:T(8,128)(2,1)S(1)}, bf16[1040,512]{1,0:T(8,128)(2,1)S(1)}, u32[]{:S(2)}, u32[]{:S(2)}) collective-permute-start(bf16[1040,512]{1,0:T(8,128)(2,1)S(1)} %get-tuple-element.54.refs_0_), channel_id=1, source_target_pairs={{0,8},{1,9},{18,26},{19,27},{36,44},{37,45},{54,62},{55,63},{72,64... | collective-permute-start | bytes 3194888 | tf_op jit(solution)/shard_map/ppermute | solution.py:32
  18.5 17.2 %collective-permute-start.7 = (bf16[384,1024]{1,0:T(8,128)(2,1)S(1)}, bf16[384,1024]{1,0:T(8,128)(2,1)S(1)}, u32[]{:S(2)}, u32[]{:S(2)}) collective-permute-start(bf16[384,1024]{1,0:T(8,128)(2,1)S(1)} %get-tuple-element.56), channel_id=1, source_target_pairs={{0,48},{1,49},{2,18},{3,19},{4,52},{5,53},{6,22},{7,23},{8,56},{9,... | collective-permute-start | bytes 2359304 | tf_op jit(solution)/shard_map/ppermute | solution.py:32
  27.2 8.5 %collective-permute-start.8 = (bf16[384,1024]{1,0:T(8,128)(2,1)S(1)}, bf16[384,1024]{1,0:T(8,128)(2,1)S(1)}, u32[]{:S(2)}, u32[]{:S(2)}) collective-permute-start(bf16[384,1024]{1,0:T(8,128)(2,1)S(1)} %collective-permute-done.1.refs_1_), channel_id=1, source_target_pairs={{0,2},{1,3},{2,0},{3,1},{4,6},{5,7},{6,4},{7,5},{8,10},{9,11},{10,... | collective-permute-start | bytes 2359304 | tf_op jit(solution)/shard_map/ppermute | solution.py:32
  35.7 4.7 %collective-permute-start.9 = (bf16[384,1024]{1,0:T(8,128)(2,1)S(1)}, bf16[384,1024]{1,0:T(8,128)(2,1)S(1)}, u32[]{:S(2)}, u32[]{:S(2)}) collective-permute-start(bf16[384,1024]{1,0:T(8,128)(2,1)S(1)} %collective-permute-done.7.refs_3_), channel_id=1, source_target_pairs={{0,2},{1,3},{2,0},{3,1},{4,6},{5,7},{6,4},{7,5},{8,10},{9,11},{10,... | collective-permute-start | bytes 2359304 | tf_op jit(solution)/shard_map/ppermute | solution.py:32
  36.9 16.4 %collective-permute-start.10 = (bf16[1040,512]{1,0:T(8,128)(2,1)S(1)}, bf16[1040,512]{1,0:T(8,128)(2,1)S(1)}, u32[]{:S(2)}, u32[]{:S(2)}) collective-permute-start(bf16[1040,512]{1,0:T(8,128)(2,1)S(1)} %shard_map.52.refs_5_), channel_id=1, source_target_pairs={{0,2},{1,3},{2,0},{3,1},{4,6},{5,7},{6,4},{7,5},{8,10},{9,11},{10,... | collective-permute-start | bytes 3194888 | tf_op jit(solution)/shard_map/ppermute | solution.py:32
  37.1 16.1 %collective-permute-start.11 = (bf16[384,1024]{1,0:T(8,128)(2,1)S(1)}, bf16[384,1024]{1,0:T(8,128)(2,1)S(1)}, u32[]{:S(2)}, u32[]{:S(2)}) collective-permute-start(bf16[384,1024]{1,0:T(8,128)(2,1)S(1)} %collective-permute-done.refs_1_), channel_id=1, source_target_pairs={{0,16},{1,17},{2,50},{3,51},{4,20},{5,21},{6,54},{7,55},{8,24},{9,... | collective-permute-start | bytes 2359304 | tf_op jit(solution)/shard_map/ppermute | solution.py:32
  37.7 15.5 %collective-permute-start.2 = (bf16[384,1024]{1,0:T(8,128)(2,1)S(1)}, bf16[384,1024]{1,0:T(8,128)(2,1)S(1)}, u32[]{:S(2)}, u32[]{:S(2)}) collective-permute-start(bf16[384,1024]{1,0:T(8,128)(2,1)S(1)} %collective-permute-done.refs_1_), channel_id=1, source_target_pairs={{0,2},{1,3},{2,0},{3,1},{4,6},{5,7},{6,4},{7,5},{8,10},{9,11},{10,... | collective-permute-start | bytes 2359304 | tf_op jit(solution)/shard_map/ppermute | solution.py:32
  37.7 26.8 %collective-permute-start.12 = (bf16[384,1024]{1,0:T(8,128)(2,1)S(1)}, bf16[384,1024]{1,0:T(8,128)(2,1)S(1)}, u32[]{:S(2)}, u32[]{:S(2)}) collective-permute-start(bf16[384,1024]{1,0:T(8,128)(2,1)S(1)} %collective-permute-done.1.refs_1_), channel_id=1, source_target_pairs={{0,16},{1,17},{2,50},{3,51},{4,20},{5,21},{6,54},{7,55},{8,24},{9,... | collective-permute-start | bytes 2359304 | tf_op jit(solution)/shard_map/ppermute | solution.py:32
  40.4 24.1 %collective-permute-start.13 = (bf16[384,1024]{1,0:T(8,128)(2,1)S(1)}, bf16[384,1024]{1,0:T(8,128)(2,1)S(1)}, u32[]{:S(2)}, u32[]{:S(2)}) collective-permute-start(bf16[384,1024]{1,0:T(8,128)(2,1)S(1)} %collective-permute-done.7.refs_3_), channel_id=1, source_target_pairs={{0,65},{1,64},{2,67},{3,66},{4,69},{5,68},{6,71},{7,70},{8,73},{9,... | collective-permute-start | bytes 2359304 | tf_op jit(solution)/shard_map/ppermute | solution.py:32
  53.2 12.1 %collective-permute-start.16 = (bf16[384,1024]{1,0:T(8,128)(2,1)S(1)}, bf16[384,1024]{1,0:T(8,128)(2,1)S(1)}, u32[]{:S(2)}, u32[]{:S(2)}) collective-permute-start(bf16[384,1024]{1,0:T(8,128)(2,1)S(1)} %collective-permute-done.11.refs_3_), channel_id=1, source_target_pairs={{0,16},{1,17},{2,50},{3,51},{4,20},{5,21},{6,54},{7,55},{8,24},{9,... | collective-permute-start | bytes 2359304 | tf_op jit(solution)/shard_map/ppermute | solution.py:32
  64.6 2.4 %collective-permute-start.14 = (bf16[384,1024]{1,0:T(8,128)(2,1)S(1)}, bf16[384,1024]{1,0:T(8,128)(2,1)S(1)}, u32[]{:S(2)}, u32[]{:S(2)}) collective-permute-start(bf16[384,1024]{1,0:T(8,128)(2,1)S(1)} %collective-permute-done.12.refs_1_), channel_id=1, source_target_pairs={{0,2},{1,3},{2,0},{3,1},{4,6},{5,7},{6,4},{7,5},{8,10},{9,11},{10,... | collective-permute-start | bytes 2359304 | tf_op jit(solution)/shard_map/ppermute | solution.py:32
  64.6 3.4 %collective-permute-start.15 = (bf16[384,1024]{1,0:T(8,128)(2,1)S(1)}, bf16[384,1024]{1,0:T(8,128)(2,1)S(1)}, u32[]{:S(2)}, u32[]{:S(2)}) collective-permute-start(bf16[384,1024]{1,0:T(8,128)(2,1)S(1)} %collective-permute-done.13.refs_5_), channel_id=1, source_target_pairs={{0,2},{1,3},{2,0},{3,1},{4,6},{5,7},{6,4},{7,5},{8,10},{9,11},{10,... | collective-permute-start | bytes 2359304 | tf_op jit(solution)/shard_map/ppermute | solution.py:32
  65.1 4.0 %collective-permute-start.17 = (bf16[384,1024]{1,0:T(8,128)(2,1)S(1)}, bf16[384,1024]{1,0:T(8,128)(2,1)S(1)}, u32[]{:S(2)}, u32[]{:S(2)}) collective-permute-start(bf16[384,1024]{1,0:T(8,128)(2,1)S(1)} %collective-permute-done.11.refs_3_), channel_id=1, source_target_pairs={{0,2},{1,3},{2,0},{3,1},{4,6},{5,7},{6,4},{7,5},{8,10},{9,11},{10,... | collective-permute-start | bytes 2359304 | tf_op jit(solution)/shard_map/ppermute | solution.py:32
  68.0 2.3 %collective-permute-start.18 = (bf16[384,1024]{1,0:T(8,128)(2,1)S(1)}, bf16[384,1024]{1,0:T(8,128)(2,1)S(1)}, u32[]{:S(2)}, u32[]{:S(2)}) collective-permute-start(bf16[384,1024]{1,0:T(8,128)(2,1)S(1)} %collective-permute-done.16.refs_7_), channel_id=1, source_target_pairs={{0,2},{1,3},{2,0},{3,1},{4,6},{5,7},{6,4},{7,5},{8,10},{9,11},{10,... | collective-permute-start | bytes 2359304 | tf_op jit(solution)/shard_map/ppermute | solution.py:32

commit v4 on v3

--- a/solution.py
+++ b/solution.py
@@ -194,56 +194,46 @@
 def opening_kernel(count, valid_rows, ids, *refs):
     refs = list(refs)
     take = lambda n: [refs.pop(0) for _ in range(n)]
-    pieces = [take(1 if k == 0 else 2) for k in range(count)]
-    turned, partner, offsets = take(3)
-    row_proj, row_off, slab, features, parts, proj_sem, in_sem = take(7)
-    rows = row_proj.shape[0]
-    own, slab_rows = rows // 2, slab.shape[1]
+    pieces = [take(2) for _ in range(count)]
+    states, turned, partner, offsets = take(4)
+    row_off, slab, features, in_sem = take(4)
+    slab_rows = states.shape[0]
+    own = turned.shape[0] - SPARE
     core = ids[(valid_rows + LAG) // slab_rows]
-    row_loads = [
-        pltpu.make_async_copy(turned.at[pl.ds(0, own)], row_proj.at[pl.ds(0, own)], proj_sem.at[0]),
-        pltpu.make_async_copy(partner.at[pl.ds(0, own)], row_proj.at[pl.ds(own, own)], proj_sem.at[1]),
-        pltpu.make_async_copy(partner.at[pl.ds(own, SPARE)], parts, proj_sem.at[2]),
-    ]
     loads = [slab_copies(pieces[k], core, slab.at[k], in_sem.at[k]) for k in range(count)]
-    start([*row_loads, *loads[0]])
+    start([copy for load in loads for copy in load])
     row_off[:own] = lane_broadcast(offsets[...])
-    wait(row_loads)
-    start([copy for load in loads[1:] for copy in load])
-    row_off[own:] = lane_broadcast(jnp.sum(parts[:, :own].astype(jnp.float32), axis=0, keepdims=True))
-    tile = slab_rows // TIME_TILES
-    for k in range(count):
-        wait(loads[k])
-        for u in range(TIME_TILES):
-            span = slice(u * tile, (u + 1) * tile)
-            turned_states = slab[k, span].T
-            for part in (slice(0, own), slice(own, rows)):
-                features[k, part, span] = row_features(
-                    row_proj[part], turned_states, row_off[part], ids[k] * slab_rows + u * tile, valid_rows
-                )
-
-
-def opening(slabs, numbers, turned, partner, offsets, slab_rows, valid_rows):
-    rows, units, count = 2 * (turned.shape[0] - SPARE), turned.shape[1], len(slabs)
+    row_off[own:] = lane_broadcast(jnp.sum(partner[own:, :own].astype(jnp.float32), axis=0, keepdims=True))
+    for k in range(count + 1):
+        if k > 0:
+            wait(loads[k - 1])
+        turned_states = (slab[k - 1] if k > 0 else states[...]).T
+        for half, proj in enumerate((turned, partner)):
+            part = slice(half * own, (half + 1) * own)
+            features[k, part] = row_features(
+                proj[:own], turned_states, row_off[part], ids[k] * slab_rows, valid_rows
+            )
+
+
+def opening(slabs, numbers, states, turned, partner, offsets, valid_rows):
+    own, units, count, slab_rows = turned.shape[0] - SPARE, turned.shape[1], len(slabs), states.shape[0]
     pieces = [p for s in slabs for p in s]
-    dma = pltpu.SemaphoreType.DMA
     return pl.pallas_call(
         functools.partial(opening_kernel, count, valid_rows),
-        in_specs=[smem_spec()] + [any_spec()] * (len(pieces) + 2) + [vmem_spec()],
-        out_specs=[vmem_spec()] * 4,
+        in_specs=[smem_spec()] + [any_spec()] * len(pieces) + [vmem_spec()] * 4,
+        out_specs=[vmem_spec()] * 3,
         out_shape=[
-            pltpu.VMEM((rows, units), jnp.bfloat16),
-            pltpu.VMEM((rows, 128), jnp.float32),
+            pltpu.VMEM((2 * own, 128), jnp.float32),
             pltpu.VMEM((count, slab_rows, units), jnp.bfloat16),
-            pltpu.VMEM((count, rows, slab_rows), jnp.bfloat16),
+            pltpu.VMEM((count + 1, 2 * own, slab_rows), jnp.bfloat16),
         ],
-        scratch_shapes=[pltpu.VMEM((SPARE, units), jnp.bfloat16), dma((3,)), dma((count, 2))],
+        scratch_shapes=[pltpu.SemaphoreType.DMA((count, 2))],
         compiler_params=pltpu.CompilerParams(vmem_limit_bytes=12 * MIB),
         cost_estimate=pl.CostEstimate(
-            flops=2 * count * slab_rows * units * rows, bytes_accessed=2 * count * slab_rows * units,
-            transcendentals=count * slab_rows * rows,
+            flops=4 * (count + 1) * slab_rows * units * own, bytes_accessed=2 * count * slab_rows * units,
+            transcendentals=2 * (count + 1) * slab_rows * own,
         ),
-    )(numbers, *pieces, turned, partner, offsets)
+    )(numbers, *pieces, in_vmem(states), in_vmem(turned), in_vmem(partner), offsets)
 
 
 def moments_kernel(count, ready, at, last, slab_rows, valid_rows, *refs):
@@ -254,17 +244,16 @@
     slabs = (valid_rows + LAG) // slab_rows
     pieces = [None] * ready + [take(2) for _ in range(count - ready)]
     if first:
-        ready_slab, ready_rows, *columns, row_proj, row_off = take(6)
-    else:
-        row_proj, row_off, col_proj, row_next, col_next = take(5)
+        own_states, ready_slab, ready_rows, panel, swapped = take(5)
+    turned, partner, row_off = take(3)
+    if last:
+        col_proj, row_next, col_next = take(3)
         take(4)
         acc_out = take(2)
     instant, lagged, tails, heads = take(4)
     if first:
         col_proj, row_next, col_next = take(3)
     slab, turned_states, row_a, row_b, col_a, col_b, in_sem = take(7)
-    if first:
-        (proj_sem,) = take(1)
     if last:
         turned_edges, out_sem = take(2)
     rows, cols = instant.shape
@@ -275,17 +264,17 @@
     number = lambda k: ids[at + k]
 
     loads = [[] if k < ready else slab_copies(pieces[k], core, slab.at[k - ready], in_sem.at[k - ready]) for k in range(count)]
-    states = lambda k: ready_slab.at[k] if k < ready else slab.at[k - ready]
+    states = lambda k: slab.at[k - ready] if k >= ready else own_states if k == 0 else ready_slab.at[k - 1]
+    row_proj = lambda h: (turned, partner)[h][:rows // 2]
     between = count - 1 if first else 0
     row_bufs = lambda k: row_next if k == between else (row_a, row_b)[k % 2]
     col_bufs = lambda k: col_next if k == between else (col_a, col_b)[k % 2]
-    col_loads = [OneOf(source, columns, col_proj, proj_sem)] if first else []
 
     def keep_borders(k):
         tails[number(k)] = states(k)[slab_rows - LAG:]
         heads[lax.rem(number(k) + slabs - 1, slabs)] = states(k)[:LAG]
 
-    start([*col_loads, *loads[ready]])
+    start(loads[ready])
 
     for buf in (col_a, col_b) + ((col_next,) if first else ()):
         buf[slab_rows:] = jnp.zeros_like(buf[slab_rows:])
@@ -297,7 +286,7 @@
         if h == 0:
             turned_states[...] = states(k)[span].T
         row_bufs(k)[part, span] = row_features(
-            row_proj[part], turned_states[...], row_off[part], number(k) * slab_rows + u * time_tile, valid_rows
+            row_proj(h), turned_states[...], row_off[part], number(k) * slab_rows + u * time_tile, valid_rows
         )
 
     def col_off(span):
@@ -312,7 +301,7 @@
         if h == 0:
             turned_edges[...] = tails[...].reshape(size, units).T
         row_bufs(count)[part, :size] = row_features(
-            row_proj[part], turned_edges[...], row_off[part], 0, (slabs - 1) * LAG
+            row_proj(h), turned_edges[...], row_off[part], 0, (slabs - 1) * LAG
         )
 
     def edge_cols(n):
@@ -366,7 +355,7 @@
             ])
 
     if first:
-        wait(col_loads)
+        col_proj[...] = jnp.where(source == 0, panel[...], swapped[...])
         for step in feature_steps(0):
             step()
         for k in range(ready):
@@ -395,12 +384,12 @@
         wait(stores[0] + stores[1])
 
 
-def moments(slabs, at, numbers, opened, panels, carry, slab_rows, valid_rows):
+def moments(slabs, at, numbers, states, opened, columns, panels, carry, slab_rows, valid_rows):
     first, last = carry is None, carry is not None
     units = slabs[0][0].shape[1]
-    cols = panels[0].shape[1] if first else carry[0].shape[1]
+    cols = panels[0].shape[0] - SPARE
     rows, borders = 2 * cols, valid_rows // slab_rows + 1
-    ready = opened[0].shape[0] if first else 1
+    ready = opened[0].shape[0] + 1 if first else 1
     count = ready + len(slabs)
     pieces = [p for s in slabs for p in s]
     end_shape = (rows, 1, cols)
@@ -419,20 +408,19 @@
     specs = [smem_spec()] + [any_spec()] * len(pieces)
     aliases = {}
     if first:
-        args += [*map(in_vmem, opened), *panels[:2], *map(in_vmem, panels[2:])]
-        specs += [vmem_spec()] * 2 + [any_spec()] * 2 + [vmem_spec()] * 2
+        args += [in_vmem(x) for x in (states, *opened, *columns, *panels)]
+        specs += [vmem_spec()] * 8
         outs = outs + [
             pltpu.VMEM((units + SPARE, cols), jnp.bfloat16),
             pltpu.VMEM((rows, slab_rows), jnp.bfloat16),
             pltpu.VMEM((slab_rows + LAG, cols), jnp.bfloat16),
         ]
         out_specs = [vmem_spec()] * 7
-        scratch.append(dma)
     else:
         outs, out_specs = [pltpu.HBM(end_shape, jnp.float32)] * 2 + outs, [hbm_spec()] * 2 + [vmem_spec()] * 4
         scratch += [pltpu.VMEM((units, borders * LAG), jnp.bfloat16), dma((2, 4))]
         args += [in_vmem(x) for x in (*panels, *carry[4:], *carry[:4])]
-        specs += [vmem_spec()] * 9
+        specs += [vmem_spec()] * 10
         aliases = {len(args) - 4 + n: 2 + n for n in range(4)}
     return pl.pallas_call(
         functools.partial(moments_kernel, count, ready, at, last, slab_rows, valid_rows),
@@ -486,19 +474,20 @@
     panel = pick(after + 3, numbers, columns, ahead, beyond, behind)
     swapped = swap(panel)
     swapped_back, swapped_over = swap(y_back), swap(over)
-    slabs = [(in_hbm(states),), (y_out, swapped_back), (y_back, swapped_out)]
-    row_proj, row_off, *opened = opening(slabs, numbers, turned, partner, line, *sizes)
+    slabs = [(y_out, swapped_back), (y_back, swapped_out)]
+    row_off, *opened = opening(slabs, numbers, states, turned, partner, line, valid_rows)
 
     over_out, y_far, over_back = move(over, out_y), move(y_out, out_y), move(y_back, crossing)
     row_off, over_out = lax.optimization_barrier((row_off, over_out))
     over_far = move(over_out, out_y)
-    carry = moments([(over, swapped_over)], 0, numbers, opened, (panel, swapped, row_proj, row_off), None, *sizes)
+    panels = (turned, partner, row_off)
+    carry = moments([(over, swapped_over)], 0, numbers, states, opened, (panel, swapped), panels, None, *sizes)
 
     *carry, y_far, over_back = lax.optimization_barrier((*carry, y_far, over_back))
     swapped_far, swapped_over_back = swap(y_far), swap(over_back)
     swapped_far, swapped_over_back, over_far = lax.optimization_barrier((swapped_far, swapped_over_back, over_far))
     slabs = [(y_far, swapped_far), (over_out, swapped_over_back), (over_back, swap(over_out)), (over_far, swap(over_far))]
-    instant, lagged, *_ = moments(slabs, 3, numbers, None, (row_proj, row_off), carry, *sizes)
+    instant, lagged, *_ = moments(slabs, 3, numbers, None, None, None, panels, carry, *sizes)
     return instant, lagged
 
 

time: 95.8 us -> 95.9 us (level)
  Pallas kernels: 46.3 us -> 44.6 us
  starting transfers between devices: 24 us -> 25.1 us
    pallas_call x1, Pallas kernels: 7.81 us -> 6.39 us  [opening(): pl.pallas_call(functools.partial(opening_kernel, count, valid_rows), in_s...]
    ppermute x19, starting transfers between devices: 24 us -> 25.1 us  [move(): return lax.ppermute(block, AXES, route(target))]
  transfers between devices with their start and end apart: 19 -> 19, of which waited for: 7 -> 8; matrix products, arithmetic and copies ran while one was open for 0% -> 0% of each run, Pallas kernels for 21% -> 19%
where the time goes in v4:
time: 95.9 us; the launch traced here: 94.1 us
  Pallas kernels  44.6 us (47%)
  starting transfers between devices  25.1 us (26%)
  waiting for transfers between devices  23.2 us (24%)
  between operations  1.11 us (1%)
    pallas_call x2, Pallas kernels, moments(): pl.pallas_call(functools.partial(moments_kernel, count, ready, at, last,...  35.4 us
    ppermute x19, starting transfers between devices, move(): return lax.ppermute(block, AXES, route(target))  25.1 us
    ppermute x19, waiting for transfers between devices, move(): return lax.ppermute(block, AXES, route(target))  23.2 us
    pallas_call x1, Pallas kernels, opening(): pl.pallas_call(functools.partial(opening_kernel, count, valid_rows), in_s...  6.39 us
    pallas_call x1, Pallas kernels, prepare(): pl.pallas_call(functools.partial(prepare_kernel, at), in_specs=[smem_spec...  2.14 us
  transfers between devices with their start and end apart: 19, of which 8 were waited for; matrix products, arithmetic and copies ran while one was open for 0% of the time, Pallas kernels for 19%

profile of v4, /device:TPU:1, one launch (start us, length us, event | category | flops | bytes accessed | tf_op | source)
XLA Modules:
  0.0 94.1 jit_solution(11428245220380261684)
XLA Ops:
  0.8 0.1 stack.51.numbers.ids.refs_0_
  0.9 2.1 %shard_map.50 = (bf16[1040,512]{1,0:T(8,128)(2,1)S(1)}, bf16[528,1024]{1,0:T(8,128)(2,1)S(1)}, bf16[384,1024]{1,0:T(8,128)(2,1)S(1)}) custom-call(s32[12]{0:T(128)S(1)} %stack.51.numbers.ids.refs_0_, bf16[1024,512]{1,0:T(8,128)(2,1)} %projection.1, f32[1,512]{1,0:T(1,128)} %bitcast.13, bf16[768,1024]{1,0:T(8,128)(2,1)} %refs_3_.1), custom_call_target="tpu_custom_call" | custom-call | tf_op jit(solution)/shard_map/pallas_call | solution.py:138
  3.0 0.7 collective-permute-start.3
  3.7 3.6 %collective-permute-start.1 = (bf16[384,1024]{1,0:T(8,128)(2,1)S(1)}, bf16[384,1024]{1,0:T(8,128)(2,1)S(1)}, u32[]{:S(2)}, u32[]{:S(2)}) collective-permute-start(bf16[384,1024]{1,0:T(8,128)(2,1)S(1)} %get-tuple-element.55), channel_id=1, source_target_pairs={{0,16},{1,17},{2,50},{3,51},{4,20},{5,21},{6,54},{7,55},{8,24},{9,... | collective-permute-start | bytes 2359304 | tf_op jit(solution)/shard_map/ppermute | solution.py:32
  7.4 3.0 %collective-permute-start = (bf16[384,1024]{1,0:T(8,128)(2,1)S(1)}, bf16[384,1024]{1,0:T(8,128)(2,1)S(1)}, u32[]{:S(2)}, u32[]{:S(2)}) collective-permute-start(bf16[384,1024]{1,0:T(8,128)(2,1)S(1)} %get-tuple-element.55), channel_id=1, source_target_pairs={{0,65},{1,64},{2,67},{3,66},{4,69},{5,68},{6,71},{7,70},{8,73},{9,... | collective-permute-start | bytes 2359304 | tf_op jit(solution)/shard_map/ppermute | solution.py:32
  10.4 0.0 copy-start
  10.4 0.0 copy-start.1
  10.4 0.0 collective-permute-start.6
  10.4 0.8 collective-permute-start.4
  11.3 0.0 collective-permute-done.3.refs_1_
  11.3 0.7 collective-permute-start.5
  12.0 6.5 %collective-permute-done.1.refs_0_ = bf16[384,1024]{1,0:T(8,128)(2,1)S(1)} collective-permute-done((bf16[384,1024]{1,0:T(8,128)(2,1)S(1)}, bf16[384,1024]{1,0:T(8,128)(2,1)S(1)}, u32[]{:S(2)}, u32[]{:S(2)}) %collective-permute-start.1) | collective-permute-done | bytes 786464 | tf_op jit(solution)/shard_map/ppermute | solution.py:32
  18.5 3.5 %collective-permute-start.7 = (bf16[384,1024]{1,0:T(8,128)(2,1)S(1)}, bf16[384,1024]{1,0:T(8,128)(2,1)S(1)}, u32[]{:S(2)}, u32[]{:S(2)}) collective-permute-start(bf16[384,1024]{1,0:T(8,128)(2,1)S(1)} %get-tuple-element.55), channel_id=1, source_target_pairs={{0,48},{1,49},{2,18},{3,19},{4,52},{5,53},{6,22},{7,23},{8,56},{9,... | collective-permute-start | bytes 2359304 | tf_op jit(solution)/shard_map/ppermute | solution.py:32
  22.0 5.2 %collective-permute-done.refs_1_ = bf16[384,1024]{1,0:T(8,128)(2,1)S(1)} collective-permute-done((bf16[384,1024]{1,0:T(8,128)(2,1)S(1)}, bf16[384,1024]{1,0:T(8,128)(2,1)S(1)}, u32[]{:S(2)}, u32[]{:S(2)}) %collective-permute-start) | collective-permute-done | bytes 786464 | tf_op jit(solution)/shard_map/ppermute | solution.py:32
  27.2 1.7 %collective-permute-start.8 = (bf16[384,1024]{1,0:T(8,128)(2,1)S(1)}, bf16[384,1024]{1,0:T(8,128)(2,1)S(1)}, u32[]{:S(2)}, u32[]{:S(2)}) collective-permute-start(bf16[384,1024]{1,0:T(8,128)(2,1)S(1)} %collective-permute-done.1.refs_0_), channel_id=1, source_target_pairs={{0,2},{1,3},{2,0},{3,1},{4,6},{5,7},{6,4},{7,5},{8,10},{9,11},{10,... | collective-permute-start | bytes 2359304 | tf_op jit(solution)/shard_map/ppermute | solution.py:32
  28.9 0.0 collective-permute-done.4.refs_3_
  28.9 6.8 %collective-permute-done.6.refs_6_.refs_9_.refs_10_ = bf16[528,1024]{1,0:T(8,128)(2,1)S(1)} collective-permute-done((bf16[528,1024]{1,0:T(8,128)(2,1)S(1)}, bf16[528,1024]{1,0:T(8,128)(2,1)S(1)}, u32[]{:S(2)}, u32[]{:S(2)}) %collective-permute-start.6) | collective-permute-done | bytes 1081376 | tf_op jit(solution)/shard_map/ppermute | solution.py:32
  35.7 0.0 collective-permute-done.7.refs_2_
  35.7 0.0 collective-permute-done.8.refs_3_
  35.7 0.0 collective-permute-done.5.refs_2_
  35.7 0.5 collective-permute-start.9
  36.2 0.7 shard_map.52.refs_6_
  36.9 0.2 collective-permute-start.10
  37.1 0.7 collective-permute-start.11
  37.7 0.0 collective-permute-start.2
  37.7 2.7 %collective-permute-start.12 = (bf16[384,1024]{1,0:T(8,128)(2,1)S(1)}, bf16[384,1024]{1,0:T(8,128)(2,1)S(1)}, u32[]{:S(2)}, u32[]{:S(2)}) collective-permute-start(bf16[384,1024]{1,0:T(8,128)(2,1)S(1)} %collective-permute-done.1.refs_0_), channel_id=1, source_target_pairs={{0,16},{1,17},{2,50},{3,51},{4,20},{5,21},{6,54},{7,55},{8,24},{9,... | collective-permute-start | bytes 2359304 | tf_op jit(solution)/shard_map/ppermute | solution.py:32
  40.4 0.0 collective-permute-done.9.refs_1_
  40.4 4.9 %collective-permute-start.13 = (bf16[384,1024]{1,0:T(8,128)(2,1)S(1)}, bf16[384,1024]{1,0:T(8,128)(2,1)S(1)}, u32[]{:S(2)}, u32[]{:S(2)}) collective-permute-start(bf16[384,1024]{1,0:T(8,128)(2,1)S(1)} %collective-permute-done.7.refs_2_), channel_id=1, source_target_pairs={{0,65},{1,64},{2,67},{3,66},{4,69},{5,68},{6,71},{7,70},{8,73},{9,... | collective-permute-start | bytes 2359304 | tf_op jit(solution)/shard_map/ppermute | solution.py:32
  45.3 0.0 copy-done
  45.3 0.0 copy-done.1
  45.3 6.4 %shard_map.51 = (f32[1024,128]{1,0:T(8,128)S(1)}, bf16[2,768,1024]{2,1,0:T(8,128)(2,1)S(1)}, bf16[3,1024,768]{2,1,0:T(8,128)(2,1)S(1)}) custom-call(s32[12]{0:T(128)S(1)} %stack.51.numbers.ids.refs_0_, bf16[384,1024]{1,0:T(8,128)(2,1)S(1)} %collective-permute-done.1.refs_0_, bf16[384,1024]{1,0:T(8,128)(2,1)S(1)} %collective-permute-done.9.refs_1_, ...), custom_call_target="tpu_custom_call" | custom-call | flops 4831838208 | bytes 3145728 | tf_op jit(solution)/shard_map/pallas_call | solution.py:221
  51.7 0.0 collective-permute-done.11.refs_3_
  51.7 0.3 collective-permute-start.16
  52.0 0.0 collective-permute-done.2.refs_2_
  52.0 0.0 collective-permute-done.10.refs_7_
  52.0 10.9 %shard_map.53 = (f32[1024,512]{1,0:T(8,128)S(1)}, f32[1024,512]{1,0:T(8,128)S(1)}, bf16[8,64,1024]{2,1,0:T(8,128)(2,1)S(1)}, bf16[8,64,1024]{2,1,0:T(8,128)(2,1)...) custom-call(s32[12]{0:T(128)S(1)} %stack.51.numbers.ids.refs_0_, ...), custom_call_target="tpu_custom_call" | custom-call | flops 16106127360 | bytes 6291456 | tf_op jit(solution)/shard_map/pallas_call | solution.py:425
  62.9 0.0 collective-permute-done.12.refs_1_
  63.0 0.0 collective-permute-done.13.refs_5_
  63.0 0.1 collective-permute-start.14
  63.1 0.5 collective-permute-start.15
  63.6 0.1 collective-permute-start.17
  63.7 1.4 %collective-permute-done.16.refs_7_ = bf16[384,1024]{1,0:T(8,128)(2,1)S(1)} collective-permute-done((bf16[384,1024]{1,0:T(8,128)(2,1)S(1)}, bf16[384,1024]{1,0:T(8,128)(2,1)S(1)}, u32[]{:S(2)}, u32[]{:S(2)}) %collective-permute-start.16) | collective-permute-done | bytes 786464 | tf_op jit(solution)/shard_map/ppermute | solution.py:32
  65.1 0.3 collective-permute-done.14.refs_2_
  65.3 1.1 %collective-permute-done.15.refs_4_ = bf16[384,1024]{1,0:T(8,128)(2,1)S(1)} collective-permute-done((bf16[384,1024]{1,0:T(8,128)(2,1)S(1)}, bf16[384,1024]{1,0:T(8,128)(2,1)S(1)}, u32[]{:S(2)}, u32[]{:S(2)}) %collective-permute-start.15) | collective-permute-done | bytes 786464 | tf_op jit(solution)/shard_map/ppermute | solution.py:32
  66.5 1.1 %collective-permute-start.18 = (bf16[384,1024]{1,0:T(8,128)(2,1)S(1)}, bf16[384,1024]{1,0:T(8,128)(2,1)S(1)}, u32[]{:S(2)}, u32[]{:S(2)}) collective-permute-start(bf16[384,1024]{1,0:T(8,128)(2,1)S(1)} %collective-permute-done.16.refs_7_), channel_id=1, source_target_pairs={{0,2},{1,3},{2,0},{3,1},{4,6},{5,7},{6,4},{7,5},{8,10},{9,11},{10,... | collective-permute-start | bytes 2359304 | tf_op jit(solution)/shard_map/ppermute | solution.py:32
  67.5 0.1 collective-permute-done.17.refs_6_
  67.6 1.8 %collective-permute-done.18.refs_8_ = bf16[384,1024]{1,0:T(8,128)(2,1)S(1)} collective-permute-done((bf16[384,1024]{1,0:T(8,128)(2,1)S(1)}, bf16[384,1024]{1,0:T(8,128)(2,1)S(1)}, u32[]{:S(2)}, u32[]{:S(2)}) %collective-permute-start.18) | collective-permute-done | bytes 786464 | tf_op jit(solution)/shard_map/ppermute | solution.py:32
  69.4 24.5 %shard_map.54 = (f32[1024,1,512]{2,1,0:T(1,128)}, f32[1024,1,512]{2,1,0:T(1,128)}, f32[1024,512]{1,0:T(8,128)S(1)}, f32[1024,512]{1,0:T(8,128)S(1)}, bf16[8,64,1...) custom-call(s32[12]{0:T(128)S(1)} %stack.51.numbers.ids.refs_0_, ...), custom_call_target="tpu_custom_call", output_to_operand_aliasing={{2}: (15, {}), {3}: (16, {}), {4}: (17, {}), {5}: (18, {})} | custom-call | flops 20132659200 | bytes 7864320 | tf_op jit(solution)/shard_map/pallas_call | solution.py:425
Async XLA Ops:
  3.0 8.3 %collective-permute-start.3 = (bf16[1040,512]{1,0:T(8,128)(2,1)S(1)}, bf16[1040,512]{1,0:T(8,128)(2,1)S(1)}, u32[]{:S(2)}, u32[]{:S(2)}) collective-permute-start(bf16[1040,512]{1,0:T(8,128)(2,1)S(1)} %get-tuple-element.53.refs_0_), channel_id=1, source_target_pairs={{0,4},{1,5},{18,22},{19,23},{36,40},{37,41},{54,58},{55,59},{72,76... | collective-permute-start | bytes 3194888 | tf_op jit(solution)/shard_map/ppermute | solution.py:32
  3.7 14.8 %collective-permute-start.1 = (bf16[384,1024]{1,0:T(8,128)(2,1)S(1)}, bf16[384,1024]{1,0:T(8,128)(2,1)S(1)}, u32[]{:S(2)}, u32[]{:S(2)}) collective-permute-start(bf16[384,1024]{1,0:T(8,128)(2,1)S(1)} %get-tuple-element.55), channel_id=1, source_target_pairs={{0,16},{1,17},{2,50},{3,51},{4,20},{5,21},{6,54},{7,55},{8,24},{9,... | collective-permute-start | bytes 2359304 | tf_op jit(solution)/shard_map/ppermute | solution.py:32
  7.4 19.8 %collective-permute-start = (bf16[384,1024]{1,0:T(8,128)(2,1)S(1)}, bf16[384,1024]{1,0:T(8,128)(2,1)S(1)}, u32[]{:S(2)}, u32[]{:S(2)}) collective-permute-start(bf16[384,1024]{1,0:T(8,128)(2,1)S(1)} %get-tuple-element.55), channel_id=1, source_target_pairs={{0,65},{1,64},{2,67},{3,66},{4,69},{5,68},{6,71},{7,70},{8,73},{9,... | collective-permute-start | bytes 2359304 | tf_op jit(solution)/shard_map/ppermute | solution.py:32
  10.4 34.9 %copy-start = (bf16[768,1024]{1,0:T(8,128)(2,1)S(1)}, bf16[768,1024]{1,0:T(8,128)(2,1)}, u32[]{:S(2)}) copy-start(bf16[768,1024]{1,0:T(8,128)(2,1)} %refs_3_.1) | copy-start | bytes 4718596
  10.4 34.9 %copy-start.1 = (f32[512]{0:T(512)S(1)}, f32[512]{0:T(512)}, u32[]{:S(2)}) copy-start(f32[512]{0:T(512)} %param.5) | copy-start | bytes 6148
  10.4 25.3 %collective-permute-start.6 = (bf16[528,1024]{1,0:T(8,128)(2,1)S(1)}, bf16[528,1024]{1,0:T(8,128)(2,1)S(1)}, u32[]{:S(2)}, u32[]{:S(2)}) collective-permute-start(bf16[528,1024]{1,0:T(8,128)(2,1)S(1)} %get-tuple-element.54.refs_5_.refs_8_.refs_9_), channel_id=1, source_target_pairs={{0,1},{1,0},{2,3},{3,2},{4,5},{5,4},{6,7},{7,6},{8,9},{9,8},{10,11... | collective-permute-start | bytes 3244040 | tf_op jit(solution)/shard_map/ppermute | solution.py:32
  10.4 18.5 %collective-permute-start.4 = (bf16[1040,512]{1,0:T(8,128)(2,1)S(1)}, bf16[1040,512]{1,0:T(8,128)(2,1)S(1)}, u32[]{:S(2)}, u32[]{:S(2)}) collective-permute-start(bf16[1040,512]{1,0:T(8,128)(2,1)S(1)} %get-tuple-element.53.refs_0_), channel_id=1, source_target_pairs={{0,12},{1,13},{18,30},{19,31},{36,32},{37,33},{54,50},{55,51},{72,... | collective-permute-start | bytes 3194888 | tf_op jit(solution)/shard_map/ppermute | solution.py:32
  11.3 24.4 %collective-permute-start.5 = (bf16[1040,512]{1,0:T(8,128)(2,1)S(1)}, bf16[1040,512]{1,0:T(8,128)(2,1)S(1)}, u32[]{:S(2)}, u32[]{:S(2)}) collective-permute-start(bf16[1040,512]{1,0:T(8,128)(2,1)S(1)} %get-tuple-element.53.refs_0_), channel_id=1, source_target_pairs={{0,8},{1,9},{18,26},{19,27},{36,44},{37,45},{54,62},{55,63},{72,64... | collective-permute-start | bytes 3194888 | tf_op jit(solution)/shard_map/ppermute | solution.py:32
  18.5 17.2 %collective-permute-start.7 = (bf16[384,1024]{1,0:T(8,128)(2,1)S(1)}, bf16[384,1024]{1,0:T(8,128)(2,1)S(1)}, u32[]{:S(2)}, u32[]{:S(2)}) collective-permute-start(bf16[384,1024]{1,0:T(8,128)(2,1)S(1)} %get-tuple-element.55), channel_id=1, source_target_pairs={{0,48},{1,49},{2,18},{3,19},{4,52},{5,53},{6,22},{7,23},{8,56},{9,... | collective-permute-start | bytes 2359304 | tf_op jit(solution)/shard_map/ppermute | solution.py:32
  27.2 8.5 %collective-permute-start.8 = (bf16[384,1024]{1,0:T(8,128)(2,1)S(1)}, bf16[384,1024]{1,0:T(8,128)(2,1)S(1)}, u32[]{:S(2)}, u32[]{:S(2)}) collective-permute-start(bf16[384,1024]{1,0:T(8,128)(2,1)S(1)} %collective-permute-done.1.refs_0_), channel_id=1, source_target_pairs={{0,2},{1,3},{2,0},{3,1},{4,6},{5,7},{6,4},{7,5},{8,10},{9,11},{10,... | collective-permute-start | bytes 2359304 | tf_op jit(solution)/shard_map/ppermute | solution.py:32
  35.7 4.7 %collective-permute-start.9 = (bf16[384,1024]{1,0:T(8,128)(2,1)S(1)}, bf16[384,1024]{1,0:T(8,128)(2,1)S(1)}, u32[]{:S(2)}, u32[]{:S(2)}) collective-permute-start(bf16[384,1024]{1,0:T(8,128)(2,1)S(1)} %collective-permute-done.7.refs_2_), channel_id=1, source_target_pairs={{0,2},{1,3},{2,0},{3,1},{4,6},{5,7},{6,4},{7,5},{8,10},{9,11},{10,... | collective-permute-start | bytes 2359304 | tf_op jit(solution)/shard_map/ppermute | solution.py:32
  36.9 15.2 %collective-permute-start.10 = (bf16[1040,512]{1,0:T(8,128)(2,1)S(1)}, bf16[1040,512]{1,0:T(8,128)(2,1)S(1)}, u32[]{:S(2)}, u32[]{:S(2)}) collective-permute-start(bf16[1040,512]{1,0:T(8,128)(2,1)S(1)} %shard_map.52.refs_6_), channel_id=1, source_target_pairs={{0,2},{1,3},{2,0},{3,1},{4,6},{5,7},{6,4},{7,5},{8,10},{9,11},{10,... | collective-permute-start | bytes 3194888 | tf_op jit(solution)/shard_map/ppermute | solution.py:32
  37.1 14.7 %collective-permute-start.11 = (bf16[384,1024]{1,0:T(8,128)(2,1)S(1)}, bf16[384,1024]{1,0:T(8,128)(2,1)S(1)}, u32[]{:S(2)}, u32[]{:S(2)}) collective-permute-start(bf16[384,1024]{1,0:T(8,128)(2,1)S(1)} %collective-permute-done.refs_1_), channel_id=1, source_target_pairs={{0,16},{1,17},{2,50},{3,51},{4,20},{5,21},{6,54},{7,55},{8,24},{9,... | collective-permute-start | bytes 2359304 | tf_op jit(solution)/shard_map/ppermute | solution.py:32
  37.7 14.3 %collective-permute-start.2 = (bf16[384,1024]{1,0:T(8,128)(2,1)S(1)}, bf16[384,1024]{1,0:T(8,128)(2,1)S(1)}, u32[]{:S(2)}, u32[]{:S(2)}) collective-permute-start(bf16[384,1024]{1,0:T(8,128)(2,1)S(1)} %collective-permute-done.refs_1_), channel_id=1, source_target_pairs={{0,2},{1,3},{2,0},{3,1},{4,6},{5,7},{6,4},{7,5},{8,10},{9,11},{10,... | collective-permute-start | bytes 2359304 | tf_op jit(solution)/shard_map/ppermute | solution.py:32
  37.7 25.2 %collective-permute-start.12 = (bf16[384,1024]{1,0:T(8,128)(2,1)S(1)}, bf16[384,1024]{1,0:T(8,128)(2,1)S(1)}, u32[]{:S(2)}, u32[]{:S(2)}) collective-permute-start(bf16[384,1024]{1,0:T(8,128)(2,1)S(1)} %collective-permute-done.1.refs_0_), channel_id=1, source_target_pairs={{0,16},{1,17},{2,50},{3,51},{4,20},{5,21},{6,54},{7,55},{8,24},{9,... | collective-permute-start | bytes 2359304 | tf_op jit(solution)/shard_map/ppermute | solution.py:32
  40.4 22.6 %collective-permute-start.13 = (bf16[384,1024]{1,0:T(8,128)(2,1)S(1)}, bf16[384,1024]{1,0:T(8,128)(2,1)S(1)}, u32[]{:S(2)}, u32[]{:S(2)}) collective-permute-start(bf16[384,1024]{1,0:T(8,128)(2,1)S(1)} %collective-permute-done.7.refs_2_), channel_id=1, source_target_pairs={{0,65},{1,64},{2,67},{3,66},{4,69},{5,68},{6,71},{7,70},{8,73},{9,... | collective-permute-start | bytes 2359304 | tf_op jit(solution)/shard_map/ppermute | solution.py:32
  51.7 13.3 %collective-permute-start.16 = (bf16[384,1024]{1,0:T(8,128)(2,1)S(1)}, bf16[384,1024]{1,0:T(8,128)(2,1)S(1)}, u32[]{:S(2)}, u32[]{:S(2)}) collective-permute-start(bf16[384,1024]{1,0:T(8,128)(2,1)S(1)} %collective-permute-done.11.refs_3_), channel_id=1, source_target_pairs={{0,16},{1,17},{2,50},{3,51},{4,20},{5,21},{6,54},{7,55},{8,24},{9,... | collective-permute-start | bytes 2359304 | tf_op jit(solution)/shard_map/ppermute | solution.py:32
  63.0 2.4 %collective-permute-start.14 = (bf16[384,1024]{1,0:T(8,128)(2,1)S(1)}, bf16[384,1024]{1,0:T(8,128)(2,1)S(1)}, u32[]{:S(2)}, u32[]{:S(2)}) collective-permute-start(bf16[384,1024]{1,0:T(8,128)(2,1)S(1)} %collective-permute-done.12.refs_1_), channel_id=1, source_target_pairs={{0,2},{1,3},{2,0},{3,1},{4,6},{5,7},{6,4},{7,5},{8,10},{9,11},{10,... | collective-permute-start | bytes 2359304 | tf_op jit(solution)/shard_map/ppermute | solution.py:32
  63.1 3.4 %collective-permute-start.15 = (bf16[384,1024]{1,0:T(8,128)(2,1)S(1)}, bf16[384,1024]{1,0:T(8,128)(2,1)S(1)}, u32[]{:S(2)}, u32[]{:S(2)}) collective-permute-start(bf16[384,1024]{1,0:T(8,128)(2,1)S(1)} %collective-permute-done.13.refs_5_), channel_id=1, source_target_pairs={{0,2},{1,3},{2,0},{3,1},{4,6},{5,7},{6,4},{7,5},{8,10},{9,11},{10,... | collective-permute-start | bytes 2359304 | tf_op jit(solution)/shard_map/ppermute | solution.py:32
  63.6 4.0 %collective-permute-start.17 = (bf16[384,1024]{1,0:T(8,128)(2,1)S(1)}, bf16[384,1024]{1,0:T(8,128)(2,1)S(1)}, u32[]{:S(2)}, u32[]{:S(2)}) collective-permute-start(bf16[384,1024]{1,0:T(8,128)(2,1)S(1)} %collective-permute-done.11.refs_3_), channel_id=1, source_target_pairs={{0,2},{1,3},{2,0},{3,1},{4,6},{5,7},{6,4},{7,5},{8,10},{9,11},{10,... | collective-permute-start | bytes 2359304 | tf_op jit(solution)/shard_map/ppermute | solution.py:32
  66.5 3.0 %collective-permute-start.18 = (bf16[384,1024]{1,0:T(8,128)(2,1)S(1)}, bf16[384,1024]{1,0:T(8,128)(2,1)S(1)}, u32[]{:S(2)}, u32[]{:S(2)}) collective-permute-start(bf16[384,1024]{1,0:T(8,128)(2,1)S(1)} %collective-permute-done.16.refs_7_), channel_id=1, source_target_pairs={{0,2},{1,3},{2,0},{3,1},{4,6},{5,7},{6,4},{7,5},{8,10},{9,11},{10,... | collective-permute-start | bytes 2359304 | tf_op jit(solution)/shard_map/ppermute | solution.py:32

commit v5 on v4

--- a/solution.py
+++ b/solution.py
@@ -465,20 +465,19 @@
     beyond = move(columns, along_z(2))
     y_out, mine = lax.optimization_barrier((y_out, mine))
     y_back = move(mine, back_y)
-    over, y_out = lax.optimization_barrier((over, y_out))
-    swapped_out = swap(y_out)
-    ahead, behind, beyond, partner, y_back, swapped_out = lax.optimization_barrier(
-        (ahead, behind, beyond, partner, y_back, swapped_out)
+    over_out = move(over, out_y)
+    ahead, behind, beyond, partner, y_out, y_back, over_out = lax.optimization_barrier(
+        (ahead, behind, beyond, partner, y_out, y_back, over_out)
     )
 
     panel = pick(after + 3, numbers, columns, ahead, beyond, behind)
     swapped = swap(panel)
-    swapped_back, swapped_over = swap(y_back), swap(over)
+    swapped_out, swapped_back, swapped_over = swap(y_out), swap(y_back), swap(over)
     slabs = [(y_out, swapped_back), (y_back, swapped_out)]
     row_off, *opened = opening(slabs, numbers, states, turned, partner, line, valid_rows)
-
-    over_out, y_far, over_back = move(over, out_y), move(y_out, out_y), move(y_back, crossing)
-    row_off, over_out = lax.optimization_barrier((row_off, over_out))
+    row_off, swapped_over_out = lax.optimization_barrier((row_off, swap(over_out)))
+
+    y_far, over_back = move(y_out, out_y), move(y_back, crossing)
     over_far = move(over_out, out_y)
     panels = (turned, partner, row_off)
     carry = moments([(over, swapped_over)], 0, numbers, states, opened, (panel, swapped), panels, None, *sizes)
@@ -486,7 +485,7 @@
     *carry, y_far, over_back = lax.optimization_barrier((*carry, y_far, over_back))
     swapped_far, swapped_over_back = swap(y_far), swap(over_back)
     swapped_far, swapped_over_back, over_far = lax.optimization_barrier((swapped_far, swapped_over_back, over_far))
-    slabs = [(y_far, swapped_far), (over_out, swapped_over_back), (over_back, swap(over_out)), (over_far, swap(over_far))]
+    slabs = [(y_far, swapped_far), (over_out, swapped_over_back), (over_back, swapped_over_out), (over_far, swap(over_far))]
     instant, lagged, *_ = moments(slabs, 3, numbers, None, None, None, panels, carry, *sizes)
     return instant, lagged
 

time: 95.9 us -> 99.5 us (1.038); the launches traced: 94.1 us -> 99.4 us
  waiting for transfers between devices: 23.2 us -> 31.9 us
  starting transfers between devices: 25.1 us -> 21.8 us
    ppermute x19, waiting for transfers between devices: 23.2 us -> 31.9 us  [move(): return lax.ppermute(block, AXES, route(target))]
    ppermute x19, starting transfers between devices: 25.1 us -> 21.8 us  [move(): return lax.ppermute(block, AXES, route(target))]
  transfers between devices with their start and end apart: 19 -> 19, of which waited for: 8 -> 9; matrix products, arithmetic and copies ran while one was open for 0% -> 0% of each run, Pallas kernels for 19% -> 18%
where the time goes in v5:
time: 99.5 us; the launch traced here: 99.4 us
  Pallas kernels  44.5 us (45%)
  waiting for transfers between devices  31.9 us (32%)
  starting transfers between devices  21.8 us (22%)
  between operations  1.08 us (1%)
    pallas_call x2, Pallas kernels, moments(): pl.pallas_call(functools.partial(moments_kernel, count, ready, at, last,...  35.3 us
    ppermute x19, waiting for transfers between devices, move(): return lax.ppermute(block, AXES, route(target))  31.9 us
    ppermute x19, starting transfers between devices, move(): return lax.ppermute(block, AXES, route(target))  21.8 us
    pallas_call x1, Pallas kernels, opening(): pl.pallas_call(functools.partial(opening_kernel, count, valid_rows), in_s...  6.38 us
    pallas_call x1, Pallas kernels, prepare(): pl.pallas_call(functools.partial(prepare_kernel, at), in_specs=[smem_spec...  2.14 us
  transfers between devices with their start and end apart: 19, of which 9 were waited for; matrix products, arithmetic and copies ran while one was open for 0% of the time, Pallas kernels for 18%

profile of v5, /device:TPU:1, one launch (start us, length us, event | category | flops | bytes accessed | tf_op | source)
XLA Modules:
  0.0 99.4 jit_solution(12852565977747254760)
XLA Ops:
  0.8 0.1 stack.51.numbers.ids.refs_0_
  0.9 2.1 %shard_map.50 = (bf16[1040,512]{1,0:T(8,128)(2,1)S(1)}, bf16[528,1024]{1,0:T(8,128)(2,1)S(1)}, bf16[384,1024]{1,0:T(8,128)(2,1)S(1)}) custom-call(s32[12]{0:T(128)S(1)} %stack.51.numbers.ids.refs_0_, bf16[1024,512]{1,0:T(8,128)(2,1)} %projection.1, f32[1,512]{1,0:T(1,128)} %bitcast.13, bf16[768,1024]{1,0:T(8,128)(2,1)} %refs_3_.1), custom_call_target="tpu_custom_call" | custom-call | tf_op jit(solution)/shard_map/pallas_call | solution.py:138
  3.0 0.7 collective-permute-start.2
  3.7 3.6 %collective-permute-start.6 = (bf16[384,1024]{1,0:T(8,128)(2,1)S(1)}, bf16[384,1024]{1,0:T(8,128)(2,1)S(1)}, u32[]{:S(2)}, u32[]{:S(2)}) collective-permute-start(bf16[384,1024]{1,0:T(8,128)(2,1)S(1)} %get-tuple-element.52), channel_id=1, source_target_pairs={{0,16},{1,17},{2,50},{3,51},{4,20},{5,21},{6,54},{7,55},{8,24},{9,... | collective-permute-start | bytes 2359304 | tf_op jit(solution)/shard_map/ppermute | solution.py:32
  7.4 3.0 %collective-permute-start = (bf16[384,1024]{1,0:T(8,128)(2,1)S(1)}, bf16[384,1024]{1,0:T(8,128)(2,1)S(1)}, u32[]{:S(2)}, u32[]{:S(2)}) collective-permute-start(bf16[384,1024]{1,0:T(8,128)(2,1)S(1)} %get-tuple-element.52), channel_id=1, source_target_pairs={{0,65},{1,64},{2,67},{3,66},{4,69},{5,68},{6,71},{7,70},{8,73},{9,... | collective-permute-start | bytes 2359304 | tf_op jit(solution)/shard_map/ppermute | solution.py:32
  10.4 0.0 copy-start
  10.4 0.0 copy-start.1
  10.4 0.0 collective-permute-start.5
  10.4 0.8 collective-permute-start.3
  11.3 0.0 collective-permute-done.2.refs_1_
  11.3 0.7 collective-permute-start.4
  12.0 6.5 %collective-permute-done.6.refs_0_ = bf16[384,1024]{1,0:T(8,128)(2,1)S(1)} collective-permute-done((bf16[384,1024]{1,0:T(8,128)(2,1)S(1)}, bf16[384,1024]{1,0:T(8,128)(2,1)S(1)}, u32[]{:S(2)}, u32[]{:S(2)}) %collective-permute-start.6) | collective-permute-done | bytes 786464 | tf_op jit(solution)/shard_map/ppermute | solution.py:32
  18.5 3.5 %collective-permute-start.7 = (bf16[384,1024]{1,0:T(8,128)(2,1)S(1)}, bf16[384,1024]{1,0:T(8,128)(2,1)S(1)}, u32[]{:S(2)}, u32[]{:S(2)}) collective-permute-start(bf16[384,1024]{1,0:T(8,128)(2,1)S(1)} %get-tuple-element.52), channel_id=1, source_target_pairs={{0,48},{1,49},{2,18},{3,19},{4,52},{5,53},{6,22},{7,23},{8,56},{9,... | collective-permute-start | bytes 2359304 | tf_op jit(solution)/shard_map/ppermute | solution.py:32
  22.0 5.2 %collective-permute-done.refs_1_ = bf16[384,1024]{1,0:T(8,128)(2,1)S(1)} collective-permute-done((bf16[384,1024]{1,0:T(8,128)(2,1)S(1)}, bf16[384,1024]{1,0:T(8,128)(2,1)S(1)}, u32[]{:S(2)}, u32[]{:S(2)}) %collective-permute-start) | collective-permute-done | bytes 786464 | tf_op jit(solution)/shard_map/ppermute | solution.py:32
  27.2 0.0 collective-permute-start.8
  27.2 0.0 collective-permute-done.3.refs_3_
  27.2 8.8 %collective-permute-done.5.refs_6_.refs_9_.refs_10_ = bf16[528,1024]{1,0:T(8,128)(2,1)S(1)} collective-permute-done((bf16[528,1024]{1,0:T(8,128)(2,1)S(1)}, bf16[528,1024]{1,0:T(8,128)(2,1)S(1)}, u32[]{:S(2)}, u32[]{:S(2)}) %collective-permute-start.5) | collective-permute-done | bytes 1081376 | tf_op jit(solution)/shard_map/ppermute | solution.py:32
  36.0 0.0 collective-permute-done.7.refs_2_
  36.0 6.0 %collective-permute-done.8.refs_3_ = bf16[384,1024]{1,0:T(8,128)(2,1)S(1)} collective-permute-done((bf16[384,1024]{1,0:T(8,128)(2,1)S(1)}, bf16[384,1024]{1,0:T(8,128)(2,1)S(1)}, u32[]{:S(2)}, u32[]{:S(2)}) %collective-permute-start.8) | collective-permute-done | bytes 786464 | tf_op jit(solution)/shard_map/ppermute | solution.py:32
  42.0 0.0 collective-permute-done.4.refs_2_
  42.0 0.1 collective-permute-start.10
  42.1 0.4 collective-permute-start.9
  42.5 0.7 shard_map.52.refs_6_
  43.2 0.2 collective-permute-start.11
  43.4 0.4 collective-permute-start.12
  43.8 0.1 collective-permute-start.1
  43.9 0.4 collective-permute-done.10.refs_3_
  44.3 0.9 collective-permute-start.13
  45.2 0.2 collective-permute-done.9.refs_1_
  45.4 4.0 %collective-permute-start.14 = (bf16[384,1024]{1,0:T(8,128)(2,1)S(1)}, bf16[384,1024]{1,0:T(8,128)(2,1)S(1)}, u32[]{:S(2)}, u32[]{:S(2)}) collective-permute-start(bf16[384,1024]{1,0:T(8,128)(2,1)S(1)} %collective-permute-done.7.refs_2_), channel_id=1, source_target_pairs={{0,65},{1,64},{2,67},{3,66},{4,69},{5,68},{6,71},{7,70},{8,73},{9,... | collective-permute-start | bytes 2359304 | tf_op jit(solution)/shard_map/ppermute | solution.py:32
  49.4 0.0 copy-done
  49.4 0.0 copy-done.1
  49.4 6.4 %shard_map.51 = (f32[1024,128]{1,0:T(8,128)S(1)}, bf16[2,768,1024]{2,1,0:T(8,128)(2,1)S(1)}, bf16[3,1024,768]{2,1,0:T(8,128)(2,1)S(1)}) custom-call(s32[12]{0:T(128)S(1)} %stack.51.numbers.ids.refs_0_, bf16[384,1024]{1,0:T(8,128)(2,1)S(1)} %collective-permute-done.6.refs_0_, bf16[384,1024]{1,0:T(8,128)(2,1)S(1)} %collective-permute-done.9.refs_1_, ...), custom_call_target="tpu_custom_call" | custom-call | flops 4831838208 | bytes 3145728 | tf_op jit(solution)/shard_map/pallas_call | solution.py:221
  55.8 0.0 collective-permute-done.12.refs_6_
  55.8 2.1 %collective-permute-start.17 = (bf16[384,1024]{1,0:T(8,128)(2,1)S(1)}, bf16[384,1024]{1,0:T(8,128)(2,1)S(1)}, u32[]{:S(2)}, u32[]{:S(2)}) collective-permute-start(bf16[384,1024]{1,0:T(8,128)(2,1)S(1)} %collective-permute-done.8.refs_3_), channel_id=1, source_target_pairs={{0,16},{1,17},{2,50},{3,51},{4,20},{5,21},{6,54},{7,55},{8,24},{9,... | collective-permute-start | bytes 2359304 | tf_op jit(solution)/shard_map/ppermute | solution.py:32
  57.9 0.0 collective-permute-done.1.refs_2_
  58.0 0.0 collective-permute-done.11.refs_7_
  58.0 10.9 %shard_map.53 = (f32[1024,512]{1,0:T(8,128)S(1)}, f32[1024,512]{1,0:T(8,128)S(1)}, bf16[8,64,1024]{2,1,0:T(8,128)(2,1)S(1)}, bf16[8,64,1024]{2,1,0:T(8,128)(2,1)...) custom-call(s32[12]{0:T(128)S(1)} %stack.51.numbers.ids.refs_0_, ...), custom_call_target="tpu_custom_call" | custom-call | flops 16106127360 | bytes 6291456 | tf_op jit(solution)/shard_map/pallas_call | solution.py:425
  68.9 0.0 collective-permute-done.13.refs_1_
  68.9 0.0 collective-permute-done.14.refs_5_
  68.9 0.5 collective-permute-start.15
  69.4 0.1 collective-permute-start.16
  69.5 0.0 collective-permute-done.17.refs_7_
  69.5 1.8 %collective-permute-done.15.refs_2_ = bf16[384,1024]{1,0:T(8,128)(2,1)S(1)} collective-permute-done((bf16[384,1024]{1,0:T(8,128)(2,1)S(1)}, bf16[384,1024]{1,0:T(8,128)(2,1)S(1)}, u32[]{:S(2)}, u32[]{:S(2)}) %collective-permute-start.15) | collective-permute-done | bytes 786464 | tf_op jit(solution)/shard_map/ppermute | solution.py:32
  71.3 1.1 %collective-permute-done.16.refs_4_ = bf16[384,1024]{1,0:T(8,128)(2,1)S(1)} collective-permute-done((bf16[384,1024]{1,0:T(8,128)(2,1)S(1)}, bf16[384,1024]{1,0:T(8,128)(2,1)S(1)}, u32[]{:S(2)}, u32[]{:S(2)}) %collective-permute-start.16) | collective-permute-done | bytes 786464 | tf_op jit(solution)/shard_map/ppermute | solution.py:32
  72.4 0.4 collective-permute-start.18
  72.8 1.9 %collective-permute-done.18.refs_8_ = bf16[384,1024]{1,0:T(8,128)(2,1)S(1)} collective-permute-done((bf16[384,1024]{1,0:T(8,128)(2,1)S(1)}, bf16[384,1024]{1,0:T(8,128)(2,1)S(1)}, u32[]{:S(2)}, u32[]{:S(2)}) %collective-permute-start.18) | collective-permute-done | bytes 786464 | tf_op jit(solution)/shard_map/ppermute | solution.py:32
  74.7 24.4 %shard_map.54 = (f32[1024,1,512]{2,1,0:T(1,128)}, f32[1024,1,512]{2,1,0:T(1,128)}, f32[1024,512]{1,0:T(8,128)S(1)}, f32[1024,512]{1,0:T(8,128)S(1)}, bf16[8,64,1...) custom-call(s32[12]{0:T(128)S(1)} %stack.51.numbers.ids.refs_0_, ...), custom_call_target="tpu_custom_call", output_to_operand_aliasing={{2}: (15, {}), {3}: (16, {}), {4}: (17, {}), {5}: (18, {})} | custom-call | flops 20132659200 | bytes 7864320 | tf_op jit(solution)/shard_map/pallas_call | solution.py:425
Async XLA Ops:
  3.0 8.3 %collective-permute-start.2 = (bf16[1040,512]{1,0:T(8,128)(2,1)S(1)}, bf16[1040,512]{1,0:T(8,128)(2,1)S(1)}, u32[]{:S(2)}, u32[]{:S(2)}) collective-permute-start(bf16[1040,512]{1,0:T(8,128)(2,1)S(1)} %get-tuple-element.49.refs_0_), channel_id=1, source_target_pairs={{0,4},{1,5},{18,22},{19,23},{36,40},{37,41},{54,58},{55,59},{72,76... | collective-permute-start | bytes 3194888 | tf_op jit(solution)/shard_map/ppermute | solution.py:32
  3.7 14.8 %collective-permute-start.6 = (bf16[384,1024]{1,0:T(8,128)(2,1)S(1)}, bf16[384,1024]{1,0:T(8,128)(2,1)S(1)}, u32[]{:S(2)}, u32[]{:S(2)}) collective-permute-start(bf16[384,1024]{1,0:T(8,128)(2,1)S(1)} %get-tuple-element.52), channel_id=1, source_target_pairs={{0,16},{1,17},{2,50},{3,51},{4,20},{5,21},{6,54},{7,55},{8,24},{9,... | collective-permute-start | bytes 2359304 | tf_op jit(solution)/shard_map/ppermute | solution.py:32
  7.4 19.8 %collective-permute-start = (bf16[384,1024]{1,0:T(8,128)(2,1)S(1)}, bf16[384,1024]{1,0:T(8,128)(2,1)S(1)}, u32[]{:S(2)}, u32[]{:S(2)}) collective-permute-start(bf16[384,1024]{1,0:T(8,128)(2,1)S(1)} %get-tuple-element.52), channel_id=1, source_target_pairs={{0,65},{1,64},{2,67},{3,66},{4,69},{5,68},{6,71},{7,70},{8,73},{9,... | collective-permute-start | bytes 2359304 | tf_op jit(solution)/shard_map/ppermute | solution.py:32
  10.4 39.0 %copy-start = (bf16[768,1024]{1,0:T(8,128)(2,1)S(1)}, bf16[768,1024]{1,0:T(8,128)(2,1)}, u32[]{:S(2)}) copy-start(bf16[768,1024]{1,0:T(8,128)(2,1)} %refs_3_.1) | copy-start | bytes 4718596
  10.4 39.0 %copy-start.1 = (f32[512]{0:T(512)S(1)}, f32[512]{0:T(512)}, u32[]{:S(2)}) copy-start(f32[512]{0:T(512)} %param.5) | copy-start | bytes 6148
  10.4 25.6 %collective-permute-start.5 = (bf16[528,1024]{1,0:T(8,128)(2,1)S(1)}, bf16[528,1024]{1,0:T(8,128)(2,1)S(1)}, u32[]{:S(2)}, u32[]{:S(2)}) collective-permute-start(bf16[528,1024]{1,0:T(8,128)(2,1)S(1)} %get-tuple-element.50.refs_5_.refs_8_.refs_9_), channel_id=1, source_target_pairs={{0,1},{1,0},{2,3},{3,2},{4,5},{5,4},{6,7},{7,6},{8,9},{9,8},{10,11... | collective-permute-start | bytes 3244040 | tf_op jit(solution)/shard_map/ppermute | solution.py:32
  10.4 16.8 %collective-permute-start.3 = (bf16[1040,512]{1,0:T(8,128)(2,1)S(1)}, bf16[1040,512]{1,0:T(8,128)(2,1)S(1)}, u32[]{:S(2)}, u32[]{:S(2)}) collective-permute-start(bf16[1040,512]{1,0:T(8,128)(2,1)S(1)} %get-tuple-element.49.refs_0_), channel_id=1, source_target_pairs={{0,12},{1,13},{18,30},{19,31},{36,32},{37,33},{54,50},{55,51},{72,... | collective-permute-start | bytes 3194888 | tf_op jit(solution)/shard_map/ppermute | solution.py:32
  11.3 30.7 %collective-permute-start.4 = (bf16[1040,512]{1,0:T(8,128)(2,1)S(1)}, bf16[1040,512]{1,0:T(8,128)(2,1)S(1)}, u32[]{:S(2)}, u32[]{:S(2)}) collective-permute-start(bf16[1040,512]{1,0:T(8,128)(2,1)S(1)} %get-tuple-element.49.refs_0_), channel_id=1, source_target_pairs={{0,8},{1,9},{18,26},{19,27},{36,44},{37,45},{54,62},{55,63},{72,64... | collective-permute-start | bytes 3194888 | tf_op jit(solution)/shard_map/ppermute | solution.py:32
  18.5 17.5 %collective-permute-start.7 = (bf16[384,1024]{1,0:T(8,128)(2,1)S(1)}, bf16[384,1024]{1,0:T(8,128)(2,1)S(1)}, u32[]{:S(2)}, u32[]{:S(2)}) collective-permute-start(bf16[384,1024]{1,0:T(8,128)(2,1)S(1)} %get-tuple-element.52), channel_id=1, source_target_pairs={{0,48},{1,49},{2,18},{3,19},{4,52},{5,53},{6,22},{7,23},{8,56},{9,... | collective-permute-start | bytes 2359304 | tf_op jit(solution)/shard_map/ppermute | solution.py:32
  27.2 14.8 %collective-permute-start.8 = (bf16[384,1024]{1,0:T(8,128)(2,1)S(1)}, bf16[384,1024]{1,0:T(8,128)(2,1)S(1)}, u32[]{:S(2)}, u32[]{:S(2)}) collective-permute-start(bf16[384,1024]{1,0:T(8,128)(2,1)S(1)} %collective-permute-done.refs_1_), channel_id=1, source_target_pairs={{0,16},{1,17},{2,50},{3,51},{4,20},{5,21},{6,54},{7,55},{8,24},{9,... | collective-permute-start | bytes 2359304 | tf_op jit(solution)/shard_map/ppermute | solution.py:32
  42.0 2.3 %collective-permute-start.10 = (bf16[384,1024]{1,0:T(8,128)(2,1)S(1)}, bf16[384,1024]{1,0:T(8,128)(2,1)S(1)}, u32[]{:S(2)}, u32[]{:S(2)}) collective-permute-start(bf16[384,1024]{1,0:T(8,128)(2,1)S(1)} %collective-permute-done.6.refs_0_), channel_id=1, source_target_pairs={{0,2},{1,3},{2,0},{3,1},{4,6},{5,7},{6,4},{7,5},{8,10},{9,11},{10,... | collective-permute-start | bytes 2359304 | tf_op jit(solution)/shard_map/ppermute | solution.py:32
  42.1 3.3 %collective-permute-start.9 = (bf16[384,1024]{1,0:T(8,128)(2,1)S(1)}, bf16[384,1024]{1,0:T(8,128)(2,1)S(1)}, u32[]{:S(2)}, u32[]{:S(2)}) collective-permute-start(bf16[384,1024]{1,0:T(8,128)(2,1)S(1)} %collective-permute-done.7.refs_2_), channel_id=1, source_target_pairs={{0,2},{1,3},{2,0},{3,1},{4,6},{5,7},{6,4},{7,5},{8,10},{9,11},{10,... | collective-permute-start | bytes 2359304 | tf_op jit(solution)/shard_map/ppermute | solution.py:32
  43.2 14.8 %collective-permute-start.11 = (bf16[1040,512]{1,0:T(8,128)(2,1)S(1)}, bf16[1040,512]{1,0:T(8,128)(2,1)S(1)}, u32[]{:S(2)}, u32[]{:S(2)}) collective-permute-start(bf16[1040,512]{1,0:T(8,128)(2,1)S(1)} %shard_map.52.refs_6_), channel_id=1, source_target_pairs={{0,2},{1,3},{2,0},{3,1},{4,6},{5,7},{6,4},{7,5},{8,10},{9,11},{10,... | collective-permute-start | bytes 3194888 | tf_op jit(solution)/shard_map/ppermute | solution.py:32
  43.4 12.4 %collective-permute-start.12 = (bf16[384,1024]{1,0:T(8,128)(2,1)S(1)}, bf16[384,1024]{1,0:T(8,128)(2,1)S(1)}, u32[]{:S(2)}, u32[]{:S(2)}) collective-permute-start(bf16[384,1024]{1,0:T(8,128)(2,1)S(1)} %collective-permute-done.8.refs_3_), channel_id=1, source_target_pairs={{0,2},{1,3},{2,0},{3,1},{4,6},{5,7},{6,4},{7,5},{8,10},{9,11},{10,... | collective-permute-start | bytes 2359304 | tf_op jit(solution)/shard_map/ppermute | solution.py:32
  43.8 14.2 %collective-permute-start.1 = (bf16[384,1024]{1,0:T(8,128)(2,1)S(1)}, bf16[384,1024]{1,0:T(8,128)(2,1)S(1)}, u32[]{:S(2)}, u32[]{:S(2)}) collective-permute-start(bf16[384,1024]{1,0:T(8,128)(2,1)S(1)} %collective-permute-done.refs_1_), channel_id=1, source_target_pairs={{0,2},{1,3},{2,0},{3,1},{4,6},{5,7},{6,4},{7,5},{8,10},{9,11},{10,... | collective-permute-start | bytes 2359304 | tf_op jit(solution)/shard_map/ppermute | solution.py:32
  44.3 24.6 %collective-permute-start.13 = (bf16[384,1024]{1,0:T(8,128)(2,1)S(1)}, bf16[384,1024]{1,0:T(8,128)(2,1)S(1)}, u32[]{:S(2)}, u32[]{:S(2)}) collective-permute-start(bf16[384,1024]{1,0:T(8,128)(2,1)S(1)} %collective-permute-done.6.refs_0_), channel_id=1, source_target_pairs={{0,16},{1,17},{2,50},{3,51},{4,20},{5,21},{6,54},{7,55},{8,24},{9,... | collective-permute-start | bytes 2359304 | tf_op jit(solution)/shard_map/ppermute | solution.py:32
  45.4 23.5 %collective-permute-start.14 = (bf16[384,1024]{1,0:T(8,128)(2,1)S(1)}, bf16[384,1024]{1,0:T(8,128)(2,1)S(1)}, u32[]{:S(2)}, u32[]{:S(2)}) collective-permute-start(bf16[384,1024]{1,0:T(8,128)(2,1)S(1)} %collective-permute-done.7.refs_2_), channel_id=1, source_target_pairs={{0,65},{1,64},{2,67},{3,66},{4,69},{5,68},{6,71},{7,70},{8,73},{9,... | collective-permute-start | bytes 2359304 | tf_op jit(solution)/shard_map/ppermute | solution.py:32
  55.8 13.6 %collective-permute-start.17 = (bf16[384,1024]{1,0:T(8,128)(2,1)S(1)}, bf16[384,1024]{1,0:T(8,128)(2,1)S(1)}, u32[]{:S(2)}, u32[]{:S(2)}) collective-permute-start(bf16[384,1024]{1,0:T(8,128)(2,1)S(1)} %collective-permute-done.8.refs_3_), channel_id=1, source_target_pairs={{0,16},{1,17},{2,50},{3,51},{4,20},{5,21},{6,54},{7,55},{8,24},{9,... | collective-permute-start | bytes 2359304 | tf_op jit(solution)/shard_map/ppermute | solution.py:32
  68.9 2.4 %collective-permute-start.15 = (bf16[384,1024]{1,0:T(8,128)(2,1)S(1)}, bf16[384,1024]{1,0:T(8,128)(2,1)S(1)}, u32[]{:S(2)}, u32[]{:S(2)}) collective-permute-start(bf16[384,1024]{1,0:T(8,128)(2,1)S(1)} %collective-permute-done.13.refs_1_), channel_id=1, source_target_pairs={{0,2},{1,3},{2,0},{3,1},{4,6},{5,7},{6,4},{7,5},{8,10},{9,11},{10,... | collective-permute-start | bytes 2359304 | tf_op jit(solution)/shard_map/ppermute | solution.py:32
  69.4 3.0 %collective-permute-start.16 = (bf16[384,1024]{1,0:T(8,128)(2,1)S(1)}, bf16[384,1024]{1,0:T(8,128)(2,1)S(1)}, u32[]{:S(2)}, u32[]{:S(2)}) collective-permute-start(bf16[384,1024]{1,0:T(8,128)(2,1)S(1)} %collective-permute-done.14.refs_5_), channel_id=1, source_target_pairs={{0,2},{1,3},{2,0},{3,1},{4,6},{5,7},{6,4},{7,5},{8,10},{9,11},{10,... | collective-permute-start | bytes 2359304 | tf_op jit(solution)/shard_map/ppermute | solution.py:32
  72.4 2.3 %collective-permute-start.18 = (bf16[384,1024]{1,0:T(8,128)(2,1)S(1)}, bf16[384,1024]{1,0:T(8,128)(2,1)S(1)}, u32[]{:S(2)}, u32[]{:S(2)}) collective-permute-start(bf16[384,1024]{1,0:T(8,128)(2,1)S(1)} %collective-permute-done.17.refs_7_), channel_id=1, source_target_pairs={{0,2},{1,3},{2,0},{3,1},{4,6},{5,7},{6,4},{7,5},{8,10},{9,11},{10,... | collective-permute-start | bytes 2359304 | tf_op jit(solution)/shard_map/ppermute | solution.py:32

commit v6 on v4

--- a/solution.py
+++ b/solution.py
@@ -362,9 +362,9 @@
             keep_borders(k)
     for k in range(count - 1 if first else count):
         ahead = []
-        steps = [functools.partial(moment_tile, k, lag, n, h) for lag in (0, LAG) for h in range(2) for n in range(COL_TILES)]
+        lags = (LAG,) if last and k == 0 else (0, LAG)
+        steps = [functools.partial(moment_tile, k, lag, n, h) for lag in lags for h in range(2) for n in range(COL_TILES)]
         if last and k == 0:
-            steps.pop(0)()
             steps.pop(0)()
         if k + 1 < count:
             wait(loads[k + 1])
@@ -377,7 +377,11 @@
             ahead = [functools.partial(edge_cols, n) for n in range(COL_TILES)]
             ahead += [functools.partial(edge_rows, h) for h in range(2)]
         interleave(steps, ahead)
-    if last:
+    if first:
+        for h in range(2):
+            for n in range(COL_TILES):
+                moment_tile(between, 0, n, h)
+    else:
         for h in range(4):
             for n in range(COL_TILES):
                 moment_tile(count, LAG, n, h, 4)

time: 95.9 us -> 94.9 us (0.990)
  transfers between devices with their start and end apart: 19 -> 19, of which waited for: 8 -> 8; matrix products, arithmetic and copies ran while one was open for 0% -> 0% of each run, Pallas kernels for 19% -> 20%
where the time goes in v6:
time: 94.9 us; the launch traced here: 93.3 us
  Pallas kernels  44.5 us (47%)
  starting transfers between devices  24.3 us (26%)
  waiting for transfers between devices  23.3 us (25%)
  between operations  1.11 us (1%)
    pallas_call x2, Pallas kernels, moments(): pl.pallas_call(functools.partial(moments_kernel, count, ready, at, last,...  35.3 us
    ppermute x19, starting transfers between devices, move(): return lax.ppermute(block, AXES, route(target))  24.3 us
    ppermute x19, waiting for transfers between devices, move(): return lax.ppermute(block, AXES, route(target))  23.3 us
    pallas_call x1, Pallas kernels, opening(): pl.pallas_call(functools.partial(opening_kernel, count, valid_rows), in_s...  6.39 us
    pallas_call x1, Pallas kernels, prepare(): pl.pallas_call(functools.partial(prepare_kernel, at), in_specs=[smem_spec...  2.14 us
  transfers between devices with their start and end apart: 19, of which 8 were waited for; matrix products, arithmetic and copies ran while one was open for 0% of the time, Pallas kernels for 20%

profile of v6, /device:TPU:1, one launch (start us, length us, event | category | flops | bytes accessed | tf_op | source)
XLA Modules:
  0.0 93.3 jit_solution(16746085394988844614)
XLA Ops:
  0.8 0.1 stack.51.numbers.ids.refs_0_
  0.9 2.1 %shard_map.50 = (bf16[1040,512]{1,0:T(8,128)(2,1)S(1)}, bf16[528,1024]{1,0:T(8,128)(2,1)S(1)}, bf16[384,1024]{1,0:T(8,128)(2,1)S(1)}) custom-call(s32[12]{0:T(128)S(1)} %stack.51.numbers.ids.refs_0_, bf16[1024,512]{1,0:T(8,128)(2,1)} %projection.1, f32[1,512]{1,0:T(1,128)} %bitcast.13, bf16[768,1024]{1,0:T(8,128)(2,1)} %refs_3_.1), custom_call_target="tpu_custom_call" | custom-call | tf_op jit(solution)/shard_map/pallas_call | solution.py:138
  3.0 0.7 collective-permute-start.3
  3.7 3.6 %collective-permute-start.1 = (bf16[384,1024]{1,0:T(8,128)(2,1)S(1)}, bf16[384,1024]{1,0:T(8,128)(2,1)S(1)}, u32[]{:S(2)}, u32[]{:S(2)}) collective-permute-start(bf16[384,1024]{1,0:T(8,128)(2,1)S(1)} %get-tuple-element.55), channel_id=1, source_target_pairs={{0,16},{1,17},{2,50},{3,51},{4,20},{5,21},{6,54},{7,55},{8,24},{9,... | collective-permute-start | bytes 2359304 | tf_op jit(solution)/shard_map/ppermute | solution.py:32
  7.4 3.0 %collective-permute-start = (bf16[384,1024]{1,0:T(8,128)(2,1)S(1)}, bf16[384,1024]{1,0:T(8,128)(2,1)S(1)}, u32[]{:S(2)}, u32[]{:S(2)}) collective-permute-start(bf16[384,1024]{1,0:T(8,128)(2,1)S(1)} %get-tuple-element.55), channel_id=1, source_target_pairs={{0,65},{1,64},{2,67},{3,66},{4,69},{5,68},{6,71},{7,70},{8,73},{9,... | collective-permute-start | bytes 2359304 | tf_op jit(solution)/shard_map/ppermute | solution.py:32
  10.4 0.0 copy-start
  10.4 0.0 copy-start.1
  10.4 0.0 collective-permute-start.6
  10.4 0.8 collective-permute-start.4
  11.3 0.0 collective-permute-done.3.refs_1_
  11.3 0.7 collective-permute-start.5
  12.0 6.5 %collective-permute-done.1.refs_0_ = bf16[384,1024]{1,0:T(8,128)(2,1)S(1)} collective-permute-done((bf16[384,1024]{1,0:T(8,128)(2,1)S(1)}, bf16[384,1024]{1,0:T(8,128)(2,1)S(1)}, u32[]{:S(2)}, u32[]{:S(2)}) %collective-permute-start.1) | collective-permute-done | bytes 786464 | tf_op jit(solution)/shard_map/ppermute | solution.py:32
  18.5 3.5 %collective-permute-start.7 = (bf16[384,1024]{1,0:T(8,128)(2,1)S(1)}, bf16[384,1024]{1,0:T(8,128)(2,1)S(1)}, u32[]{:S(2)}, u32[]{:S(2)}) collective-permute-start(bf16[384,1024]{1,0:T(8,128)(2,1)S(1)} %get-tuple-element.55), channel_id=1, source_target_pairs={{0,48},{1,49},{2,18},{3,19},{4,52},{5,53},{6,22},{7,23},{8,56},{9,... | collective-permute-start | bytes 2359304 | tf_op jit(solution)/shard_map/ppermute | solution.py:32
  22.0 5.2 %collective-permute-done.refs_1_ = bf16[384,1024]{1,0:T(8,128)(2,1)S(1)} collective-permute-done((bf16[384,1024]{1,0:T(8,128)(2,1)S(1)}, bf16[384,1024]{1,0:T(8,128)(2,1)S(1)}, u32[]{:S(2)}, u32[]{:S(2)}) %collective-permute-start) | collective-permute-done | bytes 786464 | tf_op jit(solution)/shard_map/ppermute | solution.py:32
  27.2 1.7 %collective-permute-start.8 = (bf16[384,1024]{1,0:T(8,128)(2,1)S(1)}, bf16[384,1024]{1,0:T(8,128)(2,1)S(1)}, u32[]{:S(2)}, u32[]{:S(2)}) collective-permute-start(bf16[384,1024]{1,0:T(8,128)(2,1)S(1)} %collective-permute-done.1.refs_0_), channel_id=1, source_target_pairs={{0,2},{1,3},{2,0},{3,1},{4,6},{5,7},{6,4},{7,5},{8,10},{9,11},{10,... | collective-permute-start | bytes 2359304 | tf_op jit(solution)/shard_map/ppermute | solution.py:32
  28.9 0.0 collective-permute-done.4.refs_3_
  28.9 6.8 %collective-permute-done.6.refs_6_.refs_9_.refs_10_ = bf16[528,1024]{1,0:T(8,128)(2,1)S(1)} collective-permute-done((bf16[528,1024]{1,0:T(8,128)(2,1)S(1)}, bf16[528,1024]{1,0:T(8,128)(2,1)S(1)}, u32[]{:S(2)}, u32[]{:S(2)}) %collective-permute-start.6) | collective-permute-done | bytes 1081376 | tf_op jit(solution)/shard_map/ppermute | solution.py:32
  35.7 0.0 collective-permute-done.7.refs_2_
  35.7 0.0 collective-permute-done.8.refs_3_
  35.7 0.0 collective-permute-done.5.refs_2_
  35.7 0.5 collective-permute-start.9
  36.2 0.7 shard_map.52.refs_6_
  36.9 0.2 collective-permute-start.10
  37.1 0.7 collective-permute-start.11
  37.7 0.0 collective-permute-start.2
  37.7 2.7 %collective-permute-start.12 = (bf16[384,1024]{1,0:T(8,128)(2,1)S(1)}, bf16[384,1024]{1,0:T(8,128)(2,1)S(1)}, u32[]{:S(2)}, u32[]{:S(2)}) collective-permute-start(bf16[384,1024]{1,0:T(8,128)(2,1)S(1)} %collective-permute-done.1.refs_0_), channel_id=1, source_target_pairs={{0,16},{1,17},{2,50},{3,51},{4,20},{5,21},{6,54},{7,55},{8,24},{9,... | collective-permute-start | bytes 2359304 | tf_op jit(solution)/shard_map/ppermute | solution.py:32
  40.4 0.0 collective-permute-done.9.refs_1_
  40.4 4.9 %collective-permute-start.13 = (bf16[384,1024]{1,0:T(8,128)(2,1)S(1)}, bf16[384,1024]{1,0:T(8,128)(2,1)S(1)}, u32[]{:S(2)}, u32[]{:S(2)}) collective-permute-start(bf16[384,1024]{1,0:T(8,128)(2,1)S(1)} %collective-permute-done.7.refs_2_), channel_id=1, source_target_pairs={{0,65},{1,64},{2,67},{3,66},{4,69},{5,68},{6,71},{7,70},{8,73},{9,... | collective-permute-start | bytes 2359304 | tf_op jit(solution)/shard_map/ppermute | solution.py:32
  45.3 0.0 copy-done
  45.3 0.0 copy-done.1
  45.3 6.4 %shard_map.51 = (f32[1024,128]{1,0:T(8,128)S(1)}, bf16[2,768,1024]{2,1,0:T(8,128)(2,1)S(1)}, bf16[3,1024,768]{2,1,0:T(8,128)(2,1)S(1)}) custom-call(s32[12]{0:T(128)S(1)} %stack.51.numbers.ids.refs_0_, bf16[384,1024]{1,0:T(8,128)(2,1)S(1)} %collective-permute-done.1.refs_0_, bf16[384,1024]{1,0:T(8,128)(2,1)S(1)} %collective-permute-done.9.refs_1_, ...), custom_call_target="tpu_custom_call" | custom-call | flops 4831838208 | bytes 3145728 | tf_op jit(solution)/shard_map/pallas_call | solution.py:221
  51.7 0.0 collective-permute-done.11.refs_3_
  51.7 0.3 collective-permute-start.16
  52.0 0.0 collective-permute-done.2.refs_2_
  52.0 0.0 collective-permute-done.10.refs_7_
  52.0 11.7 %shard_map.53 = (f32[1024,512]{1,0:T(8,128)S(1)}, f32[1024,512]{1,0:T(8,128)S(1)}, bf16[8,64,1024]{2,1,0:T(8,128)(2,1)S(1)}, bf16[8,64,1024]{2,1,0:T(8,128)(2,1)...) custom-call(s32[12]{0:T(128)S(1)} %stack.51.numbers.ids.refs_0_, ...), custom_call_target="tpu_custom_call" | custom-call | flops 16106127360 | bytes 6291456 | tf_op jit(solution)/shard_map/pallas_call | solution.py:429
  63.8 0.0 collective-permute-done.12.refs_1_
  63.8 0.0 collective-permute-done.13.refs_5_
  63.8 0.1 collective-permute-start.14
  63.9 0.5 collective-permute-start.15
  64.4 0.1 collective-permute-start.17
  64.5 0.6 collective-permute-done.16.refs_7_
  65.1 1.1 %collective-permute-done.14.refs_2_ = bf16[384,1024]{1,0:T(8,128)(2,1)S(1)} collective-permute-done((bf16[384,1024]{1,0:T(8,128)(2,1)S(1)}, bf16[384,1024]{1,0:T(8,128)(2,1)S(1)}, u32[]{:S(2)}, u32[]{:S(2)}) %collective-permute-start.14) | collective-permute-done | bytes 786464 | tf_op jit(solution)/shard_map/ppermute | solution.py:32
  66.2 1.1 %collective-permute-done.15.refs_4_ = bf16[384,1024]{1,0:T(8,128)(2,1)S(1)} collective-permute-done((bf16[384,1024]{1,0:T(8,128)(2,1)S(1)}, bf16[384,1024]{1,0:T(8,128)(2,1)S(1)}, u32[]{:S(2)}, u32[]{:S(2)}) %collective-permute-start.15) | collective-permute-done | bytes 786464 | tf_op jit(solution)/shard_map/ppermute | solution.py:32
  67.3 0.2 collective-permute-start.18
  67.5 0.9 collective-permute-done.17.refs_6_
  68.4 1.2 %collective-permute-done.18.refs_8_ = bf16[384,1024]{1,0:T(8,128)(2,1)S(1)} collective-permute-done((bf16[384,1024]{1,0:T(8,128)(2,1)S(1)}, bf16[384,1024]{1,0:T(8,128)(2,1)S(1)}, u32[]{:S(2)}, u32[]{:S(2)}) %collective-permute-start.18) | collective-permute-done | bytes 786464 | tf_op jit(solution)/shard_map/ppermute | solution.py:32
  69.6 23.5 %shard_map.54 = (f32[1024,1,512]{2,1,0:T(1,128)}, f32[1024,1,512]{2,1,0:T(1,128)}, f32[1024,512]{1,0:T(8,128)S(1)}, f32[1024,512]{1,0:T(8,128)S(1)}, bf16[8,64,1...) custom-call(s32[12]{0:T(128)S(1)} %stack.51.numbers.ids.refs_0_, ...), custom_call_target="tpu_custom_call", output_to_operand_aliasing={{2}: (15, {}), {3}: (16, {}), {4}: (17, {}), {5}: (18, {})} | custom-call | flops 20132659200 | bytes 7864320 | tf_op jit(solution)/shard_map/pallas_call | solution.py:429
Async XLA Ops:
  3.0 8.3 %collective-permute-start.3 = (bf16[1040,512]{1,0:T(8,128)(2,1)S(1)}, bf16[1040,512]{1,0:T(8,128)(2,1)S(1)}, u32[]{:S(2)}, u32[]{:S(2)}) collective-permute-start(bf16[1040,512]{1,0:T(8,128)(2,1)S(1)} %get-tuple-element.53.refs_0_), channel_id=1, source_target_pairs={{0,4},{1,5},{18,22},{19,23},{36,40},{37,41},{54,58},{55,59},{72,76... | collective-permute-start | bytes 3194888 | tf_op jit(solution)/shard_map/ppermute | solution.py:32
  3.7 14.8 %collective-permute-start.1 = (bf16[384,1024]{1,0:T(8,128)(2,1)S(1)}, bf16[384,1024]{1,0:T(8,128)(2,1)S(1)}, u32[]{:S(2)}, u32[]{:S(2)}) collective-permute-start(bf16[384,1024]{1,0:T(8,128)(2,1)S(1)} %get-tuple-element.55), channel_id=1, source_target_pairs={{0,16},{1,17},{2,50},{3,51},{4,20},{5,21},{6,54},{7,55},{8,24},{9,... | collective-permute-start | bytes 2359304 | tf_op jit(solution)/shard_map/ppermute | solution.py:32
  7.4 19.8 %collective-permute-start = (bf16[384,1024]{1,0:T(8,128)(2,1)S(1)}, bf16[384,1024]{1,0:T(8,128)(2,1)S(1)}, u32[]{:S(2)}, u32[]{:S(2)}) collective-permute-start(bf16[384,1024]{1,0:T(8,128)(2,1)S(1)} %get-tuple-element.55), channel_id=1, source_target_pairs={{0,65},{1,64},{2,67},{3,66},{4,69},{5,68},{6,71},{7,70},{8,73},{9,... | collective-permute-start | bytes 2359304 | tf_op jit(solution)/shard_map/ppermute | solution.py:32
  10.4 34.9 %copy-start = (bf16[768,1024]{1,0:T(8,128)(2,1)S(1)}, bf16[768,1024]{1,0:T(8,128)(2,1)}, u32[]{:S(2)}) copy-start(bf16[768,1024]{1,0:T(8,128)(2,1)} %refs_3_.1) | copy-start | bytes 4718596
  10.4 34.9 %copy-start.1 = (f32[512]{0:T(512)S(1)}, f32[512]{0:T(512)}, u32[]{:S(2)}) copy-start(f32[512]{0:T(512)} %param.5) | copy-start | bytes 6148
  10.4 25.3 %collective-permute-start.6 = (bf16[528,1024]{1,0:T(8,128)(2,1)S(1)}, bf16[528,1024]{1,0:T(8,128)(2,1)S(1)}, u32[]{:S(2)}, u32[]{:S(2)}) collective-permute-start(bf16[528,1024]{1,0:T(8,128)(2,1)S(1)} %get-tuple-element.54.refs_5_.refs_8_.refs_9_), channel_id=1, source_target_pairs={{0,1},{1,0},{2,3},{3,2},{4,5},{5,4},{6,7},{7,6},{8,9},{9,8},{10,11... | collective-permute-start | bytes 3244040 | tf_op jit(solution)/shard_map/ppermute | solution.py:32
  10.4 18.5 %collective-permute-start.4 = (bf16[1040,512]{1,0:T(8,128)(2,1)S(1)}, bf16[1040,512]{1,0:T(8,128)(2,1)S(1)}, u32[]{:S(2)}, u32[]{:S(2)}) collective-permute-start(bf16[1040,512]{1,0:T(8,128)(2,1)S(1)} %get-tuple-element.53.refs_0_), channel_id=1, source_target_pairs={{0,12},{1,13},{18,30},{19,31},{36,32},{37,33},{54,50},{55,51},{72,... | collective-permute-start | bytes 3194888 | tf_op jit(solution)/shard_map/ppermute | solution.py:32
  11.3 24.4 %collective-permute-start.5 = (bf16[1040,512]{1,0:T(8,128)(2,1)S(1)}, bf16[1040,512]{1,0:T(8,128)(2,1)S(1)}, u32[]{:S(2)}, u32[]{:S(2)}) collective-permute-start(bf16[1040,512]{1,0:T(8,128)(2,1)S(1)} %get-tuple-element.53.refs_0_), channel_id=1, source_target_pairs={{0,8},{1,9},{18,26},{19,27},{36,44},{37,45},{54,62},{55,63},{72,64... | collective-permute-start | bytes 3194888 | tf_op jit(solution)/shard_map/ppermute | solution.py:32
  18.5 17.2 %collective-permute-start.7 = (bf16[384,1024]{1,0:T(8,128)(2,1)S(1)}, bf16[384,1024]{1,0:T(8,128)(2,1)S(1)}, u32[]{:S(2)}, u32[]{:S(2)}) collective-permute-start(bf16[384,1024]{1,0:T(8,128)(2,1)S(1)} %get-tuple-element.55), channel_id=1, source_target_pairs={{0,48},{1,49},{2,18},{3,19},{4,52},{5,53},{6,22},{7,23},{8,56},{9,... | collective-permute-start | bytes 2359304 | tf_op jit(solution)/shard_map/ppermute | solution.py:32
  27.2 8.5 %collective-permute-start.8 = (bf16[384,1024]{1,0:T(8,128)(2,1)S(1)}, bf16[384,1024]{1,0:T(8,128)(2,1)S(1)}, u32[]{:S(2)}, u32[]{:S(2)}) collective-permute-start(bf16[384,1024]{1,0:T(8,128)(2,1)S(1)} %collective-permute-done.1.refs_0_), channel_id=1, source_target_pairs={{0,2},{1,3},{2,0},{3,1},{4,6},{5,7},{6,4},{7,5},{8,10},{9,11},{10,... | collective-permute-start | bytes 2359304 | tf_op jit(solution)/shard_map/ppermute | solution.py:32
  35.7 4.7 %collective-permute-start.9 = (bf16[384,1024]{1,0:T(8,128)(2,1)S(1)}, bf16[384,1024]{1,0:T(8,128)(2,1)S(1)}, u32[]{:S(2)}, u32[]{:S(2)}) collective-permute-start(bf16[384,1024]{1,0:T(8,128)(2,1)S(1)} %collective-permute-done.7.refs_2_), channel_id=1, source_target_pairs={{0,2},{1,3},{2,0},{3,1},{4,6},{5,7},{6,4},{7,5},{8,10},{9,11},{10,... | collective-permute-start | bytes 2359304 | tf_op jit(solution)/shard_map/ppermute | solution.py:32
  36.9 15.2 %collective-permute-start.10 = (bf16[1040,512]{1,0:T(8,128)(2,1)S(1)}, bf16[1040,512]{1,0:T(8,128)(2,1)S(1)}, u32[]{:S(2)}, u32[]{:S(2)}) collective-permute-start(bf16[1040,512]{1,0:T(8,128)(2,1)S(1)} %shard_map.52.refs_6_), channel_id=1, source_target_pairs={{0,2},{1,3},{2,0},{3,1},{4,6},{5,7},{6,4},{7,5},{8,10},{9,11},{10,... | collective-permute-start | bytes 3194888 | tf_op jit(solution)/shard_map/ppermute | solution.py:32
  37.1 14.7 %collective-permute-start.11 = (bf16[384,1024]{1,0:T(8,128)(2,1)S(1)}, bf16[384,1024]{1,0:T(8,128)(2,1)S(1)}, u32[]{:S(2)}, u32[]{:S(2)}) collective-permute-start(bf16[384,1024]{1,0:T(8,128)(2,1)S(1)} %collective-permute-done.refs_1_), channel_id=1, source_target_pairs={{0,16},{1,17},{2,50},{3,51},{4,20},{5,21},{6,54},{7,55},{8,24},{9,... | collective-permute-start | bytes 2359304 | tf_op jit(solution)/shard_map/ppermute | solution.py:32
  37.7 14.3 %collective-permute-start.2 = (bf16[384,1024]{1,0:T(8,128)(2,1)S(1)}, bf16[384,1024]{1,0:T(8,128)(2,1)S(1)}, u32[]{:S(2)}, u32[]{:S(2)}) collective-permute-start(bf16[384,1024]{1,0:T(8,128)(2,1)S(1)} %collective-permute-done.refs_1_), channel_id=1, source_target_pairs={{0,2},{1,3},{2,0},{3,1},{4,6},{5,7},{6,4},{7,5},{8,10},{9,11},{10,... | collective-permute-start | bytes 2359304 | tf_op jit(solution)/shard_map/ppermute | solution.py:32
  37.7 26.0 %collective-permute-start.12 = (bf16[384,1024]{1,0:T(8,128)(2,1)S(1)}, bf16[384,1024]{1,0:T(8,128)(2,1)S(1)}, u32[]{:S(2)}, u32[]{:S(2)}) collective-permute-start(bf16[384,1024]{1,0:T(8,128)(2,1)S(1)} %collective-permute-done.1.refs_0_), channel_id=1, source_target_pairs={{0,16},{1,17},{2,50},{3,51},{4,20},{5,21},{6,54},{7,55},{8,24},{9,... | collective-permute-start | bytes 2359304 | tf_op jit(solution)/shard_map/ppermute | solution.py:32
  40.4 23.4 %collective-permute-start.13 = (bf16[384,1024]{1,0:T(8,128)(2,1)S(1)}, bf16[384,1024]{1,0:T(8,128)(2,1)S(1)}, u32[]{:S(2)}, u32[]{:S(2)}) collective-permute-start(bf16[384,1024]{1,0:T(8,128)(2,1)S(1)} %collective-permute-done.7.refs_2_), channel_id=1, source_target_pairs={{0,65},{1,64},{2,67},{3,66},{4,69},{5,68},{6,71},{7,70},{8,73},{9,... | collective-permute-start | bytes 2359304 | tf_op jit(solution)/shard_map/ppermute | solution.py:32
  51.7 13.3 %collective-permute-start.16 = (bf16[384,1024]{1,0:T(8,128)(2,1)S(1)}, bf16[384,1024]{1,0:T(8,128)(2,1)S(1)}, u32[]{:S(2)}, u32[]{:S(2)}) collective-permute-start(bf16[384,1024]{1,0:T(8,128)(2,1)S(1)} %collective-permute-done.11.refs_3_), channel_id=1, source_target_pairs={{0,16},{1,17},{2,50},{3,51},{4,20},{5,21},{6,54},{7,55},{8,24},{9,... | collective-permute-start | bytes 2359304 | tf_op jit(solution)/shard_map/ppermute | solution.py:32
  63.8 2.4 %collective-permute-start.14 = (bf16[384,1024]{1,0:T(8,128)(2,1)S(1)}, bf16[384,1024]{1,0:T(8,128)(2,1)S(1)}, u32[]{:S(2)}, u32[]{:S(2)}) collective-permute-start(bf16[384,1024]{1,0:T(8,128)(2,1)S(1)} %collective-permute-done.12.refs_1_), channel_id=1, source_target_pairs={{0,2},{1,3},{2,0},{3,1},{4,6},{5,7},{6,4},{7,5},{8,10},{9,11},{10,... | collective-permute-start | bytes 2359304 | tf_op jit(solution)/shard_map/ppermute | solution.py:32
  63.9 3.4 %collective-permute-start.15 = (bf16[384,1024]{1,0:T(8,128)(2,1)S(1)}, bf16[384,1024]{1,0:T(8,128)(2,1)S(1)}, u32[]{:S(2)}, u32[]{:S(2)}) collective-permute-start(bf16[384,1024]{1,0:T(8,128)(2,1)S(1)} %collective-permute-done.13.refs_5_), channel_id=1, source_target_pairs={{0,2},{1,3},{2,0},{3,1},{4,6},{5,7},{6,4},{7,5},{8,10},{9,11},{10,... | collective-permute-start | bytes 2359304 | tf_op jit(solution)/shard_map/ppermute | solution.py:32
  64.4 4.0 %collective-permute-start.17 = (bf16[384,1024]{1,0:T(8,128)(2,1)S(1)}, bf16[384,1024]{1,0:T(8,128)(2,1)S(1)}, u32[]{:S(2)}, u32[]{:S(2)}) collective-permute-start(bf16[384,1024]{1,0:T(8,128)(2,1)S(1)} %collective-permute-done.11.refs_3_), channel_id=1, source_target_pairs={{0,2},{1,3},{2,0},{3,1},{4,6},{5,7},{6,4},{7,5},{8,10},{9,11},{10,... | collective-permute-start | bytes 2359304 | tf_op jit(solution)/shard_map/ppermute | solution.py:32
  67.3 2.3 %collective-permute-start.18 = (bf16[384,1024]{1,0:T(8,128)(2,1)S(1)}, bf16[384,1024]{1,0:T(8,128)(2,1)S(1)}, u32[]{:S(2)}, u32[]{:S(2)}) collective-permute-start(bf16[384,1024]{1,0:T(8,128)(2,1)S(1)} %collective-permute-done.16.refs_7_), channel_id=1, source_target_pairs={{0,2},{1,3},{2,0},{3,1},{4,6},{5,7},{6,4},{7,5},{8,10},{9,11},{10,... | collective-permute-start | bytes 2359304 | tf_op jit(solution)/shard_map/ppermute | solution.py:32

commit v7 on v6

--- a/solution.py
+++ b/solution.py
@@ -365,6 +365,8 @@
         lags = (LAG,) if last and k == 0 else (0, LAG)
         steps = [functools.partial(moment_tile, k, lag, n, h) for lag in lags for h in range(2) for n in range(COL_TILES)]
         if last and k == 0:
+            steps = steps[COL_TILES:]
+        if last and k == 0:
             steps.pop(0)()
         if k + 1 < count:
             wait(loads[k + 1])
@@ -376,11 +378,11 @@
         elif last:
             ahead = [functools.partial(edge_cols, n) for n in range(COL_TILES)]
             ahead += [functools.partial(edge_rows, h) for h in range(2)]
-        interleave(steps, ahead)
+        interleave(steps or [lambda: None], ahead)
     if first:
-        for h in range(2):
+        for lag, h in ((0, 0), (0, 1), (LAG, 0)):
             for n in range(COL_TILES):
-                moment_tile(between, 0, n, h)
+                moment_tile(between, lag, n, h)
     else:
         for h in range(4):
             for n in range(COL_TILES):

time: 94.9 us -> 94.9 us (level)
  no operation moved by 1% of the time
where the time goes in v7:
time: 94.9 us; the launch traced here: 93.7 us
  Pallas kernels  44.8 us (47%)
  starting transfers between devices  24.2 us (26%)
  waiting for transfers between devices  23.4 us (25%)
  between operations  1.09 us (1%)
    pallas_call x2, Pallas kernels, moments(): pl.pallas_call(functools.partial(moments_kernel, count, ready, at, last,...  35.6 us
    ppermute x19, starting transfers between devices, move(): return lax.ppermute(block, AXES, route(target))  24.2 us
    ppermute x19, waiting for transfers between devices, move(): return lax.ppermute(block, AXES, route(target))  23.4 us
    pallas_call x1, Pallas kernels, opening(): pl.pallas_call(functools.partial(opening_kernel, count, valid_rows), in_s...  6.39 us
    pallas_call x1, Pallas kernels, prepare(): pl.pallas_call(functools.partial(prepare_kernel, at), in_specs=[smem_spec...  2.14 us
  transfers between devices with their start and end apart: 19, of which 8 were waited for; matrix products, arithmetic and copies ran while one was open for 0% of the time, Pallas kernels for 20%

profile of v7, /device:TPU:1, one launch (start us, length us, event | category | flops | bytes accessed | tf_op | source)
XLA Modules:
  0.0 93.7 jit_solution(6430548282524303568)
XLA Ops:
  0.8 0.1 stack.51.numbers.ids.refs_0_
  0.9 2.1 %shard_map.50 = (bf16[1040,512]{1,0:T(8,128)(2,1)S(1)}, bf16[528,1024]{1,0:T(8,128)(2,1)S(1)}, bf16[384,1024]{1,0:T(8,128)(2,1)S(1)}) custom-call(s32[12]{0:T(128)S(1)} %stack.51.numbers.ids.refs_0_, bf16[1024,512]{1,0:T(8,128)(2,1)} %projection.1, f32[1,512]{1,0:T(1,128)} %bitcast.13, bf16[768,1024]{1,0:T(8,128)(2,1)} %refs_3_.1), custom_call_target="tpu_custom_call" | custom-call | tf_op jit(solution)/shard_map/pallas_call | solution.py:138
  3.0 0.7 collective-permute-start.3
  3.7 3.6 %collective-permute-start.1 = (bf16[384,1024]{1,0:T(8,128)(2,1)S(1)}, bf16[384,1024]{1,0:T(8,128)(2,1)S(1)}, u32[]{:S(2)}, u32[]{:S(2)}) collective-permute-start(bf16[384,1024]{1,0:T(8,128)(2,1)S(1)} %get-tuple-element.55), channel_id=1, source_target_pairs={{0,16},{1,17},{2,50},{3,51},{4,20},{5,21},{6,54},{7,55},{8,24},{9,... | collective-permute-start | bytes 2359304 | tf_op jit(solution)/shard_map/ppermute | solution.py:32
  7.4 3.0 %collective-permute-start = (bf16[384,1024]{1,0:T(8,128)(2,1)S(1)}, bf16[384,1024]{1,0:T(8,128)(2,1)S(1)}, u32[]{:S(2)}, u32[]{:S(2)}) collective-permute-start(bf16[384,1024]{1,0:T(8,128)(2,1)S(1)} %get-tuple-element.55), channel_id=1, source_target_pairs={{0,65},{1,64},{2,67},{3,66},{4,69},{5,68},{6,71},{7,70},{8,73},{9,... | collective-permute-start | bytes 2359304 | tf_op jit(solution)/shard_map/ppermute | solution.py:32
  10.4 0.0 copy-start
  10.4 0.0 copy-start.1
  10.4 0.0 collective-permute-start.6
  10.4 0.8 collective-permute-start.4
  11.3 0.0 collective-permute-done.3.refs_1_
  11.3 0.7 collective-permute-start.5
  12.0 6.5 %collective-permute-done.1.refs_0_ = bf16[384,1024]{1,0:T(8,128)(2,1)S(1)} collective-permute-done((bf16[384,1024]{1,0:T(8,128)(2,1)S(1)}, bf16[384,1024]{1,0:T(8,128)(2,1)S(1)}, u32[]{:S(2)}, u32[]{:S(2)}) %collective-permute-start.1) | collective-permute-done | bytes 786464 | tf_op jit(solution)/shard_map/ppermute | solution.py:32
  18.5 3.5 %collective-permute-start.7 = (bf16[384,1024]{1,0:T(8,128)(2,1)S(1)}, bf16[384,1024]{1,0:T(8,128)(2,1)S(1)}, u32[]{:S(2)}, u32[]{:S(2)}) collective-permute-start(bf16[384,1024]{1,0:T(8,128)(2,1)S(1)} %get-tuple-element.55), channel_id=1, source_target_pairs={{0,48},{1,49},{2,18},{3,19},{4,52},{5,53},{6,22},{7,23},{8,56},{9,... | collective-permute-start | bytes 2359304 | tf_op jit(solution)/shard_map/ppermute | solution.py:32
  22.0 5.2 %collective-permute-done.refs_1_ = bf16[384,1024]{1,0:T(8,128)(2,1)S(1)} collective-permute-done((bf16[384,1024]{1,0:T(8,128)(2,1)S(1)}, bf16[384,1024]{1,0:T(8,128)(2,1)S(1)}, u32[]{:S(2)}, u32[]{:S(2)}) %collective-permute-start) | collective-permute-done | bytes 786464 | tf_op jit(solution)/shard_map/ppermute | solution.py:32
  27.2 1.7 %collective-permute-start.8 = (bf16[384,1024]{1,0:T(8,128)(2,1)S(1)}, bf16[384,1024]{1,0:T(8,128)(2,1)S(1)}, u32[]{:S(2)}, u32[]{:S(2)}) collective-permute-start(bf16[384,1024]{1,0:T(8,128)(2,1)S(1)} %collective-permute-done.1.refs_0_), channel_id=1, source_target_pairs={{0,2},{1,3},{2,0},{3,1},{4,6},{5,7},{6,4},{7,5},{8,10},{9,11},{10,... | collective-permute-start | bytes 2359304 | tf_op jit(solution)/shard_map/ppermute | solution.py:32
  28.9 0.0 collective-permute-done.4.refs_3_
  28.9 6.8 %collective-permute-done.6.refs_6_.refs_9_.refs_10_ = bf16[528,1024]{1,0:T(8,128)(2,1)S(1)} collective-permute-done((bf16[528,1024]{1,0:T(8,128)(2,1)S(1)}, bf16[528,1024]{1,0:T(8,128)(2,1)S(1)}, u32[]{:S(2)}, u32[]{:S(2)}) %collective-permute-start.6) | collective-permute-done | bytes 1081376 | tf_op jit(solution)/shard_map/ppermute | solution.py:32
  35.7 0.0 collective-permute-done.7.refs_2_
  35.7 0.0 collective-permute-done.8.refs_3_
  35.7 0.0 collective-permute-done.5.refs_2_
  35.7 0.5 collective-permute-start.9
  36.2 0.7 shard_map.52.refs_6_
  36.9 0.2 collective-permute-start.10
  37.1 0.7 collective-permute-start.11
  37.7 0.0 collective-permute-start.2
  37.7 2.7 %collective-permute-start.12 = (bf16[384,1024]{1,0:T(8,128)(2,1)S(1)}, bf16[384,1024]{1,0:T(8,128)(2,1)S(1)}, u32[]{:S(2)}, u32[]{:S(2)}) collective-permute-start(bf16[384,1024]{1,0:T(8,128)(2,1)S(1)} %collective-permute-done.1.refs_0_), channel_id=1, source_target_pairs={{0,16},{1,17},{2,50},{3,51},{4,20},{5,21},{6,54},{7,55},{8,24},{9,... | collective-permute-start | bytes 2359304 | tf_op jit(solution)/shard_map/ppermute | solution.py:32
  40.4 0.0 collective-permute-done.9.refs_1_
  40.4 4.9 %collective-permute-start.13 = (bf16[384,1024]{1,0:T(8,128)(2,1)S(1)}, bf16[384,1024]{1,0:T(8,128)(2,1)S(1)}, u32[]{:S(2)}, u32[]{:S(2)}) collective-permute-start(bf16[384,1024]{1,0:T(8,128)(2,1)S(1)} %collective-permute-done.7.refs_2_), channel_id=1, source_target_pairs={{0,65},{1,64},{2,67},{3,66},{4,69},{5,68},{6,71},{7,70},{8,73},{9,... | collective-permute-start | bytes 2359304 | tf_op jit(solution)/shard_map/ppermute | solution.py:32
  45.3 0.0 copy-done
  45.3 0.0 copy-done.1
  45.3 6.4 %shard_map.51 = (f32[1024,128]{1,0:T(8,128)S(1)}, bf16[2,768,1024]{2,1,0:T(8,128)(2,1)S(1)}, bf16[3,1024,768]{2,1,0:T(8,128)(2,1)S(1)}) custom-call(s32[12]{0:T(128)S(1)} %stack.51.numbers.ids.refs_0_, bf16[384,1024]{1,0:T(8,128)(2,1)S(1)} %collective-permute-done.1.refs_0_, bf16[384,1024]{1,0:T(8,128)(2,1)S(1)} %collective-permute-done.9.refs_1_, ...), custom_call_target="tpu_custom_call" | custom-call | flops 4831838208 | bytes 3145728 | tf_op jit(solution)/shard_map/pallas_call | solution.py:221
  51.7 0.0 collective-permute-done.11.refs_3_
  51.7 0.3 collective-permute-start.16
  52.0 0.0 collective-permute-done.2.refs_2_
  52.0 0.0 collective-permute-done.10.refs_7_
  52.0 12.1 %shard_map.53 = (f32[1024,512]{1,0:T(8,128)S(1)}, f32[1024,512]{1,0:T(8,128)S(1)}, bf16[8,64,1024]{2,1,0:T(8,128)(2,1)S(1)}, bf16[8,64,1024]{2,1,0:T(8,128)(2,1)...) custom-call(s32[12]{0:T(128)S(1)} %stack.51.numbers.ids.refs_0_, ...), custom_call_target="tpu_custom_call" | custom-call | flops 16106127360 | bytes 6291456 | tf_op jit(solution)/shard_map/pallas_call | solution.py:431
  64.2 0.0 collective-permute-done.12.refs_1_
  64.2 0.0 collective-permute-done.13.refs_5_
  64.2 0.1 collective-permute-start.14
  64.3 0.5 collective-permute-start.15
  64.8 0.1 collective-permute-start.17
  64.9 0.2 collective-permute-done.16.refs_7_
  65.1 1.5 %collective-permute-done.14.refs_2_ = bf16[384,1024]{1,0:T(8,128)(2,1)S(1)} collective-permute-done((bf16[384,1024]{1,0:T(8,128)(2,1)S(1)}, bf16[384,1024]{1,0:T(8,128)(2,1)S(1)}, u32[]{:S(2)}, u32[]{:S(2)}) %collective-permute-start.14) | collective-permute-done | bytes 786464 | tf_op jit(solution)/shard_map/ppermute | solution.py:32
  66.6 1.1 %collective-permute-done.15.refs_4_ = bf16[384,1024]{1,0:T(8,128)(2,1)S(1)} collective-permute-done((bf16[384,1024]{1,0:T(8,128)(2,1)S(1)}, bf16[384,1024]{1,0:T(8,128)(2,1)S(1)}, u32[]{:S(2)}, u32[]{:S(2)}) %collective-permute-start.15) | collective-permute-done | bytes 786464 | tf_op jit(solution)/shard_map/ppermute | solution.py:32
  67.7 0.1 collective-permute-start.18
  67.8 1.0 %collective-permute-done.17.refs_6_ = bf16[384,1024]{1,0:T(8,128)(2,1)S(1)} collective-permute-done((bf16[384,1024]{1,0:T(8,128)(2,1)S(1)}, bf16[384,1024]{1,0:T(8,128)(2,1)S(1)}, u32[]{:S(2)}, u32[]{:S(2)}) %collective-permute-start.17) | collective-permute-done | bytes 786464 | tf_op jit(solution)/shard_map/ppermute | solution.py:32
  68.8 1.2 %collective-permute-done.18.refs_8_ = bf16[384,1024]{1,0:T(8,128)(2,1)S(1)} collective-permute-done((bf16[384,1024]{1,0:T(8,128)(2,1)S(1)}, bf16[384,1024]{1,0:T(8,128)(2,1)S(1)}, u32[]{:S(2)}, u32[]{:S(2)}) %collective-permute-start.18) | collective-permute-done | bytes 786464 | tf_op jit(solution)/shard_map/ppermute | solution.py:32
  70.0 23.5 %shard_map.54 = (f32[1024,1,512]{2,1,0:T(1,128)}, f32[1024,1,512]{2,1,0:T(1,128)}, f32[1024,512]{1,0:T(8,128)S(1)}, f32[1024,512]{1,0:T(8,128)S(1)}, bf16[8,64,1...) custom-call(s32[12]{0:T(128)S(1)} %stack.51.numbers.ids.refs_0_, ...), custom_call_target="tpu_custom_call", output_to_operand_aliasing={{2}: (15, {}), {3}: (16, {}), {4}: (17, {}), {5}: (18, {})} | custom-call | flops 20132659200 | bytes 7864320 | tf_op jit(solution)/shard_map/pallas_call | solution.py:431
Async XLA Ops:
  3.0 8.3 %collective-permute-start.3 = (bf16[1040,512]{1,0:T(8,128)(2,1)S(1)}, bf16[1040,512]{1,0:T(8,128)(2,1)S(1)}, u32[]{:S(2)}, u32[]{:S(2)}) collective-permute-start(bf16[1040,512]{1,0:T(8,128)(2,1)S(1)} %get-tuple-element.53.refs_0_), channel_id=1, source_target_pairs={{0,4},{1,5},{18,22},{19,23},{36,40},{37,41},{54,58},{55,59},{72,76... | collective-permute-start | bytes 3194888 | tf_op jit(solution)/shard_map/ppermute | solution.py:32
  3.7 14.8 %collective-permute-start.1 = (bf16[384,1024]{1,0:T(8,128)(2,1)S(1)}, bf16[384,1024]{1,0:T(8,128)(2,1)S(1)}, u32[]{:S(2)}, u32[]{:S(2)}) collective-permute-start(bf16[384,1024]{1,0:T(8,128)(2,1)S(1)} %get-tuple-element.55), channel_id=1, source_target_pairs={{0,16},{1,17},{2,50},{3,51},{4,20},{5,21},{6,54},{7,55},{8,24},{9,... | collective-permute-start | bytes 2359304 | tf_op jit(solution)/shard_map/ppermute | solution.py:32
  7.4 19.8 %collective-permute-start = (bf16[384,1024]{1,0:T(8,128)(2,1)S(1)}, bf16[384,1024]{1,0:T(8,128)(2,1)S(1)}, u32[]{:S(2)}, u32[]{:S(2)}) collective-permute-start(bf16[384,1024]{1,0:T(8,128)(2,1)S(1)} %get-tuple-element.55), channel_id=1, source_target_pairs={{0,65},{1,64},{2,67},{3,66},{4,69},{5,68},{6,71},{7,70},{8,73},{9,... | collective-permute-start | bytes 2359304 | tf_op jit(solution)/shard_map/ppermute | solution.py:32
  10.4 34.9 %copy-start = (bf16[768,1024]{1,0:T(8,128)(2,1)S(1)}, bf16[768,1024]{1,0:T(8,128)(2,1)}, u32[]{:S(2)}) copy-start(bf16[768,1024]{1,0:T(8,128)(2,1)} %refs_3_.1) | copy-start | bytes 4718596
  10.4 34.9 %copy-start.1 = (f32[512]{0:T(512)S(1)}, f32[512]{0:T(512)}, u32[]{:S(2)}) copy-start(f32[512]{0:T(512)} %param.5) | copy-start | bytes 6148
  10.4 25.3 %collective-permute-start.6 = (bf16[528,1024]{1,0:T(8,128)(2,1)S(1)}, bf16[528,1024]{1,0:T(8,128)(2,1)S(1)}, u32[]{:S(2)}, u32[]{:S(2)}) collective-permute-start(bf16[528,1024]{1,0:T(8,128)(2,1)S(1)} %get-tuple-element.54.refs_5_.refs_8_.refs_9_), channel_id=1, source_target_pairs={{0,1},{1,0},{2,3},{3,2},{4,5},{5,4},{6,7},{7,6},{8,9},{9,8},{10,11... | collective-permute-start | bytes 3244040 | tf_op jit(solution)/shard_map/ppermute | solution.py:32
  10.4 18.5 %collective-permute-start.4 = (bf16[1040,512]{1,0:T(8,128)(2,1)S(1)}, bf16[1040,512]{1,0:T(8,128)(2,1)S(1)}, u32[]{:S(2)}, u32[]{:S(2)}) collective-permute-start(bf16[1040,512]{1,0:T(8,128)(2,1)S(1)} %get-tuple-element.53.refs_0_), channel_id=1, source_target_pairs={{0,12},{1,13},{18,30},{19,31},{36,32},{37,33},{54,50},{55,51},{72,... | collective-permute-start | bytes 3194888 | tf_op jit(solution)/shard_map/ppermute | solution.py:32
  11.3 24.4 %collective-permute-start.5 = (bf16[1040,512]{1,0:T(8,128)(2,1)S(1)}, bf16[1040,512]{1,0:T(8,128)(2,1)S(1)}, u32[]{:S(2)}, u32[]{:S(2)}) collective-permute-start(bf16[1040,512]{1,0:T(8,128)(2,1)S(1)} %get-tuple-element.53.refs_0_), channel_id=1, source_target_pairs={{0,8},{1,9},{18,26},{19,27},{36,44},{37,45},{54,62},{55,63},{72,64... | collective-permute-start | bytes 3194888 | tf_op jit(solution)/shard_map/ppermute | solution.py:32
  18.5 17.2 %collective-permute-start.7 = (bf16[384,1024]{1,0:T(8,128)(2,1)S(1)}, bf16[384,1024]{1,0:T(8,128)(2,1)S(1)}, u32[]{:S(2)}, u32[]{:S(2)}) collective-permute-start(bf16[384,1024]{1,0:T(8,128)(2,1)S(1)} %get-tuple-element.55), channel_id=1, source_target_pairs={{0,48},{1,49},{2,18},{3,19},{4,52},{5,53},{6,22},{7,23},{8,56},{9,... | collective-permute-start | bytes 2359304 | tf_op jit(solution)/shard_map/ppermute | solution.py:32
  27.2 8.5 %collective-permute-start.8 = (bf16[384,1024]{1,0:T(8,128)(2,1)S(1)}, bf16[384,1024]{1,0:T(8,128)(2,1)S(1)}, u32[]{:S(2)}, u32[]{:S(2)}) collective-permute-start(bf16[384,1024]{1,0:T(8,128)(2,1)S(1)} %collective-permute-done.1.refs_0_), channel_id=1, source_target_pairs={{0,2},{1,3},{2,0},{3,1},{4,6},{5,7},{6,4},{7,5},{8,10},{9,11},{10,... | collective-permute-start | bytes 2359304 | tf_op jit(solution)/shard_map/ppermute | solution.py:32
  35.7 4.7 %collective-permute-start.9 = (bf16[384,1024]{1,0:T(8,128)(2,1)S(1)}, bf16[384,1024]{1,0:T(8,128)(2,1)S(1)}, u32[]{:S(2)}, u32[]{:S(2)}) collective-permute-start(bf16[384,1024]{1,0:T(8,128)(2,1)S(1)} %collective-permute-done.7.refs_2_), channel_id=1, source_target_pairs={{0,2},{1,3},{2,0},{3,1},{4,6},{5,7},{6,4},{7,5},{8,10},{9,11},{10,... | collective-permute-start | bytes 2359304 | tf_op jit(solution)/shard_map/ppermute | solution.py:32
  36.9 15.2 %collective-permute-start.10 = (bf16[1040,512]{1,0:T(8,128)(2,1)S(1)}, bf16[1040,512]{1,0:T(8,128)(2,1)S(1)}, u32[]{:S(2)}, u32[]{:S(2)}) collective-permute-start(bf16[1040,512]{1,0:T(8,128)(2,1)S(1)} %shard_map.52.refs_6_), channel_id=1, source_target_pairs={{0,2},{1,3},{2,0},{3,1},{4,6},{5,7},{6,4},{7,5},{8,10},{9,11},{10,... | collective-permute-start | bytes 3194888 | tf_op jit(solution)/shard_map/ppermute | solution.py:32
  37.1 14.7 %collective-permute-start.11 = (bf16[384,1024]{1,0:T(8,128)(2,1)S(1)}, bf16[384,1024]{1,0:T(8,128)(2,1)S(1)}, u32[]{:S(2)}, u32[]{:S(2)}) collective-permute-start(bf16[384,1024]{1,0:T(8,128)(2,1)S(1)} %collective-permute-done.refs_1_), channel_id=1, source_target_pairs={{0,16},{1,17},{2,50},{3,51},{4,20},{5,21},{6,54},{7,55},{8,24},{9,... | collective-permute-start | bytes 2359304 | tf_op jit(solution)/shard_map/ppermute | solution.py:32
  37.7 14.3 %collective-permute-start.2 = (bf16[384,1024]{1,0:T(8,128)(2,1)S(1)}, bf16[384,1024]{1,0:T(8,128)(2,1)S(1)}, u32[]{:S(2)}, u32[]{:S(2)}) collective-permute-start(bf16[384,1024]{1,0:T(8,128)(2,1)S(1)} %collective-permute-done.refs_1_), channel_id=1, source_target_pairs={{0,2},{1,3},{2,0},{3,1},{4,6},{5,7},{6,4},{7,5},{8,10},{9,11},{10,... | collective-permute-start | bytes 2359304 | tf_op jit(solution)/shard_map/ppermute | solution.py:32
  37.7 26.4 %collective-permute-start.12 = (bf16[384,1024]{1,0:T(8,128)(2,1)S(1)}, bf16[384,1024]{1,0:T(8,128)(2,1)S(1)}, u32[]{:S(2)}, u32[]{:S(2)}) collective-permute-start(bf16[384,1024]{1,0:T(8,128)(2,1)S(1)} %collective-permute-done.1.refs_0_), channel_id=1, source_target_pairs={{0,16},{1,17},{2,50},{3,51},{4,20},{5,21},{6,54},{7,55},{8,24},{9,... | collective-permute-start | bytes 2359304 | tf_op jit(solution)/shard_map/ppermute | solution.py:32
  40.4 23.8 %collective-permute-start.13 = (bf16[384,1024]{1,0:T(8,128)(2,1)S(1)}, bf16[384,1024]{1,0:T(8,128)(2,1)S(1)}, u32[]{:S(2)}, u32[]{:S(2)}) collective-permute-start(bf16[384,1024]{1,0:T(8,128)(2,1)S(1)} %collective-permute-done.7.refs_2_), channel_id=1, source_target_pairs={{0,65},{1,64},{2,67},{3,66},{4,69},{5,68},{6,71},{7,70},{8,73},{9,... | collective-permute-start | bytes 2359304 | tf_op jit(solution)/shard_map/ppermute | solution.py:32
  51.7 13.3 %collective-permute-start.16 = (bf16[384,1024]{1,0:T(8,128)(2,1)S(1)}, bf16[384,1024]{1,0:T(8,128)(2,1)S(1)}, u32[]{:S(2)}, u32[]{:S(2)}) collective-permute-start(bf16[384,1024]{1,0:T(8,128)(2,1)S(1)} %collective-permute-done.11.refs_3_), channel_id=1, source_target_pairs={{0,16},{1,17},{2,50},{3,51},{4,20},{5,21},{6,54},{7,55},{8,24},{9,... | collective-permute-start | bytes 2359304 | tf_op jit(solution)/shard_map/ppermute | solution.py:32
  64.2 2.4 %collective-permute-start.14 = (bf16[384,1024]{1,0:T(8,128)(2,1)S(1)}, bf16[384,1024]{1,0:T(8,128)(2,1)S(1)}, u32[]{:S(2)}, u32[]{:S(2)}) collective-permute-start(bf16[384,1024]{1,0:T(8,128)(2,1)S(1)} %collective-permute-done.12.refs_1_), channel_id=1, source_target_pairs={{0,2},{1,3},{2,0},{3,1},{4,6},{5,7},{6,4},{7,5},{8,10},{9,11},{10,... | collective-permute-start | bytes 2359304 | tf_op jit(solution)/shard_map/ppermute | solution.py:32
  64.3 3.4 %collective-permute-start.15 = (bf16[384,1024]{1,0:T(8,128)(2,1)S(1)}, bf16[384,1024]{1,0:T(8,128)(2,1)S(1)}, u32[]{:S(2)}, u32[]{:S(2)}) collective-permute-start(bf16[384,1024]{1,0:T(8,128)(2,1)S(1)} %collective-permute-done.13.refs_5_), channel_id=1, source_target_pairs={{0,2},{1,3},{2,0},{3,1},{4,6},{5,7},{6,4},{7,5},{8,10},{9,11},{10,... | collective-permute-start | bytes 2359304 | tf_op jit(solution)/shard_map/ppermute | solution.py:32
  64.8 4.0 %collective-permute-start.17 = (bf16[384,1024]{1,0:T(8,128)(2,1)S(1)}, bf16[384,1024]{1,0:T(8,128)(2,1)S(1)}, u32[]{:S(2)}, u32[]{:S(2)}) collective-permute-start(bf16[384,1024]{1,0:T(8,128)(2,1)S(1)} %collective-permute-done.11.refs_3_), channel_id=1, source_target_pairs={{0,2},{1,3},{2,0},{3,1},{4,6},{5,7},{6,4},{7,5},{8,10},{9,11},{10,... | collective-permute-start | bytes 2359304 | tf_op jit(solution)/shard_map/ppermute | solution.py:32
  67.7 2.3 %collective-permute-start.18 = (bf16[384,1024]{1,0:T(8,128)(2,1)S(1)}, bf16[384,1024]{1,0:T(8,128)(2,1)S(1)}, u32[]{:S(2)}, u32[]{:S(2)}) collective-permute-start(bf16[384,1024]{1,0:T(8,128)(2,1)S(1)} %collective-permute-done.16.refs_7_), channel_id=1, source_target_pairs={{0,2},{1,3},{2,0},{3,1},{4,6},{5,7},{6,4},{7,5},{8,10},{9,11},{10,... | collective-permute-start | bytes 2359304 | tf_op jit(solution)/shard_map/ppermute | solution.py:32
